TPU v7x, 32 devices: a whole 2x2x4 slice. The times are simulated.
32 devices in a mesh: batch: 8 (over z, x), task: 4 (over y, core).
Axes of the slice: x: 2, y: 2, z: 4, core: 2. Of those that a mesh axis runs over, the one named last changes fastest.
Arguments:
- images: bfloat16 [16, 512, 4096], P('batch', 'task'), may hold values from -6 to 6
- conv1_weight: bfloat16 [9, 512, 512], P(None, 'task'), may hold values from -0.09375 to 0.09375
- norm1_gain: float32 [512], P('task'), may hold values from 0.5 to 1.5
- norm1_bias: float32 [512], P('task'), may hold values from -3 to 3
- conv2_weight: bfloat16 [9, 512, 512], P(None, 'task'), may hold values from -0.09375 to 0.09375
- norm2_gain: float32 [512], P('task'), may hold values from 0.5 to 1.5
- norm2_bias: float32 [512], P('task'), may hold values from -3 to 3
- head_weight: bfloat16 [512, 40], P(None, 'task'), may hold values from -0.53033009 to 0.53033009, as said below
- head_bias: float32 [40], P('task'), may hold values from -3 to 3
- labels: int32 [16, 40], P('batch', 'task'), may hold values from 0 to 1
- image_counts: int32 [8], replicated, may hold values from 1 to 2, as said below
- average_weights: float32 [40], replicated, may hold values from 0.2 to 1
Outputs:
- pooled: float32 [16, 512], P('batch', 'task')
- input_grad: float32 [16, 512, 4096], P('batch', 'task')
- conv1_grad: float32 [9, 512, 512], P(None, 'task')
- norm1_gain_grad: float32 [512], P('task')
- norm1_bias_grad: float32 [512], P('task')
- conv2_grad: float32 [9, 512, 512], P(None, 'task')
- norm2_gain_grad: float32 [512], P('task')
- norm2_bias_grad: float32 [512], P('task')
- head_weight_grad: float32 [512, 40], P(None, 'task')
- head_bias_grad: float32 [40], P('task')
- task_weights: float32 [40], replicated
- average_next: float32 [40], replicated
Inputs may be any that keep to these rules, and one draw needn't show every extreme that they name: `head_weight`: head columns of differing norms. `image_counts`: real images are the first slots of each batch index; some batch index is full in every draw.
All inputs are finite; a program needn't handle non-finite values.
Results may differ from a plain program's by a relative error of at most 0.0036.
Values may be sent and summed in bfloat16 or wider, within the bound.
No kernel may reach another device: no remote copies, remote signals or barrier semaphores. Data moves between devices by JAX's collectives and lax.ppermute only.
A program may use at most 256 MiB of HBM per device.

v0:
```python
import jax
import jax.numpy as jnp
from jax import lax
from jax.sharding import PartitionSpec as P

SIDE = 64
FW_STEPS = 20


eps = 1e-05
loss_scale = 4096.0
highest = lax.Precision.HIGHEST


def edge_masks(image_side):
    column = jnp.arange(image_side * image_side, dtype=jnp.int32) % image_side
    return [
        ((column + shift_by >= 0) & (column + shift_by < image_side)).astype(jnp.float32)
        for shift_by in (-1, 0, 1)
    ]


def move(values, offset, image_side):
    margin = image_side + 1
    pad_widths = [(0, 0)] * (values.ndim - 1) + [(margin, margin)]
    padded = jnp.pad(values, pad_widths)
    return lax.slice_in_dim(
        padded, margin + offset, margin + offset + image_side * image_side, axis=values.ndim - 1
    )


def tap_offset(kernel_tap, image_side):
    return (kernel_tap // 3 - 1) * image_side + (kernel_tap % 3 - 1)


def gather_channels(values):
    return lax.all_gather(values, "task", axis=1, tiled=True)


def batch_total(values):
    return lax.psum(values, "batch")


def convolve(full_input, weight, image_side):
    shard_width = weight.shape[1]
    stacked = weight.reshape(9 * shard_width, weight.shape[2])
    products = jnp.einsum("oc,ncp->nop", stacked, full_input, preferred_element_type=jnp.float32)
    masks_list = edge_masks(image_side)
    result = jnp.zeros((full_input.shape[0], shard_width, full_input.shape[2]), jnp.float32)
    for kernel_tap in range(9):
        tap_part = products[:, kernel_tap * shard_width : (kernel_tap + 1) * shard_width, :]
        result = (
            result
            + move(tap_part, tap_offset(kernel_tap, image_side), image_side)
            * masks_list[kernel_tap % 3]
        )
    return result


def norm_stats(conv_out, valid_rows, pixel_total):
    row_weights = valid_rows[:, None, None]
    mean_value = batch_total(jnp.sum(conv_out * row_weights, axis=(0, 2))) / pixel_total
    centered = conv_out - mean_value[None, :, None]
    spread = batch_total(jnp.sum(centered * centered * row_weights, axis=(0, 2))) / pixel_total
    return (centered, lax.rsqrt(spread + eps))


def norm_backward(grad_out, centered, norm_scale, norm_gain, valid_rows, pixel_total):
    row_weights = valid_rows[:, None, None]
    normalized = centered * norm_scale[None, :, None]
    gain_grad, bias_grad = lax.psum(
        (
            jnp.sum(grad_out * normalized * row_weights, axis=(0, 2)),
            jnp.sum(grad_out * row_weights, axis=(0, 2)),
        ),
        "batch",
    )
    grad_in = (
        row_weights
        * (norm_gain * norm_scale)[None, :, None]
        * (
            grad_out
            - (bias_grad[None, :, None] + normalized * gain_grad[None, :, None]) / pixel_total
        )
    )
    return (grad_in, gain_grad, bias_grad)


def silu_slope(values):
    sigmoid_values = jax.nn.sigmoid(values)
    return sigmoid_values * (1.0 + values * (1.0 - sigmoid_values))


def transposed_stack(grad_low, image_side):
    masks_list = edge_masks(image_side)
    pieces = [
        move(
            grad_low * masks_list[kernel_tap % 3].astype(jnp.bfloat16),
            -tap_offset(kernel_tap, image_side),
            image_side,
        )
        for kernel_tap in range(9)
    ]
    return jnp.stack(pieces, axis=1)


def input_side(stacked_grad, weight):
    partial_terms = jnp.einsum(
        "koc,nkop->ncp", weight, stacked_grad, preferred_element_type=jnp.float32
    )
    return lax.psum_scatter(partial_terms, "task", scatter_dimension=1, tiled=True)


def frank_wolfe(gram_matrix, average_weights):
    task_count = gram_matrix.shape[0]
    normalized = gram_matrix / (jnp.trace(gram_matrix) / task_count)
    start_weights = average_weights / jnp.sum(average_weights)

    def advance(loop_index, current):
        slope_values = jnp.dot(normalized, current, precision=highest)
        target = jax.nn.softmax(-task_count * slope_values)
        step_rate = 1.0 / (loop_index + 4.0)
        return (1.0 - step_rate) * current + step_rate * target

    final_weights = lax.fori_loop(0, FW_STEPS, advance, start_weights)
    return (final_weights, 0.9 * start_weights + 0.1 * final_weights)


def on_device(
    images,
    conv1_weight,
    norm1_gain,
    norm1_bias,
    conv2_weight,
    norm2_gain,
    norm2_bias,
    head_weight,
    head_bias,
    labels,
    image_counts,
    average_weights,
):
    slot_count = images.shape[0]
    image_area = images.shape[2]
    image_side = SIDE
    tasks_here = head_weight.shape[1]
    total_tasks = tasks_here * lax.axis_size("task")
    own_count = lax.dynamic_index_in_dim(image_counts, lax.axis_index("batch"), keepdims=False)
    valid_rows = (jnp.arange(slot_count, dtype=jnp.int32) < own_count).astype(jnp.float32)
    image_total = jnp.sum(image_counts).astype(jnp.float32)
    pixel_total = image_total * image_area
    inputs_full = gather_channels(images)
    first_out = convolve(inputs_full, conv1_weight, image_side)
    centered_one, scale_one = norm_stats(first_out, valid_rows, pixel_total)
    normed_one = (
        centered_one * scale_one[None, :, None] * norm1_gain[None, :, None]
        + norm1_bias[None, :, None]
    )
    activity = jax.nn.silu(normed_one).astype(jnp.bfloat16)
    activity_full = gather_channels(activity)
    second_out = convolve(activity_full, conv2_weight, image_side)
    centered_two, scale_two = norm_stats(second_out, valid_rows, pixel_total)
    normed_two = (
        centered_two * scale_two[None, :, None] * norm2_gain[None, :, None]
        + norm2_bias[None, :, None]
    )
    summed = normed_two + images.astype(jnp.float32)
    pooled = jnp.mean(jax.nn.silu(summed), axis=2) * valid_rows[:, None]
    pooled_full = lax.all_gather(pooled, "task", axis=1, tiled=True)
    head_float = head_weight.astype(jnp.float32)
    logits = jnp.dot(pooled_full, head_float, precision=highest) + head_bias[None, :]
    errors = (
        valid_rows[:, None] * (jax.nn.sigmoid(logits) - labels.astype(jnp.float32)) / image_total
    )
    per_task = errors.T[:, :, None] * head_float.T[:, None, :]
    all_tasks = lax.all_gather(per_task, "task", axis=0, tiled=True)
    local_term = jnp.einsum("tnc,snc->ts", all_tasks, all_tasks, precision=highest)
    gram_matrix = lax.psum(local_term, "batch")
    scaled_all = None
    task_weights, average_next = frank_wolfe(gram_matrix, average_weights)
    scaled_all = loss_scale * total_tasks * task_weights
    own_scaled = lax.dynamic_slice_in_dim(
        scaled_all, lax.axis_index("task") * tasks_here, tasks_here
    )
    logit_grads = errors * own_scaled[None, :]
    head_weight_grad = jnp.dot(pooled_full.T, logit_grads, precision=highest)
    head_bias_grad = jnp.sum(logit_grads, axis=0)
    pooled_grad = lax.psum_scatter(
        jnp.dot(logit_grads, head_float.T, precision=highest),
        "task",
        scatter_dimension=1,
        tiled=True,
    )
    summed_grad = (valid_rows[:, None] * pooled_grad / image_area)[:, :, None] * silu_slope(summed)
    second_grad, gain_two_grad, bias_two_grad = norm_backward(
        summed_grad, centered_two, scale_two, norm2_gain, valid_rows, pixel_total
    )
    second_low = second_grad.astype(jnp.bfloat16)
    stack_two = transposed_stack(second_low, image_side)
    conv2_grad = jnp.einsum(
        "nkop,ncp->koc", stack_two, activity_full, preferred_element_type=jnp.float32
    )
    activity_grad = input_side(stack_two, conv2_weight)
    normed_grad = activity_grad * silu_slope(normed_one)
    first_grad, gain_one_grad, bias_one_grad = norm_backward(
        normed_grad, centered_one, scale_one, norm1_gain, valid_rows, pixel_total
    )
    first_low = first_grad.astype(jnp.bfloat16)
    stack_one = transposed_stack(first_low, image_side)
    conv1_grad = jnp.einsum(
        "nkop,ncp->koc", stack_one, inputs_full, preferred_element_type=jnp.float32
    )
    input_grad = summed_grad + input_side(stack_one, conv1_weight)
    conv1_grad, conv2_grad, head_weight_grad, head_bias_grad = lax.psum(
        (conv1_grad, conv2_grad, head_weight_grad, head_bias_grad), "batch"
    )
    return (
        pooled,
        input_grad,
        conv1_grad,
        gain_one_grad,
        bias_one_grad,
        conv2_grad,
        gain_two_grad,
        bias_two_grad,
        head_weight_grad,
        head_bias_grad,
        task_weights,
        average_next,
    )


def solution(mesh):
    in_specs = (
        P("batch", "task", None),
        P(None, "task", None),
        P("task"),
        P("task"),
        P(None, "task", None),
        P("task"),
        P("task"),
        P(None, "task"),
        P("task"),
        P("batch", "task"),
        P(),
        P(),
    )
    out_specs = (
        P("batch", "task"),
        P("batch", "task", None),
        P(None, "task", None),
        P("task"),
        P("task"),
        P(None, "task", None),
        P("task"),
        P("task"),
        P(None, "task"),
        P("task"),
        P(),
        P(),
    )
    return jax.shard_map(
        on_device, mesh=mesh, in_specs=in_specs, out_specs=out_specs, check_vma=False
    )
```

profile of v0, /device:TPU:0, one launch (start us, length us, event | category | flops | bytes accessed | tf_op | source)
XLA Modules:
  0.0 1037.5 jit_solution(6324568450371735016)
XLA Ops:
  14.1 59.6 %all-gather.3.cloned.1.call-done = bf16[2,512,4096]{1,2,0:T(8,128)(2,1)} async-done(((bf16[2,128,4096]{1,2,0:T(8,128)(2,1)}), bf16[2,512,4096]{1,2,0:T(8,128)(2,1)}) %all-gather.3.cloned.1.call-update) | async-done | bytes 8388624 | tf_op jit(solution)/shard_map/all_gather | solution.py:37
  73.8 22.2 %convolution_bitcast_fusion.2 = f32[2,1152,4096]{1,2,0:T(8,128)} fusion(bf16[2,512,4096]{1,2,0:T(8,128)(2,1)} %all-gather.3.cloned.1.call-done, bf16[1152,512,1]{1,0,2:T(8,128)(2,1)S(1)} %bitcast.118), kind=kOutput, calls=%fused_computation.7 | convolution fusion | flops 9663676416 | bytes 47316992 | tf_op jit(solution)/shard_map/oc,ncp->nop/dot_general | solution.py:47
  96.0 21.1 %fusion.87 = (f32[2,128,4096]{1,2,0:T(8,128)S(1)}, f32[2,128,4096]{1,2,0:T(8,128)S(1)}, f32[2,128,4096]{1,2,0:T(8,128)}, f32[2,128,4096]{1,2,0:T(8,128)}, f32[2,...) fusion(f32[2,1152,4096]{1,2,0:T(8,128)} %convolution_bitcast_fusion.2), kind=kLoop, calls=%fused_computation.174 | loop fusion | bytes 67108864 | tf_op jit(solution)/shard_map/slice | solution.py:51
  117.1 12.6 %multiply_reduce_fusion.8 = (f32[128]{0:T(128)S(1)}, f32[2,128,4096]{1,2,0:T(8,128)}) fusion(f32[2]{0:T(128)S(1)} %compare_convert_fusion, f32[2,128,4096]{1,2,0:T(8,128)S(1)} %get-tuple-element.143, f32[2,128,4096]{1,2,0:T(8,128)} %get-tuple-element.144, f32[2,128,4096]{1,2,0:T(8,128)} %get-tuple-element.145, f32[2,128,4096]{1,2,0:T(8,128)} %get-tuple-element.146, ...), kind=kLoop, calls=%fused_computation.81 | loop fusion | flops 19922816 | bytes 41992712 | tf_op jit(solution)/shard_map/reduce_sum | solution.py:62
  129.7 21.3 %psum.91 = f32[128]{0:T(128)S(1)} all-reduce(f32[128]{0:T(128)S(1)} %get-tuple-element.130), channel_id=1, replica_groups=mesh['batch'=8,'task'=4] {'batch'}, use_global_device_ids=true, to_apply=%region_1.2 | all-reduce | flops 128 | bytes 1024 | tf_op jit(solution)/shard_map/psum | solution.py:41
  154.4 17.1 %psum.92 = f32[128]{0:T(128)S(1)} all-reduce(f32[128]{0:T(128)S(1)} %multiply_reduce_fusion.7), channel_id=1, replica_groups=mesh['batch'=8,'task'=4] {'batch'}, use_global_device_ids=true, to_apply=%region_4.5 | all-reduce | flops 128 | bytes 1024 | tf_op jit(solution)/shard_map/psum | solution.py:41
  179.0 54.9 %all-gather.5.cloned.1.call-done = bf16[2,512,4096]{1,2,0:T(8,128)(2,1)} async-done(((bf16[2,128,4096]{1,2,0:T(8,128)(2,1)}), bf16[2,512,4096]{1,2,0:T(8,128)(2,1)}) %all-gather.5.cloned.1.call-update) | async-done | bytes 8388624 | tf_op jit(solution)/shard_map/all_gather | solution.py:37
  233.9 22.2 %convolution_bitcast_fusion.1 = f32[2,1152,4096]{1,2,0:T(8,128)} fusion(bf16[2,512,4096]{1,2,0:T(8,128)(2,1)} %all-gather.5.cloned.1.call-done, bf16[1152,512,1]{1,0,2:T(8,128)(2,1)S(1)} %bitcast.115), kind=kOutput, calls=%fused_computation.6 | convolution fusion | flops 9663676416 | bytes 47316992 | tf_op jit(solution)/shard_map/oc,ncp->nop/dot_general | solution.py:47
  256.1 21.1 %fusion.86 = (f32[2,128,4096]{1,2,0:T(8,128)S(1)}, f32[2,128,4096]{1,2,0:T(8,128)S(1)}, f32[2,128,4096]{1,2,0:T(8,128)}, f32[2,128,4096]{1,2,0:T(8,128)}, f32[2,...) fusion(f32[2,1152,4096]{1,2,0:T(8,128)} %convolution_bitcast_fusion.1), kind=kLoop, calls=%fused_computation.173 | loop fusion | bytes 67108864 | tf_op jit(solution)/shard_map/slice | solution.py:51
  277.2 12.6 %multiply_reduce_fusion.6 = (f32[128]{0:T(128)S(1)}, f32[2,128,4096]{1,2,0:T(8,128)}) fusion(f32[2]{0:T(128)S(1)} %compare_convert_fusion, f32[2,128,4096]{1,2,0:T(8,128)S(1)} %get-tuple-element.135, f32[2,128,4096]{1,2,0:T(8,128)} %get-tuple-element.136, f32[2,128,4096]{1,2,0:T(8,128)} %get-tuple-element.137, f32[2,128,4096]{1,2,0:T(8,128)} %get-tuple-element.138, ...), kind=kLoop, calls=%fused_computation.76 | loop fusion | flops 19922816 | bytes 41992712 | tf_op jit(solution)/shard_map/reduce_sum | solution.py:62
  289.8 21.5 %psum.93 = f32[128]{0:T(128)S(1)} all-reduce(f32[128]{0:T(128)S(1)} %get-tuple-element.128), channel_id=1, replica_groups=mesh['batch'=8,'task'=4] {'batch'}, use_global_device_ids=true, to_apply=%region_6.7 | all-reduce | flops 128 | bytes 1024 | tf_op jit(solution)/shard_map/psum | solution.py:41
  314.7 17.1 %psum.94 = f32[128]{0:T(128)S(1)} all-reduce(f32[128]{0:T(128)S(1)} %multiply_reduce_fusion.5), channel_id=1, replica_groups=mesh['batch'=8,'task'=4] {'batch'}, use_global_device_ids=true, to_apply=%region_8.9 | all-reduce | flops 128 | bytes 1024 | tf_op jit(solution)/shard_map/psum | solution.py:41
  335.8 5.1 all_gather.14
  341.2 5.5 all_gather.15
  347.0 34.9 %psum.95 = f32[40,40]{1,0:T(8,128)S(1)} all-reduce(f32[40,40]{1,0:T(8,128)S(1)} %convolution_bitcast_fusion.6), channel_id=1, replica_groups=mesh['batch'=8,'task'=4] {'batch'}, use_global_device_ids=true, to_apply=%region_11.12 | all-reduce | flops 1600 | bytes 12800 | tf_op jit(solution)/shard_map/psum | solution.py:178
  383.1 67.5 %while.13 = (s32[]{:T(128)}, f32[40]{0:T(128)S(1)}, f32[40,40]{1,0:T(8,128)S(1)}, s32[]{:T(128)}, f32[]{:T(128)}, /*index=5*/f32[]{:T(128)}) while((s32[]{:T(128)}, f32[40]{0:T(128)S(1)}, f32[40,40]{1,0:T(8,128)S(1)}, s32[]{:T(128)}, f32[]{:T(128)}, /*index=5*/f32[]{:T(128)}) %tuple.67), condition=%wide.region_16.17_spmd, body=%wide.region_13.16_spmd.sunk | while | flops 19564 | bytes 7501 | solution.py:125
  453.2 16.3 %reduce-scatter.10.cloned.1.call-done = f32[128,2]{1,0:T(8,128)} async-done(((f32[512,2]{1,0:T(8,128)}), f32[128,2]{1,0:T(8,128)}) %reduce-scatter.10.cloned.1.call-update) | async-done | bytes 1040
  474.8 21.4 %all-reduce.23 = (f32[128]{0:T(128)S(1)}, f32[128]{0:T(128)S(1)}) all-reduce(f32[128]{0:T(128)S(1)} %get-tuple-element.102, f32[128]{0:T(128)S(1)} %get-tuple-element.101), channel_id=1, replica_groups=mesh['batch'=8,'task'=4] {'batch'}, use_global_device_ids=true, to_apply=%region_21.22 | all-reduce | flops 256 | bytes 2048 | tf_op jit(solution)/shard_map/psum | solution.py:71
  496.2 5.3 broadcast_multiply_fusion.1
  508.7 6.5 copy-done.4
  515.2 14.3 %convolution_bitcast_fusion.4 = f32[2,512,4096]{1,2,0:T(8,128)} fusion(bf16[2,9,128,4096]{2,3,0,1:T(8,128)(2,1)S(1)} %bitcast_dynamic-update-slice_fusion.9, bf16[9,128,512]{2,1,0:T(8,128)(2,1)S(1)} %copy-done), kind=kOutput, calls=%fused_computation.9 | convolution fusion | flops 9663676416 | bytes 36831232 | tf_op jit(solution)/shard_map/koc,nkop->ncp/dot_general | solution.py:108
  530.0 122.1 %reduce-scatter.6.cloned.1.call-done = f32[2,128,4096]{1,2,0:T(8,128)} async-done(((f32[2,512,4096]{1,2,0:T(8,128)}), f32[2,128,4096]{1,2,0:T(8,128)}) %reduce-scatter.6.cloned.1.call-update) | async-done | bytes 4194320 | tf_op jit(solution)/shard_map/reduce_scatter | solution.py:111
  652.0 6.0 multiply_reduce_fusion.1
  658.1 38.0 %all-reduce.22 = (f32[128]{0:T(128)S(1)}, f32[128]{0:T(128)S(1)}, f32[512,10]{0,1:T(8,128)}, f32[10]{0:T(128)}) all-reduce(f32[128]{0:T(128)S(1)} %get-tuple-element.104, f32[128]{0:T(128)S(1)} %get-tuple-element.103, f32[512,10]{0,1:T(8,128)S(1)} %fusion.75, ...), channel_id=1, replica_groups=mesh['batch'=8,'task'=4] {'batch'}, use_global_device_ids=true, to_apply=%region_26.27 | all-reduce | flops 5386 | bytes 43088 | tf_op jit(solution)/shard_map/psum | solution.py:71
  707.6 6.4 copy-done.5
  714.1 14.2 %convolution_bitcast_fusion.3 = f32[2,512,4096]{1,2,0:T(8,128)} fusion(bf16[2,9,128,4096]{2,3,0,1:T(8,128)(2,1)S(1)} %bitcast_dynamic-update-slice_fusion, bf16[9,128,512]{2,1,0:T(8,128)(2,1)S(1)} %copy-done.20), kind=kOutput, calls=%fused_computation.8 | convolution fusion | flops 9663676416 | bytes 36831232 | tf_op jit(solution)/shard_map/koc,nkop->ncp/dot_general | solution.py:108
  728.6 20.7 %fusion.42 = f32[9,128,512]{2,1,0:T(8,128)} fusion(bf16[2,9,128,4096]{2,3,0,1:T(8,128)(2,1)} %copy-done.4, bf16[2,512,4096]{1,2,0:T(8,128)(2,1)} %all-gather.5.cloned.1.call-done), kind=kOutput, calls=%fused_computation.103 | convolution fusion | flops 9663676416 | bytes 29622272 | tf_op jit(solution)/shard_map/nkop,ncp->koc/dot_general | solution.py:200
  751.8 13.6 %fusion.39 = f32[9,128,512]{2,1,0:T(8,128)} fusion(bf16[2,9,128,4096]{2,3,0,1:T(8,128)(2,1)S(1)} %copy-done.6, bf16[2,512,4096]{1,2,0:T(8,128)(2,1)} %all-gather.3.cloned.1.call-done), kind=kOutput, calls=%fused_computation.102 | convolution fusion | flops 9663676416 | bytes 29622272 | tf_op jit(solution)/shard_map/nkop,ncp->koc/dot_general | solution.py:210
  765.5 85.4 %reduce-scatter.8.cloned.1.call-done = f32[2,128,4096]{1,2,0:T(8,128)} async-done(((f32[2,512,4096]{1,2,0:T(8,128)}), f32[2,128,4096]{1,2,0:T(8,128)}) %reduce-scatter.8.cloned.1.call-update) | async-done | bytes 4194320 | tf_op jit(solution)/shard_map/reduce_scatter | solution.py:111
  850.9 5.9 fusion.80
  856.7 5.6 copy.44
  862.3 163.1 %all-reduce.27.cloned.1.call-done = (f32[9,128,512]{2,1,0:T(8,128)}, f32[9,128,512]{2,1,0:T(8,128)}) async-done(((f32[9,128,512]{2,1,0:T(8,128)}, f32[9,128,512]{2,1,0:T(8,128)}), (f32[9,128,512]{2,1,0:T(8,128)}, f32[9,128,512]{2,1,0:T(8,128)})) %all-reduce.27.cloned.1.call-update) | async-done | bytes 4718608 | tf_op jit(solution)/shard_map/psum | solution.py:214
  (176 shorter events, 126.3 us)
Async XLA Ops:
  7.2 226.7 %copy-start = (bf16[9,128,512]{2,1,0:T(8,128)(2,1)S(1)}, bf16[9,128,512]{2,1,0:T(8,128)(2,1)}, u32[]{:S(2)}) copy-start(bf16[9,128,512]{2,1,0:T(8,128)(2,1)} %param.18) | copy-start | bytes 3538948
  7.2 4.4 copy-start.22
  7.2 66.6 %copy-start.19 = (bf16[9,128,512]{2,1,0:T(8,128)(2,1)S(1)}, bf16[9,128,512]{2,1,0:T(8,128)(2,1)}, u32[]{:S(2)}) copy-start(bf16[9,128,512]{2,1,0:T(8,128)(2,1)} %param.15) | copy-start | bytes 3538948
  7.2 66.6 %all-gather.3.cloned.1.call-start = ((), (), s32[]{:S(2)}) async-start(), calls=%async_computation.3 | async-start | bytes 10485760 | tf_op jit(solution)/shard_map/all_gather | solution.py:37
  11.5 222.3 %all-gather.5.cloned.1.call-start = ((), (), s32[]{:S(2)}) async-start(), calls=%async_computation.4 | async-start | bytes 10485760 | tf_op jit(solution)/shard_map/all_gather | solution.py:37
  129.7 41.9 %copy-start.11 = (f32[128]{0:T(128)S(1)}, f32[128]{0:T(128)}, u32[]{:S(2)}) copy-start(f32[128]{0:T(128)} %param.16) | copy-start | bytes 1540
  129.7 41.9 %copy-start.13 = (f32[128]{0:T(128)S(1)}, f32[128]{0:T(128)}, u32[]{:S(2)}) copy-start(f32[128]{0:T(128)} %param.17) | copy-start | bytes 1540
  171.6 5.5 copy-start.18
  171.6 7.4 copy-start.7
  176.5 292.9 %reduce-scatter.10.cloned.1.call-start = ((), (), s32[]{:S(2)}) async-start(), calls=%async_computation.7 | async-start | bytes 327680
  289.8 42.0 %copy-start.9 = (f32[128]{0:T(128)S(1)}, f32[128]{0:T(128)}, u32[]{:S(2)}) copy-start(f32[128]{0:T(128)} %param.19) | copy-start | bytes 1540
  289.8 42.0 %copy-start.2 = (bf16[2,128,4096]{1,2,0:T(8,128)(2,1)S(1)}, bf16[2,128,4096]{1,2,0:T(8,128)(2,1)}, u32[]{:S(2)}) copy-start(bf16[2,128,4096]{1,2,0:T(8,128)(2,1)} %copy.33) | copy-start | bytes 6291460
  289.8 42.0 %copy-start.10 = (f32[128]{0:T(128)S(1)}, f32[128]{0:T(128)}, u32[]{:S(2)}) copy-start(f32[128]{0:T(128)} %param.20) | copy-start | bytes 1540
  314.7 26.1 %copy-start.21 = (s32[2,10]{1,0:T(2,128)S(1)}, s32[2,10]{1,0:T(2,128)}, u32[]{:S(2)}) copy-start(s32[2,10]{1,0:T(2,128)} %param.23) | copy-start | bytes 244
  314.7 26.1 %copy-start.23 = (f32[10]{0:T(128)S(1)}, f32[10]{0:T(128)}, u32[]{:S(2)}) copy-start(f32[10]{0:T(128)} %param.22) | copy-start | bytes 124
  335.8 165.7 %copy-start.12 = (f32[2,128]{1,0:T(2,128)}, f32[2,128]{1,0:T(2,128)S(1)}, u32[]{:S(2)}) copy-start(f32[2,128]{1,0:T(2,128)S(1)} %broadcast_multiply_fusion.9) | copy-start | bytes 3076
  450.6 50.8 %copy-start.8 = (f32[40]{0:T(128)}, f32[40]{0:T(128)S(1)}, u32[]{:S(2)}) copy-start(f32[40]{0:T(128)S(1)} %get-tuple-element.214) | copy-start | bytes 484
  452.9 199.1 %reduce-scatter.6.cloned.1.call-start = ((), (), s32[]{:S(2)}) async-start(), calls=%async_computation.5 | async-start | bytes 20971520 | tf_op jit(solution)/shard_map/reduce_scatter | solution.py:111
  496.1 5.3 copy-start.14
  496.1 5.3 copy-start.15
  508.7 6.5 copy-start.4
  529.5 321.4 %reduce-scatter.8.cloned.1.call-start = ((), (), s32[]{:S(2)}) async-start(), calls=%async_computation.6 | async-start | bytes 20971520 | tf_op jit(solution)/shard_map/reduce_scatter | solution.py:111
  696.1 4.2 copy-start.16
  696.1 4.3 copy-start.17
  706.6 7.4 copy-start.20
  707.6 6.5 copy-start.5
  728.3 297.1 %all-reduce.27.cloned.1.call-start = ((), (), s32[]{:S(2)}) async-start(), calls=%async_computation.8 | async-start | bytes 9437184 | tf_op jit(solution)/shard_map/psum | solution.py:214
  728.6 23.2 %copy-start.6 = (bf16[2,9,128,4096]{2,3,0,1:T(8,128)(2,1)S(1)}, bf16[2,9,128,4096]{2,3,0,1:T(8,128)(2,1)}, u32[]{:S(2)}) copy-start(bf16[2,9,128,4096]{2,3,0,1:T(8,128)(2,1)} %copy-done.5) | copy-start | bytes 56623108
  1025.4 3.4 copy-start.3
  1025.4 4.8 copy-start.1
Sparse Core Ops, SparseCore 0:
  11.6 62.0 all-gather.2
  176.6 57.1 all-gather.4
  453.0 16.3 reduce-scatter.9
  529.6 122.4 reduce-scatter.5
  728.4 122.4 reduce-scatter.7
  855.4 169.9 all-reduce.26
where the time goes:
time: 1050 us; the launch traced here: 1040 us
  waiting for transfers between devices  501 us (48%)
  blocking collectives  182 us (17%)
  other arithmetic  128 us (12%)
  matrix products  124 us (12%)
  local copies, waits for them, and re-layouts  83.5 us (8%)
  between operations  16.4 us (2%)
    reduce_scatter x2, waiting for transfers between devices, input_side(): lax.psum_scatter(partial_terms, 'task', scatter_dimension=1, tiled=True)  207 us
    psum x1, waiting for transfers between devices, on_device(): lax.psum((conv1_grad, conv2_grad, head_weight_grad, head_bias_grad), 'bat...  163 us
    all_gather x2, waiting for transfers between devices, gather_channels(): return lax.all_gather(values, 'task', axis=1, tiled=True)  114 us
    psum x4, blocking collectives, batch_total(): return lax.psum(values, 'batch')  77.1 us
    psum x2, blocking collectives, norm_backward(): lax.psum((jnp.sum(grad_out * normalized * row_weights, axis=(0, 2)), jnp....  59.4 us
    dot_general x2, matrix products, convolve(): jnp.einsum('oc,ncp->nop', stacked, full_input, preferred_element_type=jnp...  44.4 us
    slice x2, local copies, waits for them, and re-layouts, convolve(): products[:, kernel_tap * shard_width:(kernel_tap + 1) * shard_width, :]  42.2 us
    unnamed x69, local copies, waits for them, and re-layouts  39.2 us
  transfers between devices with their start and end apart: 6, of which 6 were waited for; matrix products, arithmetic and copies ran while one was open for 5% of the time, Pallas kernels for 0%

commit v1 on v0

v1 whole, which is shorter than its diff:
```python
import functools

import jax
import jax.numpy as jnp
from jax import lax
from jax.experimental import pallas as pl
from jax.experimental.pallas import tpu as pltpu
from jax.sharding import PartitionSpec as P

SIDE = 64
FW_STEPS = 20
LANES = 128
ROWS = 8

eps = 1e-05
loss_scale = 4096.0
highest = lax.Precision.HIGHEST
f32 = jnp.float32
bf16 = jnp.bfloat16


def params(mib, **more):
    return pltpu.CompilerParams(vmem_limit_bytes=mib << 20, **more)


def cost(flops, moved):
    return pl.CostEstimate(flops=flops, bytes_accessed=moved, transcendentals=0)


VM = pl.BlockSpec(memory_space=pltpu.VMEM)
SM = pl.BlockSpec(memory_space=pltpu.SMEM)


def sigmoid(v):
    return 1.0 / (1.0 + jnp.exp(-v))


def silu_slope(v):
    s = sigmoid(v)
    return s * (1.0 + v * (1.0 - s))


def half(h):
    return slice(h * LANES, (h + 1) * LANES)


def fill_shifted(dst, src, col0, rows):
    width = src.shape[1]
    cols = slice(col0, col0 + width)
    block = 512
    zero = jnp.zeros((3, SIDE, width), bf16)
    dst[:, 0:SIDE, cols] = zero
    dst[:, SIDE + rows : SIDE + rows + SIDE, cols] = zero

    def step(i, carry):
        at = pl.multiple_of(i * block, block)
        low = src[pl.ds(at, block), :]
        to = pl.ds(pl.multiple_of(at + SIDE, SIDE), block)
        dst[1, to, cols] = low
        value = low.astype(f32)
        column = lax.broadcasted_iota(jnp.int32, (block, width), 0) & (SIDE - 1)
        dst[0, to, cols] = jnp.where(column == 0, 0.0, pltpu.roll(value, 1, 0)).astype(bf16)
        dst[2, to, cols] = jnp.where(column == SIDE - 1, 0.0, pltpu.roll(value, block - 1, 0)).astype(bf16)
        return carry

    lax.fori_loop(0, rows // block, step, 0)


def send_rows(out, rows):
    n = out.shape[0]
    out[...] = jnp.zeros(out.shape, f32)
    for at, value in rows:
        out[:, at : at + 1, :] = jnp.broadcast_to(value[None], (n, 1, LANES))


def weighted(got, weight, row):
    return jnp.sum(got[:, row, :] * weight, axis=0, keepdims=True)


def norm_coefs(got, weight_ref, h, rows):
    weight = weight_ref[...]
    count = jnp.sum(weight, axis=0, keepdims=True)
    means = got[:, h, :]
    mean = jnp.sum(means * weight, axis=0, keepdims=True) / count
    away = means - mean
    squares = jnp.sum((got[:, 2 + h, :] + rows * (away * away)) * weight, axis=0, keepdims=True)
    return mean, lax.rsqrt(squares / (count * rows) + eps)


def conv_kernel(n_parts, *refs):
    xs, w, out, stats, scratch = refs[:n_parts], *refs[n_parts:]
    rows, width = out.shape
    chunk = 1024
    for i in range(n_parts):
        fill_shifted(scratch, xs[i], i * width, rows)

    def step(j, total):
        at = pl.multiple_of(j * chunk, chunk)
        acc = None
        for k in range(9):
            dy, dx = k // 3 - 1, k % 3 - 1
            lhs = scratch[dx + 1, pl.ds(pl.multiple_of(at + SIDE * (dy + 1), SIDE), chunk), :]
            term = lax.dot_general(lhs, w[k], (((1,), (1,)), ((), ())), preferred_element_type=f32)
            acc = term if acc is None else acc + term
        out[pl.ds(at, chunk), :] = acc
        return total + jnp.sum(acc, axis=0, keepdims=True)

    total = lax.fori_loop(0, rows // chunk, step, jnp.zeros((1, width), f32))
    mean = total / rows

    def spread(j, acc):
        away = out[pl.ds(pl.multiple_of(j * chunk, chunk), chunk), :] - mean
        return acc + jnp.sum(away * away, axis=0, keepdims=True)

    squares = lax.fori_loop(0, rows // chunk, spread, jnp.zeros((1, width), f32))
    send_rows(
        stats,
        [(h, mean[:, half(h)]) for h in range(width // LANES)]
        + [(2 + h, squares[:, half(h)]) for h in range(width // LANES)],
    )


def conv_stats(x_parts, w, n_devices):
    rows, width = x_parts[0].shape
    n = len(x_parts)
    return pl.pallas_call(
        functools.partial(conv_kernel, n),
        in_specs=[VM] * (n + 1),
        out_specs=(VM, VM),
        out_shape=(
            jax.ShapeDtypeStruct((rows, width), f32),
            jax.ShapeDtypeStruct((n_devices, ROWS, LANES), f32),
        ),
        scratch_shapes=[pltpu.VMEM((3, rows + 2 * SIDE, n * width), bf16)],
        compiler_params=params(40),
        cost_estimate=cost(2 * 9 * rows * width * width * n, 16 << 20),
        name="conv_stats",
    )(*x_parts, w)


def act_kernel(c, got, weight, vecs, out, coefs):
    rows = loss_scale
    for h in range(c.shape[1] // LANES):
        mean, scale = norm_coefs(got, weight, h, rows)
        coefs[h : h + 1, :] = mean
        coefs[2 + h : 3 + h, :] = scale
        normed = (c[:, half(h)] - mean) * scale * vecs[h : h + 1, :] + vecs[2 + h : 3 + h, :]
        out[:, half(h)] = (normed * sigmoid(normed)).astype(bf16)


def blocked(block, width):
    return pl.BlockSpec((block, width), lambda i: (i, 0))


def whole(shape):
    return pl.BlockSpec(shape, lambda i: (0,) * len(shape))


def activate(c, got, weight, vecs):
    rows, width = c.shape
    block = 512
    return pl.pallas_call(
        act_kernel,
        grid=(rows // block,),
        in_specs=[blocked(block, width), whole(got.shape), whole(weight.shape), whole(vecs.shape)],
        out_specs=(blocked(block, width), whole((ROWS, LANES))),
        out_shape=(
            jax.ShapeDtypeStruct((rows, width), bf16),
            jax.ShapeDtypeStruct((ROWS, LANES), f32),
        ),
        compiler_params=params(16),
        cost_estimate=cost(20 * rows * width, 6 * rows * width),
        name="activate",
    )(c, got, weight, vecs)


def pool_kernel(meta, c, x, got, weight, vecs, labels, out, coefs, sums):
    step, last = pl.program_id(0), pl.num_programs(0) - 1
    halves = c.shape[1] // LANES

    @pl.when(step == 0)
    def _():
        sums[...] = jnp.zeros_like(sums)

    for h in range(halves):
        mean, scale = norm_coefs(got, weight, h, loss_scale)
        coefs[h : h + 1, :] = mean
        coefs[2 + h : 3 + h, :] = scale
        hat = (c[:, half(h)] - mean) * scale
        v = hat * vecs[4 + h : 5 + h, :] + vecs[6 + h : 7 + h, :] + x[:, half(h)].astype(f32)
        s = sigmoid(v)
        slope = s * (1.0 + v * (1.0 - s))
        sums[h : h + 1, :] += jnp.sum(v * s, axis=0, keepdims=True)
        sums[2 + h : 3 + h, :] += jnp.sum(slope * hat, axis=0, keepdims=True)
        sums[4 + h : 5 + h, :] += jnp.sum(slope, axis=0, keepdims=True)

    @pl.when(step == last)
    def _():
        valid = meta[3].astype(f32)
        rows = []
        for h in range(halves):
            rows.append((h, sums[h : h + 1, :] * (valid / loss_scale)))
            rows.append((2 + h, sums[2 + h : 3 + h, :]))
            rows.append((4 + h, sums[4 + h : 5 + h, :]))
        rows.append((6, labels[0:1, :]))
        rows.append((7, labels[1:2, :]))
        send_rows(out, rows)


def pool(meta, c, x, got, weight, vecs, labels):
    rows, width = c.shape
    block = 512
    return pl.pallas_call(
        pool_kernel,
        grid=(rows // block,),
        in_specs=[
            SM,
            blocked(block, width),
            blocked(block, width),
            whole(got.shape),
            whole(weight.shape),
            whole(vecs.shape),
            whole(labels.shape),
        ],
        out_specs=(whole(got.shape), whole((ROWS, LANES))),
        out_shape=(
            jax.ShapeDtypeStruct(got.shape, f32),
            jax.ShapeDtypeStruct((ROWS, LANES), f32),
        ),
        scratch_shapes=[pltpu.VMEM((ROWS, LANES), f32)],
        compiler_params=params(16),
        cost_estimate=cost(30 * rows * width, 6 * rows * width),
        name="pool",
    )(meta, c, x, got, weight, vecs, labels)


def head_kernel(n_parts, meta, got, ht, bias, valid, avg_row, avg_col, coefs, tw, an, hwg, hbg, pooled_own, pooled, slopes, shifts, labels, grads, mine_all, pooled_part):
    tasks, channels = ht.shape
    images = valid.shape[0]
    n_task = 2 * n_parts
    width = channels // n_parts
    halves = width // LANES
    r = meta[2]
    for n in range(images):
        base = (n // 2) * n_task + (n % 2) * n_parts
        for part in range(n_parts):
            for h in range(halves):
                lo = part * width + h * LANES
                pooled[n : n + 1, lo : lo + LANES] = got[base + part, h : h + 1, :]
        for h in range(halves):
            slopes[n : n + 1, half(h)] = got[base + r, 2 + h : 3 + h, :]
            shifts[n : n + 1, half(h)] = got[base + r, 4 + h : 5 + h, :]
        row = 6 + n % 2
        lab = got[(n // 2) * n_task, row : row + 1, :]
        for t in range(1, n_task):
            lab = lab + got[(n // 2) * n_task + t, row : row + 1, :]
        labels[n : n + 1, :] = lab
    pooled_all = pooled[...]
    table = ht[...]
    both_last = (((1,), (1,)), ((), ()))
    both_first = (((0,), (0,)), ((), ()))
    logits = lax.dot_general(pooled_all, table, both_last, precision=highest, preferred_element_type=f32) + bias[...]
    count = jnp.sum(valid[...], axis=0, keepdims=True)
    errors = valid[...] * (sigmoid(logits) - labels[:, 0:tasks]) / count
    gram = lax.dot_general(errors, errors, both_first, precision=highest, preferred_element_type=f32) * lax.dot_general(
        table, table, both_last, precision=highest, preferred_element_type=f32
    )
    row_id = lax.broadcasted_iota(jnp.int32, (tasks, tasks), 0)
    col_id = lax.broadcasted_iota(jnp.int32, (tasks, tasks), 1)
    trace = jnp.sum(jnp.sum(jnp.where(row_id == col_id, gram, 0.0), axis=1, keepdims=True), axis=0, keepdims=True)
    normalized = gram / (trace / tasks)
    start_row = avg_row[...] / jnp.sum(avg_row[...], axis=1, keepdims=True)
    start_col = avg_col[...] / jnp.sum(avg_col[...], axis=0, keepdims=True)
    w_row, w_col = start_row, start_col
    for j in range(FW_STEPS):
        rate = 1.0 / (j + 4.0)
        z_col = -tasks * jnp.sum(normalized * w_row, axis=1, keepdims=True)
        z_row = -tasks * jnp.sum(normalized * w_col, axis=0, keepdims=True)
        e_col = jnp.exp(z_col - jnp.max(z_col, axis=0, keepdims=True))
        e_row = jnp.exp(z_row - jnp.max(z_row, axis=1, keepdims=True))
        w_col = (1.0 - rate) * w_col + rate * (e_col / jnp.sum(e_col, axis=0, keepdims=True))
        w_row = (1.0 - rate) * w_row + rate * (e_row / jnp.sum(e_row, axis=1, keepdims=True))
    tw[...] = w_row
    an[...] = 0.9 * start_row + 0.1 * w_row
    logit_grads = errors * ((loss_scale * tasks) * w_row)
    hbg[...] = jnp.sum(logit_grads, axis=0, keepdims=True)
    hwg[...] = lax.dot_general(logit_grads, pooled_all, both_first, precision=highest, preferred_element_type=f32)
    grads[...] = jnp.dot(logit_grads, table, precision=highest, preferred_element_type=f32) / loss_scale
    own = pl.ds(pl.multiple_of(r * width, LANES), width)
    q = grads[:, own]
    mine_all[...] = q
    pooled_part[...] = pooled[:, own]
    gain = jnp.sum(q * slopes[...], axis=0, keepdims=True)
    shift = jnp.sum(q * shifts[...], axis=0, keepdims=True)
    mine = mine_all[pl.ds(2 * meta[0] + meta[1], 1), :]
    coefs[...] = jnp.zeros(coefs.shape, f32)
    for h in range(halves):
        coefs[h : h + 1, :] = gain[:, half(h)]
        coefs[2 + h : 3 + h, :] = shift[:, half(h)]
        coefs[4 + h : 5 + h, :] = mine[:, half(h)]
    for i in range(2):
        pooled_own[i : i + 1, :] = pooled_part[pl.ds(2 * meta[0] + i, 1), :]


def head(meta, got, ht, bias, valid, avg_row, avg_col, n_parts):
    tasks, channels = ht.shape
    images = valid.shape[0]
    width = channels // n_parts
    shapes = [(ROWS, LANES), (1, tasks), (1, tasks), (tasks, channels), (1, tasks), (2, width)]
    return pl.pallas_call(
        functools.partial(head_kernel, n_parts),
        in_specs=[SM] + [VM] * 6,
        out_specs=tuple(VM for _ in shapes),
        out_shape=tuple(jax.ShapeDtypeStruct(s, f32) for s in shapes),
        scratch_shapes=[
            pltpu.VMEM((images, channels), f32),
            pltpu.VMEM((images, width), f32),
            pltpu.VMEM((images, width), f32),
            pltpu.VMEM((images, LANES), f32),
            pltpu.VMEM((images, channels), f32),
            pltpu.VMEM((images, width), f32),
            pltpu.VMEM((images, width), f32),
        ],
        compiler_params=params(16),
        cost_estimate=cost(1 << 20, 1 << 20),
        name="head",
    )(meta, got, ht, bias, valid, avg_row, avg_col)


def grad_two_kernel(meta, c, x, coefs, vecs, heads, pixels, low, summed):
    valid = meta[3].astype(f32)
    for h in range(c.shape[1] // LANES):
        mean, scale = coefs[h : h + 1, :], coefs[2 + h : 3 + h, :]
        gain = vecs[4 + h : 5 + h, :]
        hat = (c[:, half(h)] - mean) * scale
        v = hat * gain + vecs[6 + h : 7 + h, :] + x[:, half(h)].astype(f32)
        dn = (valid * heads[4 + h : 5 + h, :]) * silu_slope(v)
        summed[:, half(h)] = dn
        away = (heads[2 + h : 3 + h, :] + hat * heads[h : h + 1, :]) / pixels[0]
        low[:, half(h)] = ((valid * gain * scale) * (dn - away)).astype(bf16)


def grad_two(meta, c, x, coefs, vecs, heads, pixels):
    rows, width = c.shape
    block = 512
    return pl.pallas_call(
        grad_two_kernel,
        grid=(rows // block,),
        in_specs=[
            SM,
            blocked(block, width),
            blocked(block, width),
            whole(coefs.shape),
            whole(vecs.shape),
            whole(heads.shape),
            SM,
        ],
        out_specs=(blocked(block, width), blocked(block, width)),
        out_shape=(
            jax.ShapeDtypeStruct((rows, width), bf16),
            jax.ShapeDtypeStruct((rows, width), f32),
        ),
        compiler_params=params(16),
        cost_estimate=cost(30 * rows * width, 12 * rows * width),
        name="grad_two",
    )(meta, c, x, coefs, vecs, heads, pixels)


def grad_one_kernel(meta, c, dn, got, weight, coefs, vecs, pixels, low, sums):
    valid = meta[3].astype(f32)
    for h in range(c.shape[1] // LANES):
        gain_grad = weighted(got, weight[...], h)
        bias_grad = weighted(got, weight[...], 2 + h)
        sums[h : h + 1, :] = gain_grad
        sums[2 + h : 3 + h, :] = bias_grad
        mean, scale = coefs[h : h + 1, :], coefs[2 + h : 3 + h, :]
        hat = (c[:, half(h)] - mean) * scale
        away = (bias_grad + hat * gain_grad) / pixels[0]
        low[:, half(h)] = ((valid * vecs[h : h + 1, :] * scale) * (dn[:, half(h)] - away)).astype(bf16)


def grad_one(meta, c, dn, got, weight, coefs, vecs, pixels):
    rows, width = c.shape
    block = 512
    return pl.pallas_call(
        grad_one_kernel,
        grid=(rows // block,),
        in_specs=[
            SM,
            blocked(block, width),
            blocked(block, width),
            whole(got.shape),
            whole(weight.shape),
            whole(coefs.shape),
            whole(vecs.shape),
            SM,
        ],
        out_specs=(blocked(block, width), whole((ROWS, LANES))),
        out_shape=(
            jax.ShapeDtypeStruct((rows, width), bf16),
            jax.ShapeDtypeStruct((ROWS, LANES), f32),
        ),
        compiler_params=params(16),
        cost_estimate=cost(10 * rows * width, 10 * rows * width),
        name="grad_one",
    )(meta, c, dn, got, weight, coefs, vecs, pixels)


def back_products(scratch, w, at, chunk):
    acc = None
    for k in range(9):
        dy, dx = k // 3 - 1, k % 3 - 1
        lhs = scratch[1 - dx, pl.ds(pl.multiple_of(at + SIDE * (1 - dy), SIDE), chunk), :]
        term = jnp.dot(lhs, w[k], preferred_element_type=f32)
        acc = term if acc is None else acc + term
    return acc


def back_two_kernel(n_parts, *refs):
    meta, gs = refs[0], refs[1 : 1 + n_parts]
    w, c, coefs, vecs, out, stats, scratch = refs[1 + n_parts :]
    rows, width = out.shape
    halves = width // LANES
    chunk = 1024
    for i in range(n_parts):
        fill_shifted(scratch, gs[i], i * width, rows)

    def step(j, carry):
        at = pl.multiple_of(j * chunk, chunk)
        acc = back_products(scratch, w, at, chunk)
        sums = []
        for h in range(halves):
            hat = (c[pl.ds(at, chunk), half(h)] - coefs[h : h + 1, :]) * coefs[2 + h : 3 + h, :]
            dn = acc[:, half(h)] * silu_slope(hat * vecs[h : h + 1, :] + vecs[2 + h : 3 + h, :])
            out[pl.ds(at, chunk), half(h)] = dn
            sums.append(carry[2 * h] + jnp.sum(dn * hat, axis=0, keepdims=True))
            sums.append(carry[2 * h + 1] + jnp.sum(dn, axis=0, keepdims=True))
        return tuple(sums)

    zero = jnp.zeros((1, LANES), f32)
    sums = lax.fori_loop(0, rows // chunk, step, (zero,) * (2 * halves))
    send_rows(stats, [(2 * i + h, sums[2 * h + i]) for h in range(halves) for i in range(2)])


def back_two(meta, g_parts, w, c, coefs, vecs, n_devices):
    rows, width = c.shape
    n = len(g_parts)
    return pl.pallas_call(
        functools.partial(back_two_kernel, n),
        in_specs=[SM] + [VM] * (n + 4),
        out_specs=(VM, VM),
        out_shape=(
            jax.ShapeDtypeStruct((rows, width), f32),
            jax.ShapeDtypeStruct((n_devices, ROWS, LANES), f32),
        ),
        scratch_shapes=[pltpu.VMEM((3, rows + 2 * SIDE, n * width), bf16)],
        compiler_params=params(44),
        cost_estimate=cost(2 * 9 * rows * width * width * n, 16 << 20),
        name="back_two",
    )(meta, *g_parts, w, c, coefs, vecs)


def back_one_kernel(n_parts, *refs):
    meta, gs = refs[0], refs[1 : 1 + n_parts]
    w, summed, keep, send, scratch = refs[1 + n_parts :]
    rows, width = summed.shape
    cs = width // 2
    chunk = 1024
    first = meta[1] == 0
    for i in range(n_parts):
        fill_shifted(scratch, gs[i], i * width, rows)

    def step(j, carry):
        at = pl.multiple_of(j * chunk, chunk)
        acc = back_products(scratch, w, at, chunk) + summed[pl.ds(at, chunk), :]
        a, b = acc[:, :cs], acc[:, cs:]
        keep[:, pl.ds(at, chunk)] = jnp.where(first, a, b).T
        send[:, pl.ds(at, chunk)] = jnp.where(first, b, a).T.astype(bf16)
        return carry

    lax.fori_loop(0, rows // chunk, step, 0)


def back_one(meta, g_parts, w, summed):
    rows, width = summed.shape
    n = len(g_parts)
    return pl.pallas_call(
        functools.partial(back_one_kernel, n),
        in_specs=[SM] + [VM] * (n + 2),
        out_specs=(VM, VM),
        out_shape=(
            jax.ShapeDtypeStruct((width // 2, rows), f32),
            jax.ShapeDtypeStruct((width // 2, rows), bf16),
        ),
        scratch_shapes=[pltpu.VMEM((3, rows + 2 * SIDE, n * width), bf16)],
        compiler_params=params(40),
        cost_estimate=cost(2 * 9 * rows * width * width * n, 16 << 20),
        name="back_one",
    )(meta, *g_parts, w, summed)


def weight_kernel(n_parts, *refs):
    meta, g, xs = refs[0], refs[1], refs[2 : 2 + n_parts]
    keep, send, scratch = refs[2 + n_parts :]
    rows, width = g.shape
    cs = width // 2
    first = meta[1] == 0
    fill_shifted(scratch, g, 0, rows)
    for k in range(9):
        dy, dx = k // 3 - 1, k % 3 - 1
        lo = SIDE * (1 - dy)
        lhs = scratch[1 - dx, lo : lo + rows, :]
        for i in range(n_parts):
            term = lax.dot_general(lhs, xs[i][...], (((0,), (0,)), ((), ())), preferred_element_type=f32)
            a, b = term[:cs], term[cs:]
            cols = slice(i * width, (i + 1) * width)
            keep[k, :, cols] = jnp.where(first, a, b)
            send[k, :, cols] = jnp.where(first, b, a).astype(bf16)


def weight_grad(meta, g, x_parts):
    rows, width = g.shape
    n = len(x_parts)
    shape = (9, width // 2, n * width)
    return pl.pallas_call(
        functools.partial(weight_kernel, n),
        in_specs=[SM] + [VM] * (n + 1),
        out_specs=(VM, VM),
        out_shape=(jax.ShapeDtypeStruct(shape, f32), jax.ShapeDtypeStruct(shape, bf16)),
        scratch_shapes=[pltpu.VMEM((3, rows + 2 * SIDE, width), bf16)],
        compiler_params=params(32),
        cost_estimate=cost(2 * 9 * rows * width * width * n, 16 << 20),
        name="weight_grad",
    )(meta, g, *x_parts)


def swap(values, axis, by):
    n = lax.axis_size(axis)
    return lax.ppermute(values, axis, [(i, i ^ by) for i in range(n)])


def xor_order(values, axis, r, n):
    bit = 1
    while bit < n:
        shape = values.shape
        split = values.reshape(shape[:axis] + (n // (2 * bit), 2, bit) + shape[axis + 1 :])
        values = jnp.where((r & bit) != 0, jnp.flip(split, axis + 1), split).reshape(shape)
        bit *= 2
    return values


def ordered(first, own, other, axis):
    return jnp.concatenate([jnp.where(first, own, other), jnp.where(first, other, own)], axis=axis)


def on_device(
    images,
    conv1_weight,
    norm1_gain,
    norm1_bias,
    conv2_weight,
    norm2_gain,
    norm2_bias,
    head_weight,
    head_bias,
    labels,
    image_counts,
    average_weights,
):
    n_task, n_batch = lax.axis_size("task"), lax.axis_size("batch")
    t, b = lax.axis_index("task"), lax.axis_index("batch")
    slots, cs, pixels = images.shape
    n_parts = n_task // slots
    g, r = t // n_parts, t % n_parts
    first = g == 0
    width = slots * cs
    channels = n_task * cs
    n_devices = n_task * n_batch
    tasks_here = head_weight.shape[1]
    tasks = tasks_here * n_task

    valid_images = (jnp.arange(slots)[None, :] < image_counts[:, None]).astype(f32)
    image_total = jnp.sum(image_counts).astype(f32)
    pixel_total = (image_total * pixels).reshape(1)
    own_valid = (g < lax.dynamic_index_in_dim(image_counts, b, keepdims=False)).astype(jnp.int32)
    meta = jnp.stack([b, g, r, own_valid]).astype(jnp.int32)
    same = (jnp.arange(n_parts) == r).astype(f32)
    weight = (valid_images[:, :, None] * same[None, None, :]).reshape(n_devices, 1)
    weight = jnp.broadcast_to(weight, (n_devices, LANES))

    def part_weights(w):
        full = ordered(first, w, swap(w, "task", n_parts), 1)
        full = full.reshape(9, width, slots, n_parts, cs).swapaxes(2, 3)
        return xor_order(full, 2, r, n_parts).reshape(9, width, channels)

    def back_weights(w):
        blocks = [w[:, :, i * width : (i + 1) * width] for i in range(n_parts)]
        return jnp.concatenate([blocks[0]] + [swap(blocks[i], "task", i) for i in range(1, n_parts)], axis=1)

    def all_parts(v):
        return [v] + [swap(v, "task", i) for i in range(1, n_parts)]

    w1 = part_weights(conv1_weight)
    pixel_major = jnp.swapaxes(images, 1, 2)
    own_image = jnp.where(first, pixel_major[0], pixel_major[1])
    other_image = jnp.where(first, pixel_major[1], pixel_major[0])
    x_own = ordered(first, own_image, swap(other_image, "task", n_parts), 1)
    x_parts = all_parts(x_own)
    w2 = part_weights(conv2_weight)

    lines = jnp.concatenate([norm1_gain, norm1_bias, norm2_gain, norm2_bias, head_bias])
    lines = jnp.pad(lines, (0, -lines.shape[0] % channels)).reshape(-1, channels)
    mine = jnp.concatenate([head_weight.T.astype(f32), lines])
    mine = jnp.pad(mine, ((0, -mine.shape[0] % ROWS), (0, 0)))
    gathered = lax.all_gather(mine, "task", axis=0)
    table = gathered[:, :tasks_here].reshape(tasks, slots, n_parts, cs)
    table = table.swapaxes(1, 2).reshape(tasks, channels)
    flat = gathered[:, tasks_here : tasks_here + lines.shape[0]].reshape(n_task, -1)
    bias_row = flat[:, 4 * cs : 4 * cs + tasks_here].reshape(1, tasks)
    vecs = flat[:, : 4 * cs].reshape(slots, n_parts, 4, cs)
    vecs = lax.dynamic_index_in_dim(vecs, r, axis=1, keepdims=False).swapaxes(0, 1).reshape(4, width)
    vecs = jnp.pad(vecs, ((0, 0), (0, 2 * LANES - width))).reshape(ROWS, LANES)
    label_rows = lax.dynamic_update_slice(
        jnp.zeros((slots, LANES), f32), labels.astype(f32), (0, t * tasks_here)
    )

    def exchange(rows):
        flat_rows = rows.reshape(n_devices * ROWS, LANES)
        return lax.all_to_all(flat_rows, ("batch", "task"), 0, 0, tiled=True).reshape(rows.shape)

    c1, stats = conv_stats(x_parts, w1, n_devices)
    a_own, coefs1 = activate(c1, exchange(stats), weight, vecs)
    a_parts = all_parts(a_own)
    c2, stats = conv_stats(a_parts, w2, n_devices)
    stats2 = exchange(stats)
    sums, coefs2 = pool(meta, c2, x_own, stats2, weight, vecs, label_rows)
    heads, task_weights, average_next, head_grad, bias_grad, pooled_rows = head(
        meta,
        exchange(sums),
        table,
        bias_row,
        valid_images.reshape(-1, 1),
        average_weights.reshape(1, -1),
        average_weights.reshape(-1, 1),
        n_parts,
    )

    def settle(keep, send):
        total = lax.psum(keep + swap(send, "task", n_parts).astype(f32), "batch")
        total = xor_order(total.reshape(9, cs, n_parts, slots, cs), 2, r, n_parts)
        return total.swapaxes(2, 3).reshape(9, cs, channels)

    low2, summed = grad_two(meta, c2, x_own, coefs2, vecs, heads, pixel_total)
    low2_parts = all_parts(low2)
    conv2_grad = settle(*weight_grad(meta, low2, a_parts))
    dn1, stats = back_two(meta, low2_parts, back_weights(w2), c1, coefs1, vecs, n_devices)
    low1, sums1 = grad_one(meta, c1, dn1, exchange(stats), weight, coefs1, vecs, pixel_total)
    low1_parts = all_parts(low1)
    conv1_grad = settle(*weight_grad(meta, low1, x_parts))
    keep, send = back_one(meta, low1_parts, back_weights(w1), summed)
    got = swap(send, "task", n_parts).astype(f32)
    input_grad = jnp.stack([jnp.where(first, keep, got), jnp.where(first, got, keep)])

    def own_slice(rows, at):
        line = rows[at : at + 2].reshape(-1)
        return lax.dynamic_slice_in_dim(line, g * cs, cs)

    head_weight_grad = lax.dynamic_slice_in_dim(head_grad, t * tasks_here, tasks_here, axis=0)
    head_weight_grad = head_weight_grad.reshape(tasks_here, n_parts, slots, cs).swapaxes(1, 2)
    head_weight_grad = head_weight_grad.reshape(tasks_here, channels).T
    head_bias_grad = lax.dynamic_slice_in_dim(bias_grad[0], t * tasks_here, tasks_here)
    pooled = lax.dynamic_slice_in_dim(pooled_rows, g * cs, cs, axis=1)
    return (
        pooled,
        input_grad,
        conv1_grad,
        own_slice(sums1, 0),
        own_slice(sums1, 2),
        conv2_grad,
        own_slice(heads, 0),
        own_slice(heads, 2),
        head_weight_grad,
        head_bias_grad,
        task_weights[0],
        average_next[0],
    )


def solution(mesh):
    in_specs = (
        P("batch", "task", None),
        P(None, "task", None),
        P("task"),
        P("task"),
        P(None, "task", None),
        P("task"),
        P("task"),
        P(None, "task"),
        P("task"),
        P("batch", "task"),
        P(),
        P(),
    )
    out_specs = (
        P("batch", "task"),
        P("batch", "task", None),
        P(None, "task", None),
        P("task"),
        P("task"),
        P(None, "task", None),
        P("task"),
        P("task"),
        P(None, "task"),
        P("task"),
        P(),
        P(),
    )
    return jax.shard_map(
        on_device, mesh=mesh, in_specs=in_specs, out_specs=out_specs, check_vma=False
    )
```

time: 1050 us -> 551 us (0.52)
  waiting for transfers between devices: 501 us -> 208 us
  blocking collectives: 182 us -> 48.9 us
  matrix products: 124 us -> 0 us
  Pallas kernels: 0 us -> 118 us
  other arithmetic: 128 us -> 36.8 us
  starting transfers between devices: 1.35 us -> 24.2 us
    reduce_scatter x2 -> x0, waiting for transfers between devices: 207 us -> none  [input_side(): lax.psum_scatter(partial_terms, 'task', scatter_dimension=1, tiled=True)]
    psum x7 -> x0, blocking collectives: 171 us -> none  [the longest x4 77.1 us: batch_total(): return lax.psum(values, 'batch')]
    dot_general x29 -> x0, matrix products: 123 us -> none  [the longest x2 44.4 us: convolve(): jnp.einsum('oc,ncp->nop', stacked, full_input, preferred_element_type=jnp...]
    pallas_call x0 -> x11, Pallas kernels: none -> 118 us  [the longest x2 32.1 us: conv_stats(): pl.pallas_call(functools.partial(conv_kernel, n), in_specs=[VM] * (n + 1)...]
    all_gather x2 -> x0, waiting for transfers between devices: 114 us -> none  [gather_channels(): return lax.all_gather(values, 'task', axis=1, tiled=True)]
    reduce_sum x31 -> x1, other arithmetic: 73.1 us -> 0.63 us  [on_device(): image_total = jnp.sum(image_counts).astype(f32)]
    ppermute x0 -> x12, waiting for transfers between devices: none -> 63.5 us  [swap(): return lax.ppermute(values, axis, [(i, i ^ by) for i in range(n)])]
    slice x2 -> x4, local copies, waits for them, and re-layouts: 42.2 us -> 1.83 us  [the longest x2 1.82 us: back_weights(): blocks = [w[:, :, i * width:(i + 1) * width] for i in range(n_parts)]]
  transfers between devices with their start and end apart: 6 -> 17, of which waited for: 6 -> 9; matrix products, arithmetic and copies ran while one was open for 5% -> 14% of each run, Pallas kernels for 0% -> 9%
where the time goes in v1:
time: 551 us; the launch traced here: 542 us
  waiting for transfers between devices  208 us (38%)
  Pallas kernels  118 us (21%)
  local copies, waits for them, and re-layouts  89.6 us (16%)
  blocking collectives  48.9 us (9%)
  other arithmetic  36.8 us (7%)
  starting transfers between devices  24.2 us (4%)
  between operations  16.3 us (3%)
    psum x1, waiting for transfers between devices, settle(): total = lax.psum(keep + swap(send, 'task', n_parts).astype(f32), 'batch')  123 us
    ppermute x12, waiting for transfers between devices, swap(): return lax.ppermute(values, axis, [(i, i ^ by) for i in range(n)])  63.5 us
    all_gather x1, blocking collectives, on_device(): gathered = lax.all_gather(mine, 'task', axis=0)  48.9 us
    pallas_call x2, Pallas kernels, conv_stats(): pl.pallas_call(functools.partial(conv_kernel, n), in_specs=[VM] * (n + 1)...  32.1 us
    pallas_call x2, Pallas kernels, weight_grad(): pl.pallas_call(functools.partial(weight_kernel, n), in_specs=[SM] + [VM]...  29 us
    unnamed x69, local copies, waits for them, and re-layouts  29 us
    all_to_all x4, waiting for transfers between devices, exchange(): lax.all_to_all(flat_rows, ('batch', 'task'), 0, 0, tiled=True)  21.3 us
    reshape x4, local copies, waits for them, and re-layouts, part_weights(): full = full.reshape(9, width, slots, n_parts, cs).swapaxes(2, 3)  18.9 us
  transfers between devices with their start and end apart: 17, of which 9 were waited for; matrix products, arithmetic and copies ran while one was open for 14% of the time, Pallas kernels for 9%

profile of v1, /device:TPU:0, one launch (start us, length us, event | category | flops | bytes accessed | tf_op | source)
XLA Modules:
  0.0 541.9 jit_solution(15308828440549217433)
XLA Ops:
  16.7 22.1 %collective-permute-done = bf16[4096,128]{1,0:T(8,128)(2,1)} collective-permute-done((bf16[4096,128]{1,0:T(8,128)(2,1)}, bf16[4096,128]{1,0:T(8,128)(2,1)}, u32[]{:S(2)}, u32[]{:S(2)}) %collective-permute-start) | collective-permute-done | bytes 1048608 | tf_op jit(solution)/shard_map/ppermute | solution.py:539
  41.1 48.9 %all-gather = f32[64,512]{1,0:T(8,128)S(1)} all-gather(f32[16,512]{1,0:T(8,128)S(1)} %select_maximum_fusion), channel_id=2, replica_groups=mesh['batch'=8,'task'=4] {'task'}, dimensions={0}, use_global_device_ids=true | all-gather | bytes 163840 | tf_op jit(solution)/shard_map/all_gather | solution.py:615
  95.2 6.0 %reshape.199 = bf16[9,256,2,2,128]{4,3,2,1,0:T(2,128)(2,1)} reshape(bf16[9,256,512]{2,1,0:T(8,128)(2,1)} %pad_maximum_fusion.1) | data formatting | bytes 4718592 | tf_op jit(solution)/shard_map/reshape | solution.py:593
  104.6 3.8 broadcast_select_fusion.1
  108.5 6.4 %reshape_reshape.12.refs_2_ = bf16[9,256,512]{2,1,0:T(8,128)(2,1)} reshape(bf16[9,256,2,2,128]{4,3,2,1,0:T(2,128)(2,1)} %broadcast_select_fusion.1) | data formatting | bytes 4718592 | tf_op jit(solution)/shard_map/reshape;reshape | solution.py:594
  116.6 15.7 %conv_stats.2 = (f32[4096,256]{1,0:T(8,128)S(1)}, f32[32,8,128]{2,1,0:T(8,128)}) custom-call(bf16[4096,256]{1,0:T(8,128)(2,1)S(1)} %pad_maximum_fusion.5.refs_0_.x.refs_2_, bf16[4096,256]{1,0:T(8,128)(2,1)} %collective-permute-done.1.refs_1_.refs_3_, bf16[9,256,512]{2,1,0:T(8,128)(2,1)S(1)} %copy-done.6), custom_call_target="tpu_custom_call" | custom-call | flops 9663676416 | bytes 16777216 | tf_op jit(solution)/shard_map/conv_stats/pallas_call | solution.py:126
  134.3 6.5 %all-to-all-start = ((f32[32,8,128]{2,1,0:T(8,128)}), f32[32,8,128]{2,1,0:T(8,128)S(1)}, u32[]{:S(2)}, u32[]{:S(2)}) async-start(f32[32,8,128]{2,1,0:T(8,128)} %get-tuple-element.39), calls=%async_computation | async-start | bytes 262144 | tf_op jit(solution)/shard_map/all_to_all | solution.py:629
  140.9 8.1 %all-to-all-done.got = f32[32,8,128]{2,1,0:T(8,128)S(1)} async-done(((f32[32,8,128]{2,1,0:T(8,128)}), f32[32,8,128]{2,1,0:T(8,128)S(1)}, u32[]{:S(2)}, u32[]{:S(2)}) %all-to-all-start) | async-done | bytes 131104 | tf_op jit(solution)/shard_map/all_to_all | solution.py:629
  151.3 4.2 activate.1
  159.0 6.0 %reshape.204 = bf16[9,256,2,2,128]{4,3,2,1,0:T(2,128)(2,1)} reshape(bf16[9,256,512]{2,1,0:T(8,128)(2,1)} %pad_maximum_fusion.2) | data formatting | bytes 4718592 | tf_op jit(solution)/shard_map/reshape | solution.py:593
  168.4 3.8 broadcast_select_fusion
  172.3 6.4 %reshape_reshape.13.refs_2_ = bf16[9,256,512]{2,1,0:T(8,128)(2,1)} reshape(bf16[9,256,2,2,128]{4,3,2,1,0:T(2,128)(2,1)} %broadcast_select_fusion) | data formatting | bytes 4718592 | tf_op jit(solution)/shard_map/reshape;reshape | solution.py:594
  180.4 16.4 %conv_stats.3 = (f32[4096,256]{1,0:T(8,128)S(1)}, f32[32,8,128]{2,1,0:T(8,128)}) custom-call(bf16[4096,256]{1,0:T(8,128)(2,1)} %get-tuple-element.40.refs_0_.refs_2_, bf16[4096,256]{1,0:T(8,128)(2,1)} %collective-permute-done.3.refs_1_.refs_3_, bf16[9,256,512]{2,1,0:T(8,128)(2,1)S(1)} %copy-done.8), custom_call_target="tpu_custom_call" | custom-call | flops 9663676416 | bytes 16777216 | tf_op jit(solution)/shard_map/conv_stats/pallas_call | solution.py:126
  202.8 6.7 %all-to-all-done.1.got = f32[32,8,128]{2,1,0:T(8,128)S(1)} async-done(((f32[32,8,128]{2,1,0:T(8,128)}), f32[32,8,128]{2,1,0:T(8,128)S(1)}, u32[]{:S(2)}, u32[]{:S(2)}) %all-to-all-start.1) | async-done | bytes 131104 | tf_op jit(solution)/shard_map/all_to_all | solution.py:629
  211.7 5.3 pool.1
  221.5 6.5 %all-to-all-done.2.got = f32[32,8,128]{2,1,0:T(8,128)S(1)} async-done(((f32[32,8,128]{2,1,0:T(8,128)}), f32[32,8,128]{2,1,0:T(8,128)S(1)}, u32[]{:S(2)}, u32[]{:S(2)}) %all-to-all-start.2) | async-done | bytes 131104 | tf_op jit(solution)/shard_map/all_to_all | solution.py:629
  227.9 5.7 %head.1 = (f32[8,128]{1,0:T(8,128)S(1)}, f32[1,40]{1,0:T(1,128)}, f32[1,40]{1,0:T(1,128)}, f32[40,512]{1,0:T(8,128)S(1)}, f32[1,40]{1,0:T(1,128)S(1)}, /*index=5*/f32[2,256]{1,0:T(2,128)S(1)}) custom-call(s32[4]{0:T(128)S(1)} %pad_add_fusion.meta.refs_0_, f32[32,8,128]{2,1,0:T(8,128)S(1)} %all-to-all-done.2.got, f32[40,512]{1,0:T(8,128)S(1)} %reshape.206.ht, ...), custom_call_target="tpu_custom_call" | custom-call | flops 1048576 | bytes 1048576 | tf_op jit(solution)/shard_map/head/pallas_call | solution.py:310
  235.9 3.8 grad_two.1
  241.9 3.7 collective-permute-done.6
  245.8 18.0 %back_two.1 = (f32[4096,256]{1,0:T(8,128)}, f32[32,8,128]{2,1,0:T(8,128)}) custom-call(s32[4]{0:T(128)S(1)} %pad_add_fusion.meta.refs_0_, bf16[4096,256]{1,0:T(8,128)(2,1)S(1)} %get-tuple-element.47.refs_1_, bf16[4096,256]{1,0:T(8,128)(2,1)S(1)} %collective-permute-done.5.refs_2_, bf16[9,512,256]{2,1,0:T(8,128)(2,1)S(1)} %pad_maximum_fusion.3.refs_3_, ...), custom_call_target="tpu_custom_call" | custom-call | flops 9663676416 | bytes 16777216 | tf_op jit(solution)/shard_map/back_two/pallas_call | solution.py:448
  268.0 14.3 %weight_grad.3 = (f32[9,128,512]{2,1,0:T(8,128)S(1)}, bf16[9,128,512]{2,1,0:T(8,128)(2,1)}) custom-call(s32[4]{0:T(128)S(1)} %pad_add_fusion.meta.refs_0_, bf16[4096,256]{1,0:T(8,128)(2,1)S(1)} %copy-done.19, bf16[4096,256]{1,0:T(8,128)(2,1)} %get-tuple-element.40.refs_0_.refs_2_, bf16[4096,256]{1,0:T(8,128)(2,1)} %collective-permute-done.3.refs_1_.refs_3_), custom_call_target="tpu_custom_call" | custom-call | flops 9663676416 | bytes 16777216 | tf_op jit(solution)/shard_map/weight_grad/pallas_call | solution.py:525
  289.9 4.3 grad_one.1
  294.2 14.7 %weight_grad.2 = (f32[9,128,512]{2,1,0:T(8,128)S(1)}, bf16[9,128,512]{2,1,0:T(8,128)(2,1)}) custom-call(s32[4]{0:T(128)S(1)} %pad_add_fusion.meta.refs_0_, bf16[4096,256]{1,0:T(8,128)(2,1)} %get-tuple-element.51.refs_1_, bf16[4096,256]{1,0:T(8,128)(2,1)S(1)} %pad_maximum_fusion.5.refs_0_.x.refs_2_, bf16[4096,256]{1,0:T(8,128)(2,1)} %collective-permute-done.1.refs_1_.refs_3_), custom_call_target="tpu_custom_call" | custom-call | flops 9663676416 | bytes 16777216 | tf_op jit(solution)/shard_map/weight_grad/pallas_call | solution.py:525
  315.6 4.1 reshape_reshape.15
  319.7 17.8 %collective-permute-done.10 = bf16[9,128,512]{2,1,0:T(8,128)(2,1)} collective-permute-done((bf16[9,128,512]{2,1,0:T(8,128)(2,1)}, bf16[9,128,512]{2,1,0:T(8,128)(2,1)}, u32[]{:S(2)}, u32[]{:S(2)}) %collective-permute-start.10) | collective-permute-done | bytes 1179680 | tf_op jit(solution)/shard_map/ppermute | solution.py:539
  340.6 3.9 reshape_reshape.14
  348.4 15.6 %back_one.1 = (f32[128,4096]{1,0:T(8,128)S(1)}, bf16[128,4096]{1,0:T(8,128)(2,1)S(1)}) custom-call(s32[4]{0:T(128)S(1)} %pad_add_fusion.meta.refs_0_, bf16[4096,256]{1,0:T(8,128)(2,1)} %get-tuple-element.51.refs_1_, bf16[4096,256]{1,0:T(8,128)(2,1)} %collective-permute-done.7.refs_2_, bf16[9,512,256]{2,1,0:T(8,128)(2,1)S(1)} %pad_maximum_fusion.4.refs_3_, ...), custom_call_target="tpu_custom_call" | custom-call | flops 9663676416 | bytes 16777216 | tf_op jit(solution)/shard_map/back_one/pallas_call | solution.py:487
  369.9 18.8 %collective-permute-done.9 = bf16[128,4096]{1,0:T(8,128)(2,1)} collective-permute-done((bf16[128,4096]{1,0:T(8,128)(2,1)S(1)}, bf16[128,4096]{1,0:T(8,128)(2,1)}, u32[]{:S(2)}, u32[]{:S(2)}) %collective-permute-start.9) | collective-permute-done | bytes 1048608 | tf_op jit(solution)/shard_map/ppermute | solution.py:539
  392.7 123.2 %all-reduce.5.cloned.1.call-done = (f32[9,128,1,2,1,2,128]{6,5,3,1,0,4,2:T(2,128)}, f32[9,128,1,2,1,2,128]{6,5,3,1,0,4,2:T(2,128)}) async-done(((f32[9,128,1,2,1,2,128]{6,5,3,1,0,4,2:T(2,128)}, f32[9,128,1,2,1,2,128]{6,5,3,1,0,4,2:T(2,128)}), (f32[9,128,1,2,1,2,128]{6,5,3,1,0,4,2:T(2,128)}, f32[9,128,1,2,1,2,128]{6,5,3,1,0,4,2:T(2,128)})) %all-reduce.5.cloned.1.call-update) | async-done | bytes 4718608 | tf_op jit(solution)/shard_map/psum | solution.py:649
  516.0 3.7 fusion
  523.7 4.1 reshape.216
  530.5 4.1 reshape.212
  (154 shorter events, 92.6 us)
Async XLA Ops:
  10.3 4.2 copy-start.22
  10.4 6.1 %copy-start.26 = (f32[128]{0:T(128)S(1)}, f32[128]{0:T(128)}, u32[]{:S(2)}) copy-start(f32[128]{0:T(128)} %param.14) | copy-start | bytes 1540
  10.4 6.1 %copy-start.27 = (f32[128]{0:T(128)S(1)}, f32[128]{0:T(128)}, u32[]{:S(2)}) copy-start(f32[128]{0:T(128)} %param.15) | copy-start | bytes 1540
  10.4 6.2 %copy-start.28 = (f32[128]{0:T(128)S(1)}, f32[128]{0:T(128)}, u32[]{:S(2)}) copy-start(f32[128]{0:T(128)} %param.17) | copy-start | bytes 1540
  10.4 6.2 %copy-start.29 = (f32[128]{0:T(128)S(1)}, f32[128]{0:T(128)}, u32[]{:S(2)}) copy-start(f32[128]{0:T(128)} %param.18) | copy-start | bytes 1540
  10.4 6.2 %copy-start.25 = (s32[8]{0:T(128)S(1)}, s32[8]{0:T(128)}, u32[]{:S(2)}) copy-start(s32[8]{0:T(128)} %param.22) | copy-start | bytes 100
  11.5 27.3 %collective-permute-start = (bf16[4096,128]{1,0:T(8,128)(2,1)}, bf16[4096,128]{1,0:T(8,128)(2,1)}, u32[]{:S(2)}, u32[]{:S(2)}) collective-permute-start(bf16[4096,128]{1,0:T(8,128)(2,1)} %select_bitcast_fusion), channel_id=1, source_target_pairs={{0,2},{1,3},{2,0},{3,1},{4,6},{5,7},{6,4},{7,5},{8,10},{9,11},{10,... | collective-permute-start | bytes 3145736 | tf_op jit(solution)/shard_map/ppermute | solution.py:539
  14.5 75.5 %collective-permute-start.2 = (bf16[9,128,512]{2,1,0:T(8,128)(2,1)}, bf16[9,128,512]{2,1,0:T(8,128)(2,1)}, u32[]{:S(2)}, u32[]{:S(2)}) collective-permute-start(bf16[9,128,512]{2,1,0:T(8,128)(2,1)} %param.13), channel_id=1, source_target_pairs={{0,2},{1,3},{2,0},{3,1},{4,6},{5,7},{6,4},{7,5},{8,10},{9,11},{10,... | collective-permute-start | bytes 3538952 | tf_op jit(solution)/shard_map/ppermute | solution.py:539
  14.5 75.4 %collective-permute-start.4 = (bf16[9,128,512]{2,1,0:T(8,128)(2,1)S(1)}, bf16[9,128,512]{2,1,0:T(8,128)(2,1)}, u32[]{:S(2)}, u32[]{:S(2)}) collective-permute-start(bf16[9,128,512]{2,1,0:T(8,128)(2,1)S(1)} %copy-done.22), channel_id=1, source_target_pairs={{0,2},{1,3},{2,0},{3,1},{4,6},{5,7},{6,4},{7,5},{8,10},{9,11},{10,... | collective-permute-start | bytes 3538952 | tf_op jit(solution)/shard_map/ppermute | solution.py:539
  40.4 74.5 %collective-permute-start.1 = (bf16[4096,256]{1,0:T(8,128)(2,1)S(1)}, bf16[4096,256]{1,0:T(8,128)(2,1)}, u32[]{:S(2)}, u32[]{:S(2)}) collective-permute-start(bf16[4096,256]{1,0:T(8,128)(2,1)S(1)} %pad_maximum_fusion.5.refs_0_.x.refs_2_), channel_id=1, source_target_pairs={{0,1},{1,0},{2,3},{3,2},{4,5},{5,4},{6,7},{7,6},{8,9},{9,8},{10,11... | collective-permute-start | bytes 6291464 | tf_op jit(solution)/shard_map/ppermute | solution.py:539
  134.3 14.8 %all-to-all-start = ((f32[32,8,128]{2,1,0:T(8,128)}), f32[32,8,128]{2,1,0:T(8,128)S(1)}, u32[]{:S(2)}, u32[]{:S(2)}) async-start(f32[32,8,128]{2,1,0:T(8,128)} %get-tuple-element.39), calls=%async_computation | async-start | bytes 262144 | tf_op jit(solution)/shard_map/all_to_all | solution.py:629
  155.6 23.1 %collective-permute-start.3 = (bf16[4096,256]{1,0:T(8,128)(2,1)}, bf16[4096,256]{1,0:T(8,128)(2,1)}, u32[]{:S(2)}, u32[]{:S(2)}) collective-permute-start(bf16[4096,256]{1,0:T(8,128)(2,1)} %get-tuple-element.40.refs_0_.refs_2_), channel_id=1, source_target_pairs={{0,1},{1,0},{2,3},{3,2},{4,5},{5,4},{6,7},{7,6},{8,9},{9,8},{10,11... | collective-permute-start | bytes 6291464 | tf_op jit(solution)/shard_map/ppermute | solution.py:539
  180.4 22.2 %copy-start.24 = (s32[2,10]{1,0:T(2,128)S(1)}, s32[2,10]{1,0:T(2,128)}, u32[]{:S(2)}) copy-start(s32[2,10]{1,0:T(2,128)} %param.21) | copy-start | bytes 244
  198.7 10.8 %all-to-all-start.1 = ((f32[32,8,128]{2,1,0:T(8,128)}), f32[32,8,128]{2,1,0:T(8,128)S(1)}, u32[]{:S(2)}, u32[]{:S(2)}) async-start(f32[32,8,128]{2,1,0:T(8,128)} %get-tuple-element.42), calls=%async_computation.1 | async-start | bytes 262144 | tf_op jit(solution)/shard_map/all_to_all | solution.py:629
  211.7 9.4 %copy-start.15 = (f32[40]{0:T(128)S(1)}, f32[40]{0:T(128)}, u32[]{:S(2)}) copy-start(f32[40]{0:T(128)} %param.23) | copy-start | bytes 484
  217.0 11.0 %all-to-all-start.2 = ((f32[32,8,128]{2,1,0:T(8,128)}), f32[32,8,128]{2,1,0:T(8,128)S(1)}, u32[]{:S(2)}, u32[]{:S(2)}) async-start(f32[32,8,128]{2,1,0:T(8,128)} %get-tuple-element.43), calls=%async_computation.2 | async-start | bytes 262144 | tf_op jit(solution)/shard_map/all_to_all | solution.py:629
  235.9 4.1 copy-start.9
  239.7 6.1 %copy-start.18 = (bf16[4096,256]{1,0:T(8,128)(2,1)}, bf16[4096,256]{1,0:T(8,128)(2,1)S(1)}, u32[]{:S(2)}) copy-start(bf16[4096,256]{1,0:T(8,128)(2,1)S(1)} %get-tuple-element.47.refs_1_) | copy-start | bytes 6291460
  239.7 6.1 %collective-permute-start.5 = (bf16[4096,256]{1,0:T(8,128)(2,1)S(1)}, bf16[4096,256]{1,0:T(8,128)(2,1)S(1)}, u32[]{:S(2)}, u32[]{:S(2)}) collective-permute-start(bf16[4096,256]{1,0:T(8,128)(2,1)S(1)} %get-tuple-element.47.refs_1_), channel_id=1, source_target_pairs={{0,1},{1,0},{2,3},{3,2},{4,5},{5,4},{6,7},{7,6},{8,9},{9,8},{10,11... | collective-permute-start | bytes 6291464 | tf_op jit(solution)/shard_map/ppermute | solution.py:539
  241.7 3.9 collective-permute-start.6
  263.8 21.7 %all-to-all-start.3 = ((f32[32,8,128]{2,1,0:T(8,128)}), f32[32,8,128]{2,1,0:T(8,128)S(1)}, u32[]{:S(2)}, u32[]{:S(2)}) async-start(f32[32,8,128]{2,1,0:T(8,128)} %get-tuple-element.50), calls=%async_computation.3 | async-start | bytes 262144 | tf_op jit(solution)/shard_map/all_to_all | solution.py:629
  266.4 249.6 %all-reduce.5.cloned.1.call-start = ((), (), s32[]{:S(2)}) async-start(), calls=%async_computation.4 | async-start | bytes 9437184 | tf_op jit(solution)/shard_map/psum | solution.py:649
  283.9 28.7 %collective-permute-start.11 = (bf16[9,128,512]{2,1,0:T(8,128)(2,1)}, bf16[9,128,512]{2,1,0:T(8,128)(2,1)}, u32[]{:S(2)}, u32[]{:S(2)}) collective-permute-start(bf16[9,128,512]{2,1,0:T(8,128)(2,1)} %get-tuple-element.59), channel_id=1, source_target_pairs={{0,2},{1,3},{2,0},{3,1},{4,6},{5,7},{6,4},{7,5},{8,10},{9,11},{10,... | collective-permute-start | bytes 3538952 | tf_op jit(solution)/shard_map/ppermute | solution.py:539
  294.2 15.1 %copy-start.7 = (bf16[9,256,512]{2,1,0:T(8,128)(2,1)S(1)}, bf16[9,256,512]{2,1,0:T(8,128)(2,1)}, u32[]{:S(2)}) copy-start(bf16[9,256,512]{2,1,0:T(8,128)(2,1)} %reshape_reshape.12.refs_2_) | copy-start | bytes 7077892
  308.9 3.7 copy-start.12
  308.9 28.6 %collective-permute-start.10 = (bf16[9,128,512]{2,1,0:T(8,128)(2,1)}, bf16[9,128,512]{2,1,0:T(8,128)(2,1)}, u32[]{:S(2)}, u32[]{:S(2)}) collective-permute-start(bf16[9,128,512]{2,1,0:T(8,128)(2,1)} %get-tuple-element.56), channel_id=1, source_target_pairs={{0,2},{1,3},{2,0},{3,1},{4,6},{5,7},{6,4},{7,5},{8,10},{9,11},{10,... | collective-permute-start | bytes 3538952 | tf_op jit(solution)/shard_map/ppermute | solution.py:539
  309.3 38.1 %collective-permute-start.7 = (bf16[4096,256]{1,0:T(8,128)(2,1)}, bf16[4096,256]{1,0:T(8,128)(2,1)}, u32[]{:S(2)}, u32[]{:S(2)}) collective-permute-start(bf16[4096,256]{1,0:T(8,128)(2,1)} %get-tuple-element.51.refs_1_), channel_id=1, source_target_pairs={{0,1},{1,0},{2,3},{3,2},{4,5},{5,4},{6,7},{7,6},{8,9},{9,8},{10,11... | collective-permute-start | bytes 6291464 | tf_op jit(solution)/shard_map/ppermute | solution.py:539
  311.3 33.3 %collective-permute-start.8 = (bf16[9,256,256]{2,1,0:T(8,128)(2,1)}, bf16[9,256,256]{2,1,0:T(8,128)(2,1)}, u32[]{:S(2)}, u32[]{:S(2)}) collective-permute-start(bf16[9,256,256]{2,1,0:T(8,128)(2,1)} %get-tuple-element.71), channel_id=1, source_target_pairs={{0,1},{1,0},{2,3},{3,2},{4,5},{5,4},{6,7},{7,6},{8,9},{9,8},{10,11... | collective-permute-start | bytes 3538952 | tf_op jit(solution)/shard_map/ppermute | solution.py:539
  315.6 21.8 %copy-start.14 = (f32[9,128,512]{2,1,0:T(8,128)S(1)}, f32[9,128,512]{2,1,0:T(8,128)}, u32[]{:S(2)}) copy-start(f32[9,128,512]{2,1,0:T(8,128)} %copy-done.13) | copy-start | bytes 7077892
  345.8 2.5 copy-start.17
  364.0 24.7 %collective-permute-start.9 = (bf16[128,4096]{1,0:T(8,128)(2,1)S(1)}, bf16[128,4096]{1,0:T(8,128)(2,1)}, u32[]{:S(2)}, u32[]{:S(2)}) collective-permute-start(bf16[128,4096]{1,0:T(8,128)(2,1)S(1)} %get-tuple-element.54), channel_id=1, source_target_pairs={{0,2},{1,3},{2,0},{3,1},{4,6},{5,7},{6,4},{7,5},{8,10},{9,11},{10,... | collective-permute-start | bytes 3145736 | tf_op jit(solution)/shard_map/ppermute | solution.py:539
  516.0 3.7 copy-start.21
  (16 other events, 28.5 us)
Sparse Core Ops, SparseCore 0:
  344.7 171.2 all-reduce.4

commit v2 on v1

--- a/solution.py
+++ b/solution.py
@@ -44,8 +44,7 @@
     return slice(h * LANES, (h + 1) * LANES)
 
 
-def fill_shifted(dst, src, col0, rows):
-    width = src.shape[1]
+def fill_shifted(dst, load, col0, width, rows):
     cols = slice(col0, col0 + width)
     block = 512
     zero = jnp.zeros((3, SIDE, width), bf16)
@@ -54,7 +53,7 @@
 
     def step(i, carry):
         at = pl.multiple_of(i * block, block)
-        low = src[pl.ds(at, block), :]
+        low = load(at, block)
         to = pl.ds(pl.multiple_of(at + SIDE, SIDE), block)
         dst[1, to, cols] = low
         value = low.astype(f32)
@@ -66,9 +65,46 @@
     lax.fori_loop(0, rows // block, step, 0)
 
 
-def send_rows(out, rows):
+def fill_part(dst, part, first, col0, rows):
+    if len(part) == 1:
+        v = part[0]
+        fill_shifted(dst, lambda at, n: v[pl.ds(at, n), :], col0, v.shape[1], rows)
+        return
+    own, other = part
+    width = own.shape[1]
+
+    def pick(one, two):
+        return lambda at, n: jnp.where(first, one[pl.ds(at, n), :], two[pl.ds(at, n), :])
+
+    fill_shifted(dst, pick(own, other), col0, width, rows)
+    fill_shifted(dst, pick(other, own), col0 + width, width, rows)
+
+
+def load_slice(ref, k, s, width):
+    if width % LANES == 0:
+        return ref[k, :, pl.ds(pl.multiple_of(s * width, LANES), width)]
+    per = LANES // width
+    both = ref[k, :, pl.ds(pl.multiple_of(s // per * LANES, LANES), LANES)]
+    out = both[:, 0:width]
+    for i in range(1, per):
+        out = jnp.where(s % per == i, both[:, i * width : (i + 1) * width], out)
+    return out
+
+
+def weight_rows(meta, cs):
+    g, x = meta[1], meta[4]
+    hs = cs // 2
+    return [
+        pl.ds(pl.multiple_of(g * cs, cs), cs),
+        pl.ds(pl.multiple_of((1 - g) * cs + x * hs, hs), hs),
+        pl.ds(pl.multiple_of((1 - g) * cs + (1 - x) * hs, hs), hs),
+    ]
+
+
+def send_rows(out, rows, base=None):
     n = out.shape[0]
-    out[...] = jnp.zeros(out.shape, f32)
+    start = jnp.zeros((ROWS, LANES), f32) if base is None else base
+    out[...] = jnp.broadcast_to(start[None], out.shape)
     for at, value in rows:
         out[:, at : at + 1, :] = jnp.broadcast_to(value[None], (n, 1, LANES))
 
@@ -87,14 +123,28 @@
     return mean, lax.rsqrt(squares / (count * rows) + eps)
 
 
-def conv_kernel(n_parts, *refs):
-    xs, w, out, stats, scratch = refs[:n_parts], *refs[n_parts:]
+def conv_kernel(n_parts, per_part, meta, extra, *refs):
+    pieces, refs = refs[:3], refs[3:]
+    xs, (out, stats, scratch, w) = refs[: n_parts * per_part], refs[n_parts * per_part :]
     rows, width = out.shape
+    cs = width // 2
     chunk = 1024
+    r = meta[2]
     for i in range(n_parts):
-        fill_shifted(scratch, xs[i], i * width, rows)
-
-    def step(j, total):
+        fill_part(scratch, xs[i * per_part : (i + 1) * per_part], meta[1] == 0, i * width, rows)
+
+    def place(k, carry):
+        for piece, to in zip(pieces, weight_rows(meta, cs)):
+            for i in range(n_parts):
+                for s in range(2):
+                    lo = i * width + s * cs
+                    w[k, to, lo : lo + cs] = load_slice(piece, k, s * n_parts + (r ^ i), cs)
+        return carry
+
+    lax.fori_loop(0, 9, place, 0)
+
+    def step(j, carry):
+        mean, squares = carry
         at = pl.multiple_of(j * chunk, chunk)
         acc = None
         for k in range(9):
@@ -103,48 +153,66 @@
             term = lax.dot_general(lhs, w[k], (((1,), (1,)), ((), ())), preferred_element_type=f32)
             acc = term if acc is None else acc + term
         out[pl.ds(at, chunk), :] = acc
-        return total + jnp.sum(acc, axis=0, keepdims=True)
-
-    total = lax.fori_loop(0, rows // chunk, step, jnp.zeros((1, width), f32))
-    mean = total / rows
-
-    def spread(j, acc):
-        away = out[pl.ds(pl.multiple_of(j * chunk, chunk), chunk), :] - mean
-        return acc + jnp.sum(away * away, axis=0, keepdims=True)
-
-    squares = lax.fori_loop(0, rows // chunk, spread, jnp.zeros((1, width), f32))
+        here = jnp.sum(acc, axis=0, keepdims=True) / chunk
+        away = out[pl.ds(at, chunk), :] - here
+        spread = jnp.sum(away * away, axis=0, keepdims=True)
+        before = jnp.asarray(j, f32)
+        gap = here - mean
+        share = before / (before + 1.0)
+        return mean + gap / (before + 1.0), squares + spread + gap * gap * (share * chunk)
+
+    zero = jnp.zeros((1, width), f32)
+    mean, squares = lax.fori_loop(0, rows // chunk, step, (zero, zero))
     send_rows(
         stats,
         [(h, mean[:, half(h)]) for h in range(width // LANES)]
         + [(2 + h, squares[:, half(h)]) for h in range(width // LANES)],
+        extra[...],
     )
 
 
-def conv_stats(x_parts, w, n_devices):
-    rows, width = x_parts[0].shape
-    n = len(x_parts)
-    return pl.pallas_call(
-        functools.partial(conv_kernel, n),
-        in_specs=[VM] * (n + 1),
+def conv_stats(meta, extra, pieces, parts, n_devices):
+    cs = pieces[0].shape[1]
+    rows, width, channels = parts[0][0].shape[0], 2 * cs, pieces[0].shape[2]
+    n, per_part = len(parts), len(parts[0])
+    return pl.pallas_call(
+        functools.partial(conv_kernel, n, per_part),
+        in_specs=[SM] + [VM] * (4 + n * per_part),
         out_specs=(VM, VM),
         out_shape=(
             jax.ShapeDtypeStruct((rows, width), f32),
             jax.ShapeDtypeStruct((n_devices, ROWS, LANES), f32),
         ),
-        scratch_shapes=[pltpu.VMEM((3, rows + 2 * SIDE, n * width), bf16)],
-        compiler_params=params(40),
-        cost_estimate=cost(2 * 9 * rows * width * width * n, 16 << 20),
+        scratch_shapes=[
+            pltpu.VMEM((3, rows + 2 * SIDE, channels), bf16),
+            pltpu.VMEM((9, width, channels), bf16),
+        ],
+        compiler_params=params(60),
+        cost_estimate=cost(2 * 9 * rows * width * channels, 16 << 20),
         name="conv_stats",
-    )(*x_parts, w)
-
-
-def act_kernel(c, got, weight, vecs, out, coefs):
-    rows = loss_scale
-    for h in range(c.shape[1] // LANES):
-        mean, scale = norm_coefs(got, weight, h, rows)
-        coefs[h : h + 1, :] = mean
-        coefs[2 + h : 3 + h, :] = scale
-        normed = (c[:, half(h)] - mean) * scale * vecs[h : h + 1, :] + vecs[2 + h : 3 + h, :]
+    )(meta, extra, *pieces, *[v for part in parts for v in part])
+
+
+def act_kernel(n_parts, meta, c, got, weight, out, coefs):
+    halves = c.shape[1] // LANES
+    cs = c.shape[1] // 2
+
+    @pl.when(pl.program_id(0) == 0)
+    def _():
+        coefs[...] = jnp.zeros(coefs.shape, f32)
+        for h in range(halves):
+            mean, scale = norm_coefs(got, weight, h, loss_scale)
+            coefs[h : h + 1, :] = mean
+            coefs[2 + h : 3 + h, :] = scale
+        for v in range(4):
+            for g in range(2):
+                row = got[g * n_parts + meta[2], 4 + v : 5 + v, 0:cs]
+                lo = g * cs
+                coefs[4 + 2 * v + lo // LANES : 5 + 2 * v + lo // LANES, lo % LANES : lo % LANES + cs] = row
+
+    for h in range(halves):
+        normed = (c[:, half(h)] - coefs[h : h + 1, :]) * coefs[2 + h : 3 + h, :]
+        normed = normed * coefs[4 + h : 5 + h, :] + coefs[6 + h : 7 + h, :]
         out[:, half(h)] = (normed * sigmoid(normed)).astype(bf16)
 
 
@@ -156,38 +224,92 @@
     return pl.BlockSpec(shape, lambda i: (0,) * len(shape))
 
 
-def activate(c, got, weight, vecs):
+def activate(meta, c, got, weight, n_parts):
     rows, width = c.shape
-    block = 512
-    return pl.pallas_call(
-        act_kernel,
+    block = 1024
+    return pl.pallas_call(
+        functools.partial(act_kernel, n_parts),
         grid=(rows // block,),
-        in_specs=[blocked(block, width), whole(got.shape), whole(weight.shape), whole(vecs.shape)],
-        out_specs=(blocked(block, width), whole((ROWS, LANES))),
+        in_specs=[SM, blocked(block, width), whole(got.shape), whole(weight.shape)],
+        out_specs=(blocked(block, width), whole((2 * ROWS, LANES))),
         out_shape=(
             jax.ShapeDtypeStruct((rows, width), bf16),
-            jax.ShapeDtypeStruct((ROWS, LANES), f32),
+            jax.ShapeDtypeStruct((2 * ROWS, LANES), f32),
         ),
-        compiler_params=params(16),
+        compiler_params=params(60),
         cost_estimate=cost(20 * rows * width, 6 * rows * width),
         name="activate",
-    )(c, got, weight, vecs)
-
-
-def pool_kernel(meta, c, x, got, weight, vecs, labels, out, coefs, sums):
+    )(meta, c, got, weight)
+
+
+def turn_kernel(meta, images, own, other):
+    g = meta[1]
+    own[...] = images[g].T
+    other[...] = images[1 - g].T
+
+
+def turn(meta, images):
+    slots, cs, rows = images.shape
+    block = 1024
+    return pl.pallas_call(
+        turn_kernel,
+        grid=(rows // block,),
+        in_specs=[SM, pl.BlockSpec((slots, cs, block), lambda i: (0, 0, i))],
+        out_specs=(blocked(block, cs), blocked(block, cs)),
+        out_shape=(jax.ShapeDtypeStruct((rows, cs), bf16),) * 2,
+        compiler_params=params(60),
+        cost_estimate=cost(1 << 20, 8 * rows * cs),
+        name="turn",
+    )(meta, images)
+
+
+def join_kernel(meta, keep, got, out):
+    g = meta[1]
+    out[g] = keep[...]
+    out[1 - g] = got[...].astype(f32)
+
+
+def join(meta, keep, got):
+    cs, rows = keep.shape
+    block = 1024
+    piece = pl.BlockSpec((cs, block), lambda i: (0, i))
+    return pl.pallas_call(
+        join_kernel,
+        grid=(rows // block,),
+        in_specs=[SM, piece, piece],
+        out_specs=pl.BlockSpec((2, cs, block), lambda i: (0, 0, i)),
+        out_shape=jax.ShapeDtypeStruct((2, cs, rows), f32),
+        compiler_params=params(60),
+        cost_estimate=cost(1 << 20, 14 * rows * cs),
+        name="join",
+    )(meta, keep, got)
+
+
+def picked(first, own, other, h, cs):
+    if cs == LANES:
+        return jnp.where(first, *((own[...], other[...]) if h == 0 else (other[...], own[...])))
+    one, two = own[...], other[...]
+    return jnp.concatenate([jnp.where(first, one, two), jnp.where(first, two, one)], axis=1)
+
+
+def pool_kernel(meta, c, own, other, got, weight, coefs1, labels, out, coefs, sums):
     step, last = pl.program_id(0), pl.num_programs(0) - 1
     halves = c.shape[1] // LANES
+    first = meta[1] == 0
 
     @pl.when(step == 0)
     def _():
         sums[...] = jnp.zeros_like(sums)
+        coefs[...] = jnp.zeros(coefs.shape, f32)
+        for h in range(halves):
+            mean, scale = norm_coefs(got, weight, h, loss_scale)
+            coefs[h : h + 1, :] = mean
+            coefs[2 + h : 3 + h, :] = scale
 
     for h in range(halves):
-        mean, scale = norm_coefs(got, weight, h, loss_scale)
-        coefs[h : h + 1, :] = mean
-        coefs[2 + h : 3 + h, :] = scale
-        hat = (c[:, half(h)] - mean) * scale
-        v = hat * vecs[4 + h : 5 + h, :] + vecs[6 + h : 7 + h, :] + x[:, half(h)].astype(f32)
+        hat = (c[:, half(h)] - coefs[h : h + 1, :]) * coefs[2 + h : 3 + h, :]
+        x = picked(first, own, other, h, c.shape[1] // 2).astype(f32)
+        v = hat * coefs1[8 + h : 9 + h, :] + coefs1[10 + h : 11 + h, :] + x
         s = sigmoid(v)
         slope = s * (1.0 + v * (1.0 - s))
         sums[h : h + 1, :] += jnp.sum(v * s, axis=0, keepdims=True)
@@ -207,19 +329,20 @@
         send_rows(out, rows)
 
 
-def pool(meta, c, x, got, weight, vecs, labels):
+def pool(meta, c, own, other, got, weight, coefs1, labels):
     rows, width = c.shape
-    block = 512
+    block = 1024
     return pl.pallas_call(
         pool_kernel,
         grid=(rows // block,),
         in_specs=[
             SM,
             blocked(block, width),
-            blocked(block, width),
+            blocked(block, width // 2),
+            blocked(block, width // 2),
             whole(got.shape),
             whole(weight.shape),
-            whole(vecs.shape),
+            whole(coefs1.shape),
             whole(labels.shape),
         ],
         out_specs=(whole(got.shape), whole((ROWS, LANES))),
@@ -228,10 +351,10 @@
             jax.ShapeDtypeStruct((ROWS, LANES), f32),
         ),
         scratch_shapes=[pltpu.VMEM((ROWS, LANES), f32)],
-        compiler_params=params(16),
+        compiler_params=params(60),
         cost_estimate=cost(30 * rows * width, 6 * rows * width),
         name="pool",
-    )(meta, c, x, got, weight, vecs, labels)
+    )(meta, c, own, other, got, weight, coefs1, labels)
 
 
 def head_kernel(n_parts, meta, got, ht, bias, valid, avg_row, avg_col, coefs, tw, an, hwg, hbg, pooled_own, pooled, slopes, shifts, labels, grads, mine_all, pooled_part):
@@ -321,37 +444,40 @@
             pltpu.VMEM((images, width), f32),
             pltpu.VMEM((images, width), f32),
         ],
-        compiler_params=params(16),
+        compiler_params=params(60),
         cost_estimate=cost(1 << 20, 1 << 20),
         name="head",
     )(meta, got, ht, bias, valid, avg_row, avg_col)
 
 
-def grad_two_kernel(meta, c, x, coefs, vecs, heads, pixels, low, summed):
+def grad_two_kernel(meta, c, own, other, coefs, coefs1, heads, pixels, low, summed):
     valid = meta[3].astype(f32)
+    first = meta[1] == 0
     for h in range(c.shape[1] // LANES):
         mean, scale = coefs[h : h + 1, :], coefs[2 + h : 3 + h, :]
-        gain = vecs[4 + h : 5 + h, :]
+        gain = coefs1[8 + h : 9 + h, :]
         hat = (c[:, half(h)] - mean) * scale
-        v = hat * gain + vecs[6 + h : 7 + h, :] + x[:, half(h)].astype(f32)
+        x = picked(first, own, other, h, c.shape[1] // 2).astype(f32)
+        v = hat * gain + coefs1[10 + h : 11 + h, :] + x
         dn = (valid * heads[4 + h : 5 + h, :]) * silu_slope(v)
         summed[:, half(h)] = dn
         away = (heads[2 + h : 3 + h, :] + hat * heads[h : h + 1, :]) / pixels[0]
         low[:, half(h)] = ((valid * gain * scale) * (dn - away)).astype(bf16)
 
 
-def grad_two(meta, c, x, coefs, vecs, heads, pixels):
+def grad_two(meta, c, own, other, coefs, coefs1, heads, pixels):
     rows, width = c.shape
-    block = 512
+    block = 1024
     return pl.pallas_call(
         grad_two_kernel,
         grid=(rows // block,),
         in_specs=[
             SM,
             blocked(block, width),
-            blocked(block, width),
+            blocked(block, width // 2),
+            blocked(block, width // 2),
             whole(coefs.shape),
-            whole(vecs.shape),
+            whole(coefs1.shape),
             whole(heads.shape),
             SM,
         ],
@@ -360,28 +486,33 @@
             jax.ShapeDtypeStruct((rows, width), bf16),
             jax.ShapeDtypeStruct((rows, width), f32),
         ),
-        compiler_params=params(16),
+        compiler_params=params(60),
         cost_estimate=cost(30 * rows * width, 12 * rows * width),
         name="grad_two",
-    )(meta, c, x, coefs, vecs, heads, pixels)
-
-
-def grad_one_kernel(meta, c, dn, got, weight, coefs, vecs, pixels, low, sums):
+    )(meta, c, own, other, coefs, coefs1, heads, pixels)
+
+
+def grad_one_kernel(meta, c, dn, got, weight, coefs, pixels, low, sums):
     valid = meta[3].astype(f32)
-    for h in range(c.shape[1] // LANES):
-        gain_grad = weighted(got, weight[...], h)
-        bias_grad = weighted(got, weight[...], 2 + h)
-        sums[h : h + 1, :] = gain_grad
-        sums[2 + h : 3 + h, :] = bias_grad
+    halves = c.shape[1] // LANES
+
+    @pl.when(pl.program_id(0) == 0)
+    def _():
+        sums[...] = jnp.zeros(sums.shape, f32)
+        for h in range(halves):
+            sums[h : h + 1, :] = weighted(got, weight[...], h)
+            sums[2 + h : 3 + h, :] = weighted(got, weight[...], 2 + h)
+
+    for h in range(halves):
         mean, scale = coefs[h : h + 1, :], coefs[2 + h : 3 + h, :]
         hat = (c[:, half(h)] - mean) * scale
-        away = (bias_grad + hat * gain_grad) / pixels[0]
-        low[:, half(h)] = ((valid * vecs[h : h + 1, :] * scale) * (dn[:, half(h)] - away)).astype(bf16)
-
-
-def grad_one(meta, c, dn, got, weight, coefs, vecs, pixels):
+        away = (sums[2 + h : 3 + h, :] + hat * sums[h : h + 1, :]) / pixels[0]
+        low[:, half(h)] = ((valid * coefs[4 + h : 5 + h, :] * scale) * (dn[:, half(h)] - away)).astype(bf16)
+
+
+def grad_one(meta, c, dn, got, weight, coefs, pixels):
     rows, width = c.shape
-    block = 512
+    block = 1024
     return pl.pallas_call(
         grad_one_kernel,
         grid=(rows // block,),
@@ -392,7 +523,6 @@
             whole(got.shape),
             whole(weight.shape),
             whole(coefs.shape),
-            whole(vecs.shape),
             SM,
         ],
         out_specs=(blocked(block, width), whole((ROWS, LANES))),
@@ -400,10 +530,28 @@
             jax.ShapeDtypeStruct((rows, width), bf16),
             jax.ShapeDtypeStruct((ROWS, LANES), f32),
         ),
-        compiler_params=params(16),
+        compiler_params=params(60),
         cost_estimate=cost(10 * rows * width, 10 * rows * width),
         name="grad_one",
-    )(meta, c, dn, got, weight, coefs, vecs, pixels)
+    )(meta, c, dn, got, weight, coefs, pixels)
+
+
+def back_setup(meta, n_parts, pieces, gs, w, scratch, rows, width):
+    cs = width // 2
+    r = meta[2]
+    for i in range(n_parts):
+        fill_part(scratch, [gs[i]], None, i * width, rows)
+
+    def place(k, carry):
+        for i in range(n_parts):
+            spots = weight_rows(meta, cs)
+            for piece, to in zip(pieces[3 * i : 3 * i + 3], spots):
+                to = pl.ds(pl.multiple_of(to.start + i * width, cs // 2), to.size)
+                for s in range(2):
+                    w[k, to, s * cs : (s + 1) * cs] = load_slice(piece, k, s * n_parts + r, cs)
+        return carry
+
+    lax.fori_loop(0, 9, place, 0)
 
 
 def back_products(scratch, w, at, chunk):
@@ -416,14 +564,13 @@
     return acc
 
 
-def back_two_kernel(n_parts, *refs):
-    meta, gs = refs[0], refs[1 : 1 + n_parts]
-    w, c, coefs, vecs, out, stats, scratch = refs[1 + n_parts :]
+def back_two_kernel(n_parts, meta, *refs):
+    pieces, gs, refs = refs[: 3 * n_parts], refs[3 * n_parts : 4 * n_parts], refs[4 * n_parts :]
+    c, coefs, out, stats, scratch, w = refs
     rows, width = out.shape
     halves = width // LANES
     chunk = 1024
-    for i in range(n_parts):
-        fill_shifted(scratch, gs[i], i * width, rows)
+    back_setup(meta, n_parts, pieces, gs, w, scratch, rows, width)
 
     def step(j, carry):
         at = pl.multiple_of(j * chunk, chunk)
@@ -431,7 +578,7 @@
         sums = []
         for h in range(halves):
             hat = (c[pl.ds(at, chunk), half(h)] - coefs[h : h + 1, :]) * coefs[2 + h : 3 + h, :]
-            dn = acc[:, half(h)] * silu_slope(hat * vecs[h : h + 1, :] + vecs[2 + h : 3 + h, :])
+            dn = acc[:, half(h)] * silu_slope(hat * coefs[4 + h : 5 + h, :] + coefs[6 + h : 7 + h, :])
             out[pl.ds(at, chunk), half(h)] = dn
             sums.append(carry[2 * h] + jnp.sum(dn * hat, axis=0, keepdims=True))
             sums.append(carry[2 * h + 1] + jnp.sum(dn, axis=0, keepdims=True))
@@ -442,33 +589,39 @@
     send_rows(stats, [(2 * i + h, sums[2 * h + i]) for h in range(halves) for i in range(2)])
 
 
-def back_two(meta, g_parts, w, c, coefs, vecs, n_devices):
+def back_scratch(rows, width, n):
+    return [
+        pltpu.VMEM((3, rows + 2 * SIDE, n * width), bf16),
+        pltpu.VMEM((9, n * width, width), bf16),
+    ]
+
+
+def back_two(meta, pieces, g_parts, c, coefs, n_devices):
     rows, width = c.shape
     n = len(g_parts)
     return pl.pallas_call(
         functools.partial(back_two_kernel, n),
-        in_specs=[SM] + [VM] * (n + 4),
+        in_specs=[SM] + [VM] * (4 * n + 2),
         out_specs=(VM, VM),
         out_shape=(
             jax.ShapeDtypeStruct((rows, width), f32),
             jax.ShapeDtypeStruct((n_devices, ROWS, LANES), f32),
         ),
-        scratch_shapes=[pltpu.VMEM((3, rows + 2 * SIDE, n * width), bf16)],
-        compiler_params=params(44),
+        scratch_shapes=back_scratch(rows, width, n),
+        compiler_params=params(60),
         cost_estimate=cost(2 * 9 * rows * width * width * n, 16 << 20),
         name="back_two",
-    )(meta, *g_parts, w, c, coefs, vecs)
-
-
-def back_one_kernel(n_parts, *refs):
-    meta, gs = refs[0], refs[1 : 1 + n_parts]
-    w, summed, keep, send, scratch = refs[1 + n_parts :]
+    )(meta, *pieces, *g_parts, c, coefs)
+
+
+def back_one_kernel(n_parts, meta, *refs):
+    pieces, gs, refs = refs[: 3 * n_parts], refs[3 * n_parts : 4 * n_parts], refs[4 * n_parts :]
+    summed, keep, send, scratch, w = refs
     rows, width = summed.shape
     cs = width // 2
     chunk = 1024
     first = meta[1] == 0
-    for i in range(n_parts):
-        fill_shifted(scratch, gs[i], i * width, rows)
+    back_setup(meta, n_parts, pieces, gs, w, scratch, rows, width)
 
     def step(j, carry):
         at = pl.multiple_of(j * chunk, chunk)
@@ -481,57 +634,64 @@
     lax.fori_loop(0, rows // chunk, step, 0)
 
 
-def back_one(meta, g_parts, w, summed):
+def back_one(meta, pieces, g_parts, summed):
     rows, width = summed.shape
     n = len(g_parts)
     return pl.pallas_call(
         functools.partial(back_one_kernel, n),
-        in_specs=[SM] + [VM] * (n + 2),
+        in_specs=[SM] + [VM] * (4 * n + 1),
         out_specs=(VM, VM),
         out_shape=(
             jax.ShapeDtypeStruct((width // 2, rows), f32),
             jax.ShapeDtypeStruct((width // 2, rows), bf16),
         ),
-        scratch_shapes=[pltpu.VMEM((3, rows + 2 * SIDE, n * width), bf16)],
-        compiler_params=params(40),
+        scratch_shapes=back_scratch(rows, width, n),
+        compiler_params=params(60),
         cost_estimate=cost(2 * 9 * rows * width * width * n, 16 << 20),
         name="back_one",
-    )(meta, *g_parts, w, summed)
-
-
-def weight_kernel(n_parts, *refs):
-    meta, g, xs = refs[0], refs[1], refs[2 : 2 + n_parts]
-    keep, send, scratch = refs[2 + n_parts :]
+    )(meta, *pieces, *g_parts, summed)
+
+
+def weight_kernel(n_parts, per_part, meta, g, *refs):
+    xs, (keep, send, scratch) = refs[: n_parts * per_part], refs[n_parts * per_part :]
     rows, width = g.shape
     cs = width // 2
     first = meta[1] == 0
-    fill_shifted(scratch, g, 0, rows)
+    fill_part(scratch, [g], None, 0, rows)
+    rights = []
+    for i in range(n_parts):
+        part = xs[i * per_part : (i + 1) * per_part]
+        if per_part == 1:
+            rights.append(part[0][...])
+        else:
+            own, other = part[0][...], part[1][...]
+            rights.append(jnp.concatenate([jnp.where(first, own, other), jnp.where(first, other, own)], axis=1))
     for k in range(9):
         dy, dx = k // 3 - 1, k % 3 - 1
         lo = SIDE * (1 - dy)
         lhs = scratch[1 - dx, lo : lo + rows, :]
         for i in range(n_parts):
-            term = lax.dot_general(lhs, xs[i][...], (((0,), (0,)), ((), ())), preferred_element_type=f32)
+            term = lax.dot_general(lhs, rights[i], (((0,), (0,)), ((), ())), preferred_element_type=f32)
             a, b = term[:cs], term[cs:]
             cols = slice(i * width, (i + 1) * width)
             keep[k, :, cols] = jnp.where(first, a, b)
             send[k, :, cols] = jnp.where(first, b, a).astype(bf16)
 
 
-def weight_grad(meta, g, x_parts):
+def weight_grad(meta, g, parts):
     rows, width = g.shape
-    n = len(x_parts)
+    n, per_part = len(parts), len(parts[0])
     shape = (9, width // 2, n * width)
     return pl.pallas_call(
-        functools.partial(weight_kernel, n),
-        in_specs=[SM] + [VM] * (n + 1),
+        functools.partial(weight_kernel, n, per_part),
+        in_specs=[SM] + [VM] * (n * per_part + 1),
         out_specs=(VM, VM),
         out_shape=(jax.ShapeDtypeStruct(shape, f32), jax.ShapeDtypeStruct(shape, bf16)),
         scratch_shapes=[pltpu.VMEM((3, rows + 2 * SIDE, width), bf16)],
-        compiler_params=params(32),
+        compiler_params=params(60),
         cost_estimate=cost(2 * 9 * rows * width * width * n, 16 << 20),
         name="weight_grad",
-    )(meta, g, *x_parts)
+    )(meta, g, *[v for part in parts for v in part])
 
 
 def swap(values, axis, by):
@@ -539,18 +699,38 @@
     return lax.ppermute(values, axis, [(i, i ^ by) for i in range(n)])
 
 
-def xor_order(values, axis, r, n):
+def xor_order(values, r):
     bit = 1
-    while bit < n:
-        shape = values.shape
-        split = values.reshape(shape[:axis] + (n // (2 * bit), 2, bit) + shape[axis + 1 :])
-        values = jnp.where((r & bit) != 0, jnp.flip(split, axis + 1), split).reshape(shape)
+    while bit < len(values):
+        flip = (r & bit) != 0
+        values = [jnp.where(flip, values[i ^ bit], v) for i, v in enumerate(values)]
         bit *= 2
     return values
 
 
-def ordered(first, own, other, axis):
-    return jnp.concatenate([jnp.where(first, own, other), jnp.where(first, other, own)], axis=axis)
+def gate(values, *others):
+    return lax.optimization_barrier((values, *others))[0]
+
+
+def scatter_stage(total, stage, kind, after=None):
+    stride, size = stage
+    k = (lax.axis_index("batch") // stride) % size
+    split = total.reshape(size, -1, total.shape[1])
+    total = lax.dynamic_index_in_dim(split, k, keepdims=False)
+    got = [
+        swap(lax.dynamic_index_in_dim(split, k ^ j, keepdims=False).astype(kind), "batch", stride * j)
+        for j in range(1, size)
+    ]
+    for v in got:
+        total = total + (v if after is None else gate(v, after)).astype(f32)
+    return total
+
+
+def gather_stage(out, stage):
+    stride, size = stage
+    k = (lax.axis_index("batch") // stride) % size
+    pieces = [out] + [swap(out, "batch", stride * j) for j in range(1, size)]
+    return jnp.concatenate(xor_order(pieces, k), axis=0)
 
 
 def on_device(
@@ -583,43 +763,40 @@
     image_total = jnp.sum(image_counts).astype(f32)
     pixel_total = (image_total * pixels).reshape(1)
     own_valid = (g < lax.dynamic_index_in_dim(image_counts, b, keepdims=False)).astype(jnp.int32)
-    meta = jnp.stack([b, g, r, own_valid]).astype(jnp.int32)
+    meta = jnp.stack([b, g, r, own_valid, b % 2]).astype(jnp.int32)
     same = (jnp.arange(n_parts) == r).astype(f32)
     weight = (valid_images[:, :, None] * same[None, None, :]).reshape(n_devices, 1)
     weight = jnp.broadcast_to(weight, (n_devices, LANES))
 
-    def part_weights(w):
-        full = ordered(first, w, swap(w, "task", n_parts), 1)
-        full = full.reshape(9, width, slots, n_parts, cs).swapaxes(2, 3)
-        return xor_order(full, 2, r, n_parts).reshape(9, width, channels)
-
-    def back_weights(w):
-        blocks = [w[:, :, i * width : (i + 1) * width] for i in range(n_parts)]
-        return jnp.concatenate([blocks[0]] + [swap(blocks[i], "task", i) for i in range(1, n_parts)], axis=1)
+    def weight_pieces(w, after=None):
+        halves = w.reshape(9, 2, cs // 2, channels)
+        sent = lax.dynamic_index_in_dim(halves, b % 2, axis=1, keepdims=False)
+        if after is not None:
+            sent = gate(sent, after)
+        return [w, swap(sent, "task", n_parts)]
+
+    def all_pieces(pieces):
+        return [swap(v, "task", i) if i else v for i in range(n_parts) for v in pieces]
 
     def all_parts(v):
         return [v] + [swap(v, "task", i) for i in range(1, n_parts)]
 
-    w1 = part_weights(conv1_weight)
-    pixel_major = jnp.swapaxes(images, 1, 2)
-    own_image = jnp.where(first, pixel_major[0], pixel_major[1])
-    other_image = jnp.where(first, pixel_major[1], pixel_major[0])
-    x_own = ordered(first, own_image, swap(other_image, "task", n_parts), 1)
-    x_parts = all_parts(x_own)
-    w2 = part_weights(conv2_weight)
-
-    lines = jnp.concatenate([norm1_gain, norm1_bias, norm2_gain, norm2_bias, head_bias])
-    lines = jnp.pad(lines, (0, -lines.shape[0] % channels)).reshape(-1, channels)
+    w1 = weight_pieces(conv1_weight)
+    w1.append(swap(w1[1], "batch", 1))
+    x_own, x_send = turn(meta, images)
+    x_other = swap(gate(x_send, w1[1]), "task", n_parts)
+    x_parts = list(zip(all_parts(x_own), all_parts(gate(x_other, w1[2]))))
+    w2 = weight_pieces(conv2_weight, x_other)
+
+    lines = jnp.pad(head_bias, (0, channels - tasks_here)).reshape(1, channels)
     mine = jnp.concatenate([head_weight.T.astype(f32), lines])
     mine = jnp.pad(mine, ((0, -mine.shape[0] % ROWS), (0, 0)))
-    gathered = lax.all_gather(mine, "task", axis=0)
-    table = gathered[:, :tasks_here].reshape(tasks, slots, n_parts, cs)
-    table = table.swapaxes(1, 2).reshape(tasks, channels)
-    flat = gathered[:, tasks_here : tasks_here + lines.shape[0]].reshape(n_task, -1)
-    bias_row = flat[:, 4 * cs : 4 * cs + tasks_here].reshape(1, tasks)
-    vecs = flat[:, : 4 * cs].reshape(slots, n_parts, 4, cs)
-    vecs = lax.dynamic_index_in_dim(vecs, r, axis=1, keepdims=False).swapaxes(0, 1).reshape(4, width)
-    vecs = jnp.pad(vecs, ((0, 0), (0, 2 * LANES - width))).reshape(ROWS, LANES)
+    every = xor_order([mine] + [swap(mine, "task", i) for i in range(1, n_task)], t)
+    table = jnp.concatenate([v[:tasks_here] for v in every])
+    table = table.reshape(tasks, slots, n_parts, cs).swapaxes(1, 2).reshape(tasks, channels)
+    bias_row = jnp.concatenate([v[tasks_here, :tasks_here] for v in every]).reshape(1, tasks)
+    vecs = jnp.stack([norm1_gain, norm1_bias, norm2_gain, norm2_bias])
+    vecs = jnp.pad(vecs, ((4, 0), (0, LANES - cs)))
     label_rows = lax.dynamic_update_slice(
         jnp.zeros((slots, LANES), f32), labels.astype(f32), (0, t * tasks_here)
     )
@@ -628,12 +805,12 @@
         flat_rows = rows.reshape(n_devices * ROWS, LANES)
         return lax.all_to_all(flat_rows, ("batch", "task"), 0, 0, tiled=True).reshape(rows.shape)
 
-    c1, stats = conv_stats(x_parts, w1, n_devices)
-    a_own, coefs1 = activate(c1, exchange(stats), weight, vecs)
-    a_parts = all_parts(a_own)
-    c2, stats = conv_stats(a_parts, w2, n_devices)
-    stats2 = exchange(stats)
-    sums, coefs2 = pool(meta, c2, x_own, stats2, weight, vecs, label_rows)
+    c1, stats = conv_stats(meta, vecs, w1, x_parts, n_devices)
+    w2.append(swap(gate(w2[1], stats), "batch", 1))
+    a_own, coefs1 = activate(meta, c1, exchange(stats), weight, n_parts)
+    a_parts = [[v] for v in all_parts(gate(a_own, w2[2]))]
+    c2, stats = conv_stats(meta, vecs, w2, a_parts, n_devices)
+    sums, coefs2 = pool(meta, c2, x_own, x_other, exchange(stats), weight, coefs1, label_rows)
     heads, task_weights, average_next, head_grad, bias_grad, pooled_rows = head(
         meta,
         exchange(sums),
@@ -645,21 +822,45 @@
         n_parts,
     )
 
-    def settle(keep, send):
-        total = lax.psum(keep + swap(send, "task", n_parts).astype(f32), "batch")
-        total = xor_order(total.reshape(9, cs, n_parts, slots, cs), 2, r, n_parts)
-        return total.swapaxes(2, 3).reshape(9, cs, channels)
-
-    low2, summed = grad_two(meta, c2, x_own, coefs2, vecs, heads, pixel_total)
+    def assemble(done):
+        parts = [v.reshape(9, cs, -1)[:, :, i * width : (i + 1) * width] for v in done for i in range(v.shape[1] // width)]
+        out = [
+            v.astype(f32)
+            for s in range(slots)
+            for v in xor_order([part[:, :, s * cs : (s + 1) * cs] for part in parts], r)
+        ]
+        return jnp.concatenate(out, axis=2)
+
+    def both_groups(keep, got):
+        return (keep + got.astype(f32)).reshape(9 * cs, -1)
+
+    bits = n_batch.bit_length() - 1
+    near = 1 << (bits // 2)
+    stages = [(1, near), (near, n_batch // near)]
+    low2, summed = grad_two(meta, c2, x_own, x_other, coefs2, coefs1, heads, pixel_total)
     low2_parts = all_parts(low2)
-    conv2_grad = settle(*weight_grad(meta, low2, a_parts))
-    dn1, stats = back_two(meta, low2_parts, back_weights(w2), c1, coefs1, vecs, n_devices)
-    low1, sums1 = grad_one(meta, c1, dn1, exchange(stats), weight, coefs1, vecs, pixel_total)
+    keep2, send2 = weight_grad(meta, low2, a_parts)
+    got2 = swap(send2, "task", n_parts)
+    dn1, stats = back_two(meta, all_pieces(w2), [gate(low2_parts[0], keep2)] + low2_parts[1:], c1, coefs1, n_devices)
+    low1, sums1 = grad_one(meta, c1, dn1, exchange(stats), weight, coefs1, pixel_total)
+    sum2 = scatter_stage(both_groups(keep2, gate(got2, dn1)), stages[0], bf16)
     low1_parts = all_parts(low1)
-    conv1_grad = settle(*weight_grad(meta, low1, x_parts))
-    keep, send = back_one(meta, low1_parts, back_weights(w1), summed)
-    got = swap(send, "task", n_parts).astype(f32)
-    input_grad = jnp.stack([jnp.where(first, keep, got), jnp.where(first, got, keep)])
+    pairs = []
+    for part in x_parts:
+        pairs.append(weight_grad(meta, gate(low1, pairs[-1][0]) if pairs else low1, [part]))
+    got1 = [swap(send, "task", n_parts) for _, send in pairs]
+    low1_parts[0] = gate(low1_parts[0], pairs[-1][0])
+    keep, send = back_one(meta, all_pieces(w1), low1_parts, summed)
+    sum2 = scatter_stage(gate(sum2, pairs[-1][0]), stages[1], f32, keep)
+    sum1 = [scatter_stage(both_groups(pair[0], gate(v, keep)), stages[0], bf16) for pair, v in zip(pairs, got1)]
+    sum2 = gather_stage(sum2.astype(bf16), stages[1])
+    sum1 = [scatter_stage(v, stages[1], bf16) for v in sum1]
+    sum2 = gather_stage(sum2, stages[0])
+    sum1 = [gather_stage(v.astype(bf16), stages[1]) for v in sum1]
+    sum1 = [gather_stage(v, stages[0]) for v in sum1]
+    input_grad = join(meta, keep, swap(send, "task", n_parts))
+    conv1_grad = assemble(sum1)
+    conv2_grad = assemble([sum2])
 
     def own_slice(rows, at):
         line = rows[at : at + 2].reshape(-1)

time: 551 us -> 346 us (0.63)
  waiting for transfers between devices: 208 us -> 85.4 us
  local copies, waits for them, and re-layouts: 89.6 us -> 15.5 us
  blocking collectives: 48.9 us -> 0 us
  starting transfers between devices: 24.2 us -> 68.6 us
  Pallas kernels: 118 us -> 156 us
  other arithmetic: 36.8 us -> 10.4 us
  between operations: 16.3 us -> 3.07 us
    psum x1 -> x0, waiting for transfers between devices: 123 us -> none  [settle(): total = lax.psum(keep + swap(send, 'task', n_parts).astype(f32), 'batch')]
    all_gather x1 -> x0, blocking collectives: 48.9 us -> none  [on_device(): gathered = lax.all_gather(mine, 'task', axis=0)]
    ppermute x12 -> x47, starting transfers between devices: 9.73 us -> 53.4 us  [swap(): return lax.ppermute(values, axis, [(i, i ^ by) for i in range(n)])]
    reshape x11 -> x3, local copies, waits for them, and re-layouts: 27.5 us -> 0.8 us  [on_device(): table.reshape(tasks, slots, n_parts, cs).swapaxes(1, 2)]
    unnamed x69 -> x60, local copies, waits for them, and re-layouts: 29 us -> 4.79 us
    pallas_call x5 -> x8, Pallas kernels: 65.3 us -> 87.5 us  [the longest x2 38.8 us: conv_stats(): pl.pallas_call(functools.partial(conv_kernel, n, per_part), in_specs=[SM]...]
    another operation x4 -> x1, local copies, waits for them, and re-layouts: 20.8 us -> 0.67 us  [on_device(): meta = jnp.stack([b, g, r, own_valid, b % 2]).astype(jnp.int32)]
    select_n x5 -> x9, other arithmetic: 13.8 us -> 0.76 us  [xor_order(): values = [jnp.where(flip, values[i ^ bit], v) for i, v in enumerate(values)]]
  transfers between devices with their start and end apart: 17 -> 51, of which waited for: 9 -> 20; matrix products, arithmetic and copies ran while one was open for 14% -> 6% of each run, Pallas kernels for 9% -> 33%
where the time goes in v2:
time: 346 us; the launch traced here: 339 us
  Pallas kernels  156 us (45%)
  waiting for transfers between devices  85.4 us (25%)
  starting transfers between devices  68.6 us (20%)
  local copies, waits for them, and re-layouts  15.5 us (4%)
  other arithmetic  10.4 us (3%)
    ppermute x47, starting transfers between devices, swap(): return lax.ppermute(values, axis, [(i, i ^ by) for i in range(n)])  53.4 us
    ppermute x47, waiting for transfers between devices, swap(): return lax.ppermute(values, axis, [(i, i ^ by) for i in range(n)])  52.9 us
    pallas_call x2, Pallas kernels, conv_stats(): pl.pallas_call(functools.partial(conv_kernel, n, per_part), in_specs=[SM]...  38.8 us
    pallas_call x3, Pallas kernels, weight_grad(): pl.pallas_call(functools.partial(weight_kernel, n, per_part), in_specs=[S...  35.3 us
    all_to_all x4, waiting for transfers between devices, exchange(): lax.all_to_all(flat_rows, ('batch', 'task'), 0, 0, tiled=True)  32.5 us
    pallas_call x1, Pallas kernels, back_two(): pl.pallas_call(functools.partial(back_two_kernel, n), in_specs=[SM] + [VM...  21.5 us
    pallas_call x1, Pallas kernels, back_one(): pl.pallas_call(functools.partial(back_one_kernel, n), in_specs=[SM] + [VM...  20.3 us
    all_to_all x4, starting transfers between devices, exchange(): lax.all_to_all(flat_rows, ('batch', 'task'), 0, 0, tiled=True)  15.2 us
  transfers between devices with their start and end apart: 51, of which 20 were waited for; matrix products, arithmetic and copies ran while one was open for 6% of the time, Pallas kernels for 33%

profile of v2, /device:TPU:0, one launch (start us, length us, event | category | flops | bytes accessed | tf_op | source)
XLA Modules:
  0.0 338.7 jit_solution(10675387401874218316)
XLA Ops:
  1.9 3.0 collective-permute-start
  6.8 4.0 %turn.1 = (bf16[4096,128]{1,0:T(8,128)(2,1)}, bf16[4096,128]{1,0:T(8,128)(2,1)}) custom-call(s32[5]{0:T(128)} %stack.42.meta, bf16[2,128,4096]{2,1,0:T(8,128)(2,1)} %images.1), custom_call_target="tpu_custom_call" | custom-call | flops 1048576 | bytes 4194304 | tf_op jit(solution)/shard_map/turn/pallas_call | solution.py:254
  10.8 7.6 %collective-permute-done.refs_1_ = bf16[9,64,512]{2,1,0:T(8,128)(2,1)} collective-permute-done((bf16[9,64,512]{2,1,0:T(8,128)(2,1)S(1)}, bf16[9,64,512]{2,1,0:T(8,128)(2,1)}, u32[]{:S(2)}, u32[]{:S(2)}) %collective-permute-start) | collective-permute-done | bytes 589856 | tf_op jit(solution)/shard_map/ppermute | solution.py:699
  21.6 12.6 %collective-permute-done.3.refs_2_ = bf16[9,64,512]{2,1,0:T(8,128)(2,1)S(1)} collective-permute-done((bf16[9,64,512]{2,1,0:T(8,128)(2,1)}, bf16[9,64,512]{2,1,0:T(8,128)(2,1)S(1)}, u32[]{:S(2)}, u32[]{:S(2)}) %collective-permute-start.3) | collective-permute-done | bytes 589856 | tf_op jit(solution)/shard_map/ppermute | solution.py:699
  34.2 8.7 %collective-permute-done.1.refs_4_.other.refs_1_ = bf16[4096,128]{1,0:T(8,128)(2,1)S(1)} collective-permute-done((bf16[4096,128]{1,0:T(8,128)(2,1)}, bf16[4096,128]{1,0:T(8,128)(2,1)S(1)}, u32[]{:S(2)}, u32[]{:S(2)}) %collective-permute-start.1) | collective-permute-done | bytes 1048608 | tf_op jit(solution)/shard_map/ppermute | solution.py:699
  46.1 19.8 %conv_stats.2 = (f32[4096,256]{1,0:T(8,128)}, f32[32,8,128]{2,1,0:T(8,128)}) custom-call(s32[5]{0:T(128)} %stack.42.meta, f32[8,128]{1,0:T(8,128)} %select_maximum_fusion.1.extra, bf16[9,128,512]{2,1,0:T(8,128)(2,1)} %refs_0_.7, bf16[9,64,512]{2,1,0:T(8,128)(2,1)} %collective-permute-done.refs_1_, bf16[9,64,512]{2,1,0:T(8,128)(2,1)} %copy-done.26, ...), custom_call_target="tpu_custom_call" | custom-call | flops 9663676416 | bytes 16777216 | tf_op jit(solution)/shard_map/conv_stats/pallas_call | solution.py:178
  67.6 4.4 %all-to-all-start = ((f32[32,8,128]{2,1,0:T(8,128)}), f32[32,8,128]{2,1,0:T(8,128)S(1)}, u32[]{:S(2)}, u32[]{:S(2)}) async-start(f32[32,8,128]{2,1,0:T(8,128)} %get-tuple-element.62), calls=%async_computation | async-start | bytes 262144 | tf_op jit(solution)/shard_map/all_to_all | solution.py:806
  72.1 11.0 %all-to-all-done.got = f32[32,8,128]{2,1,0:T(8,128)S(1)} async-done(((f32[32,8,128]{2,1,0:T(8,128)}), f32[32,8,128]{2,1,0:T(8,128)S(1)}, u32[]{:S(2)}, u32[]{:S(2)}) %all-to-all-start) | async-done | bytes 131104 | tf_op jit(solution)/shard_map/all_to_all | solution.py:806
  83.9 5.0 %activate.1 = (bf16[4096,256]{1,0:T(8,128)(2,1)}, f32[16,128]{1,0:T(8,128)}) custom-call(s32[5]{0:T(128)} %stack.42.meta, f32[4096,256]{1,0:T(8,128)} %get-tuple-element.64.c.refs_8_, f32[32,8,128]{2,1,0:T(8,128)} %copy-done.5, f32[32,128]{1,0:T(8,128)} %broadcast_in_dim.4.weight), custom_call_target="tpu_custom_call" | custom-call | flops 20971520 | bytes 6291456 | tf_op jit(solution)/shard_map/activate/pallas_call | solution.py:230
  94.2 19.0 %conv_stats.3 = (f32[4096,256]{1,0:T(8,128)}, f32[32,8,128]{2,1,0:T(8,128)}) custom-call(s32[5]{0:T(128)} %stack.42.meta, f32[8,128]{1,0:T(8,128)} %select_maximum_fusion.1.extra, bf16[9,128,512]{2,1,0:T(8,128)(2,1)} %refs_0_.6, bf16[9,64,512]{2,1,0:T(8,128)(2,1)} %copy-done.27, bf16[9,64,512]{2,1,0:T(8,128)(2,1)} %copy-done.28, ...), custom_call_target="tpu_custom_call" | custom-call | flops 9663676416 | bytes 16777216 | tf_op jit(solution)/shard_map/conv_stats/pallas_call | solution.py:178
  113.3 5.4 %all-to-all-start.1 = ((f32[32,8,128]{2,1,0:T(8,128)}), f32[32,8,128]{2,1,0:T(8,128)S(1)}, u32[]{:S(2)}, u32[]{:S(2)}) async-start(f32[32,8,128]{2,1,0:T(8,128)} %get-tuple-element.68), calls=%async_computation.1 | async-start | bytes 262144 | tf_op jit(solution)/shard_map/all_to_all | solution.py:806
  119.5 7.4 %all-to-all-done.1.got = f32[32,8,128]{2,1,0:T(8,128)S(1)} async-done(((f32[32,8,128]{2,1,0:T(8,128)}), f32[32,8,128]{2,1,0:T(8,128)S(1)}, u32[]{:S(2)}, u32[]{:S(2)}) %all-to-all-start.1) | async-done | bytes 131104 | tf_op jit(solution)/shard_map/all_to_all | solution.py:806
  127.5 6.9 %pool.1 = (f32[32,8,128]{2,1,0:T(8,128)}, f32[8,128]{1,0:T(8,128)}) custom-call(s32[5]{0:T(128)} %stack.42.meta, f32[4096,256]{1,0:T(8,128)} %get-tuple-element.67.c, bf16[4096,128]{1,0:T(8,128)(2,1)} %get-tuple-element.60.refs_3_.own.refs_0_, bf16[4096,128]{1,0:T(8,128)(2,1)} %copy-done, f32[32,8,128]{2,1,0:T(8,128)} %copy-done.4, ...), custom_call_target="tpu_custom_call" | custom-call | flops 31457280 | bytes 6291456 | tf_op jit(solution)/shard_map/pool/pallas_call | solution.py:335
  134.4 2.7 all-to-all-start.2
  137.8 7.6 %all-to-all-done.2.got = f32[32,8,128]{2,1,0:T(8,128)S(1)} async-done(((f32[32,8,128]{2,1,0:T(8,128)}), f32[32,8,128]{2,1,0:T(8,128)S(1)}, u32[]{:S(2)}, u32[]{:S(2)}) %all-to-all-start.2) | async-done | bytes 131104 | tf_op jit(solution)/shard_map/all_to_all | solution.py:806
  146.0 6.4 %head.1 = (f32[8,128]{1,0:T(8,128)}, f32[1,40]{1,0:T(1,128)}, f32[1,40]{1,0:T(1,128)}, f32[40,512]{1,0:T(8,128)}, f32[1,40]{1,0:T(1,128)}, /*index=5*/f32[2,256]{1,0:T(2,128)}) custom-call(s32[5]{0:T(128)} %stack.42.meta, f32[32,8,128]{2,1,0:T(8,128)} %copy-done.6, f32[40,512]{1,0:T(8,128)} %reshape.196.ht, f32[1,40]{1,0:T(1,128)} %maximum_bitcast_fusion.bias, ...), custom_call_target="tpu_custom_call" | custom-call | flops 1048576 | bytes 1048576 | tf_op jit(solution)/shard_map/head/pallas_call | solution.py:433
  152.4 7.4 %grad_two.1 = (bf16[4096,256]{1,0:T(8,128)(2,1)}, f32[4096,256]{1,0:T(8,128)}) custom-call(s32[5]{0:T(128)} %stack.42.meta, f32[4096,256]{1,0:T(8,128)} %get-tuple-element.67.c, bf16[4096,128]{1,0:T(8,128)(2,1)} %get-tuple-element.60.refs_3_.own.refs_0_, bf16[4096,128]{1,0:T(8,128)(2,1)} %copy-done, f32[8,128]{1,0:T(8,128)} %get-tuple-element.72.coefs, ...), custom_call_target="tpu_custom_call" | custom-call | flops 31457280 | bytes 12582912 | tf_op jit(solution)/shard_map/grad_two/pallas_call | solution.py:471
  161.1 15.8 %weight_grad.3 = (f32[9,128,512]{2,1,0:T(8,128)}, bf16[9,128,512]{2,1,0:T(8,128)(2,1)}) custom-call(s32[5]{0:T(128)} %stack.42.meta, bf16[4096,256]{1,0:T(8,128)(2,1)} %get-tuple-element.76.g.refs_6_, bf16[4096,256]{1,0:T(8,128)(2,1)} %get-tuple-element.66.refs_3_.refs_0_, bf16[4096,256]{1,0:T(8,128)(2,1)} %collective-permute-done.7.refs_4_.refs_1_), custom_call_target="tpu_custom_call" | custom-call | flops 9663676416 | bytes 16777216 | tf_op jit(solution)/shard_map/weight_grad/pallas_call | solution.py:685
  180.5 21.5 %back_two.1 = (f32[4096,256]{1,0:T(8,128)}, f32[32,8,128]{2,1,0:T(8,128)}) custom-call(s32[5]{0:T(128)} %stack.42.meta, bf16[9,128,512]{2,1,0:T(8,128)(2,1)} %refs_0_.6, bf16[9,64,512]{2,1,0:T(8,128)(2,1)} %copy-done.27, bf16[9,64,512]{2,1,0:T(8,128)(2,1)} %copy-done.28, bf16[9,128,512]{2,1,0:T(8,128)(2,1)} %collective-permute-done.14.refs_3_, ...), custom_call_target="tpu_custom_call" | custom-call | flops 9663676416 | bytes 16777216 | tf_op jit(solution)/shard_map/back_two/pallas_call | solution.py:602
  202.0 2.7 all-to-all-start.3
  206.5 6.5 %all-to-all-done.3.got = f32[32,8,128]{2,1,0:T(8,128)S(1)} async-done(((f32[32,8,128]{2,1,0:T(8,128)}), f32[32,8,128]{2,1,0:T(8,128)S(1)}, u32[]{:S(2)}, u32[]{:S(2)}) %all-to-all-start.3) | async-done | bytes 131104 | tf_op jit(solution)/shard_map/all_to_all | solution.py:806
  213.6 5.6 %grad_one.1 = (bf16[4096,256]{1,0:T(8,128)(2,1)}, f32[8,128]{1,0:T(8,128)}) custom-call(s32[5]{0:T(128)} %stack.42.meta, f32[4096,256]{1,0:T(8,128)} %get-tuple-element.64.c.refs_8_, f32[4096,256]{1,0:T(8,128)} %get-tuple-element.77.dn, f32[32,8,128]{2,1,0:T(8,128)} %copy-done.7, f32[32,128]{1,0:T(8,128)} %broadcast_in_dim.4.weight, ...), custom_call_target="tpu_custom_call" | custom-call | flops 10485760 | bytes 10485760 | tf_op jit(solution)/shard_map/grad_one/pallas_call | solution.py:516
  223.1 9.6 %weight_grad.4 = (f32[9,128,256]{2,1,0:T(8,128)}, bf16[9,128,256]{2,1,0:T(8,128)(2,1)}) custom-call(s32[5]{0:T(128)} %stack.42.meta, bf16[4096,256]{1,0:T(8,128)(2,1)} %get-tuple-element.83.g.refs_6_, bf16[4096,128]{1,0:T(8,128)(2,1)} %get-tuple-element.60.refs_3_.own.refs_0_, bf16[4096,128]{1,0:T(8,128)(2,1)} %copy-done), custom_call_target="tpu_custom_call" | custom-call | flops 4831838208 | bytes 16777216 | tf_op jit(solution)/shard_map/weight_grad/pallas_call | solution.py:685
  232.7 9.9 %weight_grad.5 = (f32[9,128,256]{2,1,0:T(8,128)}, bf16[9,128,256]{2,1,0:T(8,128)(2,1)}) custom-call(s32[5]{0:T(128)} %stack.42.meta, bf16[4096,256]{1,0:T(8,128)(2,1)} %get-tuple-element.83.g.refs_6_, bf16[4096,128]{1,0:T(8,128)(2,1)} %copy-done.24, bf16[4096,128]{1,0:T(8,128)(2,1)} %collective-permute-done.5.refs_6_.refs_1_), custom_call_target="tpu_custom_call" | custom-call | flops 4831838208 | bytes 16777216 | tf_op jit(solution)/shard_map/weight_grad/pallas_call | solution.py:685
  249.2 2.5 collective-permute-start.42
  251.7 20.3 %back_one.1 = (f32[128,4096]{1,0:T(8,128)}, bf16[128,4096]{1,0:T(8,128)(2,1)}) custom-call(s32[5]{0:T(128)} %stack.42.meta, bf16[9,128,512]{2,1,0:T(8,128)(2,1)} %refs_0_.7, bf16[9,64,512]{2,1,0:T(8,128)(2,1)} %collective-permute-done.refs_1_, bf16[9,64,512]{2,1,0:T(8,128)(2,1)} %copy-done.26, bf16[9,128,512]{2,1,0:T(8,128)(2,1)} %collective-permute-done.11.refs_3_, ...), custom_call_target="tpu_custom_call" | custom-call | flops 9663676416 | bytes 16777216 | tf_op jit(solution)/shard_map/back_one/pallas_call | solution.py:640
  273.5 9.8 %collective-permute-start.44 = (bf16[144,512]{1,0:T(8,128)(2,1)S(1)}, bf16[144,512]{1,0:T(8,128)(2,1)S(1)}, u32[]{:S(2)}, u32[]{:S(2)}) collective-permute-start(bf16[144,512]{1,0:T(8,128)(2,1)S(1)} %fusion.5), channel_id=1, source_target_pairs={{0,16},{4,20},{8,24},{12,28},{16,0},{20,4},{24,8},{28,12},{1,17},{... | collective-permute-start | bytes 442376 | tf_op jit(solution)/shard_map/ppermute | solution.py:699
  286.6 3.9 %collective-permute-done.44 = bf16[144,512]{1,0:T(8,128)(2,1)S(1)} collective-permute-done((bf16[144,512]{1,0:T(8,128)(2,1)S(1)}, bf16[144,512]{1,0:T(8,128)(2,1)S(1)}, u32[]{:S(2)}, u32[]{:S(2)}) %collective-permute-start.44) | collective-permute-done | bytes 147488 | tf_op jit(solution)/shard_map/ppermute | solution.py:699
  295.9 3.4 collective-permute-done.30
  301.0 2.8 collective-permute-done.23
  326.4 2.9 collective-permute-done.37
  333.9 4.4 %join.1 = f32[2,128,4096]{2,1,0:T(8,128)} custom-call(s32[5]{0:T(128)} %stack.42.meta, f32[128,4096]{1,0:T(8,128)} %get-tuple-element.85.keep, bf16[128,4096]{1,0:T(8,128)(2,1)} %copy-done.3), custom_call_target="tpu_custom_call" | custom-call | flops 1048576 | bytes 7340032 | tf_op jit(solution)/shard_map/join/pallas_call | solution.py:276
  (214 shorter events, 74.9 us)
Async XLA Ops:
  1.9 16.5 %collective-permute-start = (bf16[9,64,512]{2,1,0:T(8,128)(2,1)S(1)}, bf16[9,64,512]{2,1,0:T(8,128)(2,1)}, u32[]{:S(2)}, u32[]{:S(2)}) collective-permute-start(bf16[9,64,512]{2,1,0:T(8,128)(2,1)S(1)} %dynamic-slice_bitcast_fusion), channel_id=1, source_target_pairs={{0,2},{1,3},{2,0},{3,1},{4,6},{5,7},{6,4},{7,5},{8,10},{9,11},{10,... | collective-permute-start | bytes 1769480 | tf_op jit(solution)/shard_map/ppermute | solution.py:699
  18.3 24.6 %collective-permute-start.1 = (bf16[4096,128]{1,0:T(8,128)(2,1)}, bf16[4096,128]{1,0:T(8,128)(2,1)S(1)}, u32[]{:S(2)}, u32[]{:S(2)}) collective-permute-start(bf16[4096,128]{1,0:T(8,128)(2,1)} %get-tuple-element.58), channel_id=1, source_target_pairs={{0,2},{1,3},{2,0},{3,1},{4,6},{5,7},{6,4},{7,5},{8,10},{9,11},{10,... | collective-permute-start | bytes 3145736 | tf_op jit(solution)/shard_map/ppermute | solution.py:699
  20.1 14.1 %collective-permute-start.3 = (bf16[9,64,512]{2,1,0:T(8,128)(2,1)}, bf16[9,64,512]{2,1,0:T(8,128)(2,1)S(1)}, u32[]{:S(2)}, u32[]{:S(2)}) collective-permute-start(bf16[9,64,512]{2,1,0:T(8,128)(2,1)} %collective-permute-done.refs_1_), channel_id=1, source_target_pairs={{0,4},{4,0},{8,12},{12,8},{16,20},{20,16},{24,28},{28,24},{1,5},{5... | collective-permute-start | bytes 1769480 | tf_op jit(solution)/shard_map/ppermute | solution.py:699
  21.6 23.6 %collective-permute-start.4 = (bf16[4096,128]{1,0:T(8,128)(2,1)}, bf16[4096,128]{1,0:T(8,128)(2,1)S(1)}, u32[]{:S(2)}, u32[]{:S(2)}) collective-permute-start(bf16[4096,128]{1,0:T(8,128)(2,1)} %get-tuple-element.60.refs_3_.own.refs_0_), channel_id=1, source_target_pairs={{0,1},{1,0},{2,3},{3,2},{4,5},{5,4},{6,7},{7,6},{8,9},{9,8},{10,11... | collective-permute-start | bytes 3145736 | tf_op jit(solution)/shard_map/ppermute | solution.py:699
  43.6 22.3 %collective-permute-start.2 = (bf16[9,64,512]{2,1,0:T(8,128)(2,1)S(1)}, bf16[9,64,512]{2,1,0:T(8,128)(2,1)S(1)}, u32[]{:S(2)}, u32[]{:S(2)}) collective-permute-start(bf16[9,64,512]{2,1,0:T(8,128)(2,1)S(1)} %dynamic-slice_bitcast_fusion.1), channel_id=1, source_target_pairs={{0,2},{1,3},{2,0},{3,1},{4,6},{5,7},{6,4},{7,5},{8,10},{9,11},{10,... | collective-permute-start | bytes 1769480 | tf_op jit(solution)/shard_map/ppermute | solution.py:699
  65.9 23.0 %collective-permute-start.6 = (bf16[9,64,512]{2,1,0:T(8,128)(2,1)S(1)}, bf16[9,64,512]{2,1,0:T(8,128)(2,1)S(1)}, u32[]{:S(2)}, u32[]{:S(2)}) collective-permute-start(bf16[9,64,512]{2,1,0:T(8,128)(2,1)S(1)} %collective-permute-done.2.refs_1_), channel_id=1, source_target_pairs={{0,4},{4,0},{8,12},{12,8},{16,20},{20,16},{24,28},{28,24},{1,5},{5... | collective-permute-start | bytes 1769480 | tf_op jit(solution)/shard_map/ppermute | solution.py:699
  67.6 15.6 %all-to-all-start = ((f32[32,8,128]{2,1,0:T(8,128)}), f32[32,8,128]{2,1,0:T(8,128)S(1)}, u32[]{:S(2)}, u32[]{:S(2)}) async-start(f32[32,8,128]{2,1,0:T(8,128)} %get-tuple-element.62), calls=%async_computation | async-start | bytes 262144 | tf_op jit(solution)/shard_map/all_to_all | solution.py:806
  113.3 13.6 %all-to-all-start.1 = ((f32[32,8,128]{2,1,0:T(8,128)}), f32[32,8,128]{2,1,0:T(8,128)S(1)}, u32[]{:S(2)}, u32[]{:S(2)}) async-start(f32[32,8,128]{2,1,0:T(8,128)} %get-tuple-element.68), calls=%async_computation.1 | async-start | bytes 262144 | tf_op jit(solution)/shard_map/all_to_all | solution.py:806
  134.4 11.0 %all-to-all-start.2 = ((f32[32,8,128]{2,1,0:T(8,128)}), f32[32,8,128]{2,1,0:T(8,128)S(1)}, u32[]{:S(2)}, u32[]{:S(2)}) async-start(f32[32,8,128]{2,1,0:T(8,128)} %get-tuple-element.70), calls=%async_computation.2 | async-start | bytes 262144 | tf_op jit(solution)/shard_map/all_to_all | solution.py:806
  159.8 19.4 %collective-permute-start.17 = (bf16[4096,256]{1,0:T(8,128)(2,1)}, bf16[4096,256]{1,0:T(8,128)(2,1)S(1)}, u32[]{:S(2)}, u32[]{:S(2)}) collective-permute-start(bf16[4096,256]{1,0:T(8,128)(2,1)} %get-tuple-element.76.g.refs_6_), channel_id=1, source_target_pairs={{0,1},{1,0},{2,3},{3,2},{4,5},{5,4},{6,7},{7,6},{8,9},{9,8},{10,11... | collective-permute-start | bytes 6291464 | tf_op jit(solution)/shard_map/ppermute | solution.py:699
  160.0 18.3 %collective-permute-start.14 = (bf16[9,128,512]{2,1,0:T(8,128)(2,1)S(1)}, bf16[9,128,512]{2,1,0:T(8,128)(2,1)}, u32[]{:S(2)}, u32[]{:S(2)}) collective-permute-start(bf16[9,128,512]{2,1,0:T(8,128)(2,1)S(1)} %copy-done.9), channel_id=1, source_target_pairs={{0,1},{1,0},{2,3},{3,2},{4,5},{5,4},{6,7},{7,6},{8,9},{9,8},{10,11... | collective-permute-start | bytes 3538952 | tf_op jit(solution)/shard_map/ppermute | solution.py:699
  160.3 86.9 %collective-permute-start.11 = (bf16[9,128,512]{2,1,0:T(8,128)(2,1)}, bf16[9,128,512]{2,1,0:T(8,128)(2,1)}, u32[]{:S(2)}, u32[]{:S(2)}) collective-permute-start(bf16[9,128,512]{2,1,0:T(8,128)(2,1)} %refs_0_.7), channel_id=1, source_target_pairs={{0,1},{1,0},{2,3},{3,2},{4,5},{5,4},{6,7},{7,6},{8,9},{9,8},{10,11... | collective-permute-start | bytes 3538952 | tf_op jit(solution)/shard_map/ppermute | solution.py:699
  160.6 18.0 %collective-permute-start.15 = (bf16[9,64,512]{2,1,0:T(8,128)(2,1)}, bf16[9,64,512]{2,1,0:T(8,128)(2,1)}, u32[]{:S(2)}, u32[]{:S(2)}) collective-permute-start(bf16[9,64,512]{2,1,0:T(8,128)(2,1)} %copy-done.27), channel_id=1, source_target_pairs={{0,1},{1,0},{2,3},{3,2},{4,5},{5,4},{6,7},{7,6},{8,9},{9,8},{10,11... | collective-permute-start | bytes 1769480 | tf_op jit(solution)/shard_map/ppermute | solution.py:699
  160.8 18.0 %collective-permute-start.16 = (bf16[9,64,512]{2,1,0:T(8,128)(2,1)}, bf16[9,64,512]{2,1,0:T(8,128)(2,1)}, u32[]{:S(2)}, u32[]{:S(2)}) collective-permute-start(bf16[9,64,512]{2,1,0:T(8,128)(2,1)} %copy-done.28), channel_id=1, source_target_pairs={{0,1},{1,0},{2,3},{3,2},{4,5},{5,4},{6,7},{7,6},{8,9},{9,8},{10,11... | collective-permute-start | bytes 1769480 | tf_op jit(solution)/shard_map/ppermute | solution.py:699
  178.3 67.6 %collective-permute-start.12 = (bf16[9,64,512]{2,1,0:T(8,128)(2,1)}, bf16[9,64,512]{2,1,0:T(8,128)(2,1)}, u32[]{:S(2)}, u32[]{:S(2)}) collective-permute-start(bf16[9,64,512]{2,1,0:T(8,128)(2,1)} %collective-permute-done.refs_1_), channel_id=1, source_target_pairs={{0,1},{1,0},{2,3},{3,2},{4,5},{5,4},{6,7},{7,6},{8,9},{9,8},{10,11... | collective-permute-start | bytes 1769480 | tf_op jit(solution)/shard_map/ppermute | solution.py:699
  178.6 69.3 %collective-permute-start.13 = (bf16[9,64,512]{2,1,0:T(8,128)(2,1)}, bf16[9,64,512]{2,1,0:T(8,128)(2,1)}, u32[]{:S(2)}, u32[]{:S(2)}) collective-permute-start(bf16[9,64,512]{2,1,0:T(8,128)(2,1)} %copy-done.26), channel_id=1, source_target_pairs={{0,1},{1,0},{2,3},{3,2},{4,5},{5,4},{6,7},{7,6},{8,9},{9,8},{10,11... | collective-permute-start | bytes 1769480 | tf_op jit(solution)/shard_map/ppermute | solution.py:699
  178.8 41.2 %collective-permute-start.38 = (bf16[9,128,512]{2,1,0:T(8,128)(2,1)}, bf16[9,128,512]{2,1,0:T(8,128)(2,1)}, u32[]{:S(2)}, u32[]{:S(2)}) collective-permute-start(bf16[9,128,512]{2,1,0:T(8,128)(2,1)} %get-tuple-element.92), channel_id=1, source_target_pairs={{0,2},{1,3},{2,0},{3,1},{4,6},{5,7},{6,4},{7,5},{8,10},{9,11},{10,... | collective-permute-start | bytes 3538952 | tf_op jit(solution)/shard_map/ppermute | solution.py:699
  202.0 11.0 %all-to-all-start.3 = ((f32[32,8,128]{2,1,0:T(8,128)}), f32[32,8,128]{2,1,0:T(8,128)S(1)}, u32[]{:S(2)}, u32[]{:S(2)}) async-start(f32[32,8,128]{2,1,0:T(8,128)} %get-tuple-element.78), calls=%async_computation.3 | async-start | bytes 262144 | tf_op jit(solution)/shard_map/all_to_all | solution.py:806
  219.3 29.9 %collective-permute-start.18 = (bf16[4096,256]{1,0:T(8,128)(2,1)}, bf16[4096,256]{1,0:T(8,128)(2,1)}, u32[]{:S(2)}, u32[]{:S(2)}) collective-permute-start(bf16[4096,256]{1,0:T(8,128)(2,1)} %get-tuple-element.83.g.refs_6_), channel_id=1, source_target_pairs={{0,1},{1,0},{2,3},{3,2},{4,5},{5,4},{6,7},{7,6},{8,9},{9,8},{10,11... | collective-permute-start | bytes 6291464 | tf_op jit(solution)/shard_map/ppermute | solution.py:699
  222.6 21.3 %collective-permute-start.39 = (bf16[576,512]{1,0:T(8,128)(2,1)S(1)}, bf16[576,512]{1,0:T(8,128)(2,1)}, u32[]{:S(2)}, u32[]{:S(2)}) collective-permute-start(bf16[576,512]{1,0:T(8,128)(2,1)S(1)} %fusion), channel_id=1, source_target_pairs={{0,4},{4,0},{8,12},{12,8},{16,20},{20,16},{24,28},{28,24},{1,5},{5... | collective-permute-start | bytes 1769480 | tf_op jit(solution)/shard_map/ppermute | solution.py:699
  243.8 39.5 %collective-permute-start.20 = (bf16[9,128,256]{2,1,0:T(8,128)(2,1)}, bf16[9,128,256]{2,1,0:T(8,128)(2,1)S(1)}, u32[]{:S(2)}, u32[]{:S(2)}) collective-permute-start(bf16[9,128,256]{2,1,0:T(8,128)(2,1)} %get-tuple-element.87), channel_id=1, source_target_pairs={{0,2},{1,3},{2,0},{3,1},{4,6},{5,7},{6,4},{7,5},{8,10},{9,11},{10,... | collective-permute-start | bytes 1769480 | tf_op jit(solution)/shard_map/ppermute | solution.py:699
  245.9 39.0 %collective-permute-start.29 = (bf16[9,128,256]{2,1,0:T(8,128)(2,1)}, bf16[9,128,256]{2,1,0:T(8,128)(2,1)S(1)}, u32[]{:S(2)}, u32[]{:S(2)}) collective-permute-start(bf16[9,128,256]{2,1,0:T(8,128)(2,1)} %get-tuple-element.89), channel_id=1, source_target_pairs={{0,2},{1,3},{2,0},{3,1},{4,6},{5,7},{6,4},{7,5},{8,10},{9,11},{10,... | collective-permute-start | bytes 1769480 | tf_op jit(solution)/shard_map/ppermute | solution.py:699
  247.3 24.7 %collective-permute-start.40 = (f32[144,512]{1,0:T(8,128)S(1)}, f32[144,512]{1,0:T(8,128)S(1)}, u32[]{:S(2)}, u32[]{:S(2)}) collective-permute-start(f32[144,512]{1,0:T(8,128)S(1)} %get-tuple-element.108), channel_id=1, source_target_pairs={{0,8},{4,12},{8,0},{12,4},{16,24},{20,28},{24,16},{28,20},{1,9},{5... | collective-permute-start | bytes 884744 | tf_op jit(solution)/shard_map/ppermute | solution.py:699
  247.9 24.0 %collective-permute-start.41 = (f32[144,512]{1,0:T(8,128)S(1)}, f32[144,512]{1,0:T(8,128)S(1)}, u32[]{:S(2)}, u32[]{:S(2)}) collective-permute-start(f32[144,512]{1,0:T(8,128)S(1)} %get-tuple-element.110), channel_id=1, source_target_pairs={{0,16},{4,20},{8,24},{12,28},{16,0},{20,4},{24,8},{28,12},{1,17},{... | collective-permute-start | bytes 884744 | tf_op jit(solution)/shard_map/ppermute | solution.py:699
  249.2 22.8 %collective-permute-start.42 = (f32[144,512]{1,0:T(8,128)S(1)}, f32[144,512]{1,0:T(8,128)S(1)}, u32[]{:S(2)}, u32[]{:S(2)}) collective-permute-start(f32[144,512]{1,0:T(8,128)S(1)} %get-tuple-element.109), channel_id=1, source_target_pairs={{0,24},{4,28},{8,16},{12,20},{16,8},{20,12},{24,0},{28,4},{1,25},{... | collective-permute-start | bytes 884744 | tf_op jit(solution)/shard_map/ppermute | solution.py:699
  272.1 13.7 %collective-permute-start.43 = (bf16[144,512]{1,0:T(8,128)(2,1)S(1)}, bf16[144,512]{1,0:T(8,128)(2,1)S(1)}, u32[]{:S(2)}, u32[]{:S(2)}) collective-permute-start(bf16[144,512]{1,0:T(8,128)(2,1)S(1)} %fusion.5), channel_id=1, source_target_pairs={{0,24},{4,28},{8,16},{12,20},{16,8},{20,12},{24,0},{28,4},{1,25},{... | collective-permute-start | bytes 442376 | tf_op jit(solution)/shard_map/ppermute | solution.py:699
  273.5 17.1 %collective-permute-start.44 = (bf16[144,512]{1,0:T(8,128)(2,1)S(1)}, bf16[144,512]{1,0:T(8,128)(2,1)S(1)}, u32[]{:S(2)}, u32[]{:S(2)}) collective-permute-start(bf16[144,512]{1,0:T(8,128)(2,1)S(1)} %fusion.5), channel_id=1, source_target_pairs={{0,16},{4,20},{8,24},{12,28},{16,0},{20,4},{24,8},{28,12},{1,17},{... | collective-permute-start | bytes 442376 | tf_op jit(solution)/shard_map/ppermute | solution.py:699
  283.5 10.3 %collective-permute-start.21 = (bf16[576,256]{1,0:T(8,128)(2,1)S(1)}, bf16[576,256]{1,0:T(8,128)(2,1)S(1)}, u32[]{:S(2)}, u32[]{:S(2)}) collective-permute-start(bf16[576,256]{1,0:T(8,128)(2,1)S(1)} %fusion.1), channel_id=1, source_target_pairs={{0,4},{4,0},{8,12},{12,8},{16,20},{20,16},{24,28},{28,24},{1,5},{5... | collective-permute-start | bytes 884744 | tf_op jit(solution)/shard_map/ppermute | solution.py:699
  285.1 14.2 %collective-permute-start.30 = (bf16[576,256]{1,0:T(8,128)(2,1)S(1)}, bf16[576,256]{1,0:T(8,128)(2,1)S(1)}, u32[]{:S(2)}, u32[]{:S(2)}) collective-permute-start(bf16[576,256]{1,0:T(8,128)(2,1)S(1)} %fusion.2), channel_id=1, source_target_pairs={{0,4},{4,0},{8,12},{12,8},{16,20},{20,16},{24,28},{28,24},{1,5},{5... | collective-permute-start | bytes 884744 | tf_op jit(solution)/shard_map/ppermute | solution.py:699
  285.8 47.0 %collective-permute-start.19 = (bf16[128,4096]{1,0:T(8,128)(2,1)S(1)}, bf16[128,4096]{1,0:T(8,128)(2,1)S(1)}, u32[]{:S(2)}, u32[]{:S(2)}) collective-permute-start(bf16[128,4096]{1,0:T(8,128)(2,1)S(1)} %copy-done.25), channel_id=1, source_target_pairs={{0,2},{1,3},{2,0},{3,1},{4,6},{5,7},{6,4},{7,5},{8,10},{9,11},{10,... | collective-permute-start | bytes 3145736 | tf_op jit(solution)/shard_map/ppermute | solution.py:699
  291.4 32.1 %collective-permute-start.46 = (bf16[576,512]{1,0:T(8,128)(2,1)S(1)}, bf16[576,512]{1,0:T(8,128)(2,1)S(1)}, u32[]{:S(2)}, u32[]{:S(2)}) collective-permute-start(bf16[576,512]{1,0:T(8,128)(2,1)S(1)} %pad_maximum_fusion.3), channel_id=1, source_target_pairs={{0,4},{4,0},{8,12},{12,8},{16,20},{20,16},{24,28},{28,24},{1,5},{5... | collective-permute-start | bytes 1769480 | tf_op jit(solution)/shard_map/ppermute | solution.py:699
  295.7 8.1 %collective-permute-start.23 = (bf16[144,256]{1,0:T(8,128)(2,1)S(1)}, bf16[144,256]{1,0:T(8,128)(2,1)S(1)}, u32[]{:S(2)}, u32[]{:S(2)}) collective-permute-start(bf16[144,256]{1,0:T(8,128)(2,1)S(1)} %get-tuple-element.123), channel_id=1, source_target_pairs={{0,16},{4,20},{8,24},{12,28},{16,0},{20,4},{24,8},{28,12},{1,17},{... | collective-permute-start | bytes 221192 | tf_op jit(solution)/shard_map/ppermute | solution.py:699
  (49 other events, 521.0 us)

commit v3 on v1

v3 whole, which is shorter than its diff:
```python
import functools

import jax
import jax.numpy as jnp
from jax import lax
from jax.experimental import pallas as pl
from jax.experimental.pallas import tpu as pltpu
from jax.sharding import PartitionSpec as P

SIDE = 64
FW_STEPS = 20
LANES = 128
ROWS = 8

eps = 1e-05
loss_scale = 4096.0
highest = lax.Precision.HIGHEST
f32 = jnp.float32
bf16 = jnp.bfloat16


def params(mib, **more):
    return pltpu.CompilerParams(vmem_limit_bytes=mib << 20, **more)


def cost(flops, moved):
    return pl.CostEstimate(flops=flops, bytes_accessed=moved, transcendentals=0)


VM = pl.BlockSpec(memory_space=pltpu.VMEM)
HB = pl.BlockSpec(memory_space=pl.ANY)
SM = pl.BlockSpec(memory_space=pltpu.SMEM)


def sigmoid(v):
    return 1.0 / (1.0 + jnp.exp(-v))


def silu_slope(v):
    s = sigmoid(v)
    return s * (1.0 + v * (1.0 - s))


def half(h):
    return slice(h * LANES, (h + 1) * LANES)


def held(values):
    return pltpu.with_memory_space_constraint(values, pltpu.VMEM)


def away(values):
    return pltpu.with_memory_space_constraint(values, pltpu.HBM)


def vmem_out(shape, kind):
    return pltpu.VMEM(shape, kind)


def hbm_out(shape, kind):
    return pltpu.HBM(shape, kind)


def column_is(rows, width, at):
    return (lax.broadcasted_iota(jnp.int32, (rows, width), 0) & (SIDE - 1)) == at


def moved(v, e):
    rows, width = v.shape
    if e == 0:
        return v
    edge = SIDE - 1 if e == 1 else 0
    return jnp.where(column_is(rows, width, edge), 0.0, pltpu.roll(v, rows - 1 if e == 1 else 1, 0))


def aligned(cs):
    return cs % LANES == 0


def column_plan(meta, parts, n_parts, cs):
    g, r = meta[1], meta[2]
    plan = []
    for i, part in enumerate(parts):
        if not aligned(cs):
            plan.append((part[0], slice(0, 2 * cs), i * 2 * cs))
            continue
        for s in range(2):
            place = s * n_parts + (r ^ i) if len(part) == 1 else (g, 1 - g)[s] * n_parts + (r ^ i)
            ref, cols = (part[0], slice(s * cs, (s + 1) * cs)) if len(part) == 1 else (part[s], slice(0, cs))
            plan.append((ref, cols, pl.multiple_of(place * cs, cs)))
    return plan


def place_columns(dst, plan, first_row):
    rows = plan[0][0].shape[0]
    block = 512

    def step(j, carry):
        at = pl.multiple_of(j * block, block)
        for ref, cols, to in plan:
            width = cols.stop - cols.start
            dst[pl.ds(pl.multiple_of(at + first_row, SIDE), block), pl.ds(to, width)] = ref[pl.ds(at, block), cols]
        return carry

    lax.fori_loop(0, rows // block, step, 0)


def clear_ends(dst, rows):
    zero = jnp.zeros((SIDE, dst.shape[1]), dst.dtype)
    dst[0:SIDE, :] = zero
    dst[SIDE + rows : SIDE + rows + SIDE, :] = zero


def piece_rows(meta, cs, base, n_pieces):
    g, q = meta[1], meta[4]
    qs = cs // (n_pieces - 1)
    return [pl.ds(pl.multiple_of(base + g * cs, cs), cs)] + [
        pl.ds(pl.multiple_of(base + (1 - g) * cs + (q ^ i if n_pieces > 2 else 0) * qs, qs), qs)
        for i in range(n_pieces - 1)
    ]


def forward_copies(meta, pieces, w, cs, sems):
    if not aligned(cs):
        return [pltpu.make_async_copy(pieces[0], w, sems.at[0])]
    spots = piece_rows(meta, cs, 0, len(pieces))
    return [pltpu.make_async_copy(p, w.at[:, to, :], sems.at[i]) for i, (p, to) in enumerate(zip(pieces, spots))]


def backward_copies(meta, pieces, w, cs, n_parts, sems):
    width = 2 * cs
    if not aligned(cs):
        return [
            pltpu.make_async_copy(p, w.at[:, pl.ds(i * width, width), :], sems.at[i]) for i, p in enumerate(pieces)
        ]
    copies = []
    for i in range(n_parts):
        each = len(pieces) // n_parts
        for p, to in zip(pieces[each * i : each * (i + 1)], piece_rows(meta, cs, i * width, each)):
            for s in range(2):
                cols = pl.ds(pl.multiple_of((s * n_parts + meta[2]) * cs, cs), cs)
                copies.append(
                    pltpu.make_async_copy(p.at[:, :, cols], w.at[:, to, pl.ds(s * cs, cs)], sems.at[len(copies)])
                )
    return copies


def part_half(part, first, rows, h):
    if len(part) == 1:
        return part[0][rows, half(h)].astype(f32)
    own, other = part[0][rows, :], part[1][rows, :]
    return (jnp.where(first, own, other) if h == 0 else jnp.where(first, other, own)).astype(f32)


def row_blocks(rows, block, body, start):
    def step(j, carry):
        return body(pl.ds(pl.multiple_of(j * block, block), block), carry)

    return lax.fori_loop(0, rows // block, step, start)


def send_rows(out, rows, base=None):
    n = out.shape[0]
    start = jnp.zeros((ROWS, LANES), f32) if base is None else base
    out[...] = jnp.broadcast_to(start[None], out.shape)
    for at, value in rows:
        out[:, at : at + 1, :] = jnp.broadcast_to(value[None], (n, 1, LANES))


def weighted(got, weight):
    return jnp.sum(got[...] * weight[...], axis=0)


def norm_coefs(got, weight, rows):
    w = weight[...]
    values = got[...]
    count = jnp.sum(w, axis=0)
    total = jnp.sum(values * w, axis=0)
    mean = total / count
    off = values - mean[None]
    apart = jnp.sum(off * off * w, axis=0)
    squares = total[2:4] + rows * apart[0:2]
    return mean[0:2], lax.rsqrt(squares / (count[0:2] * rows) + eps)


def stream_in(source, buffer, sems, block):
    rows = buffer.shape[0]

    def copy(j):
        at = pl.ds(pl.multiple_of(j * block, block), block)
        return pltpu.make_async_copy(source.at[at, :], buffer.at[at, :], sems.at[j])

    for j in range(rows // block):
        copy(j).start()
    return lambda j: copy(j).wait()


def stream_out(buffer, target, sems, block):
    rows = buffer.shape[0]

    def copy(j):
        at = pl.ds(pl.multiple_of(j * block, block), block)
        return pltpu.make_async_copy(buffer.at[at, :], target.at[at, :], sems.at[j])

    def finish():
        for j in range(rows // block):
            copy(j).wait()

    return (lambda j: copy(j).start()), finish


def stream_scratch(rows, width, block):
    return [pltpu.VMEM((rows, width), f32), pltpu.SemaphoreType.DMA((rows // block,))]


BLOCK = 512
CHUNK = 1024


def conv_kernel(parts_of, n_parts, n_pieces, meta, extra, *refs):
    pieces, refs = refs[:n_pieces], refs[n_pieces:]
    n = sum(parts_of)
    xs, (target, stats, scratch, w, sems, out, out_sems) = refs[:n], refs[n:]
    parts, at = [], 0
    for size in parts_of:
        parts.append(xs[at : at + size])
        at += size
    rows, width = out.shape
    cs = width // 2
    chunk = CHUNK
    send, finish = stream_out(out, target, out_sems, chunk)
    copies = forward_copies(meta, pieces, w, cs, sems)
    for c in copies:
        c.start()
    clear_ends(scratch, rows)
    place_columns(scratch, column_plan(meta, parts, n_parts, cs), SIDE)
    for c in copies:
        c.wait()

    def step(j, carry):
        mean, squares = carry
        at = pl.multiple_of(j * chunk, chunk)
        total = None
        for dx in (0, 1, -1):
            acc = None
            for dy in (-1, 0, 1):
                lhs = scratch[pl.ds(pl.multiple_of(at + SIDE * (dy + 1), SIDE), chunk), :]
                tap = w[3 * (dy + 1) + dx + 1]
                term = lax.dot_general(lhs, tap, (((1,), (1,)), ((), ())), preferred_element_type=f32)
                acc = term if acc is None else acc + term
            acc = moved(acc, dx)
            total = acc if total is None else total + acc
        out[pl.ds(at, chunk), :] = total
        send(j)
        here = jnp.sum(total, axis=0, keepdims=True) / chunk
        away = out[pl.ds(at, chunk), :] - here
        spread = jnp.sum(away * away, axis=0, keepdims=True)
        before = jnp.asarray(j, f32)
        gap = here - mean
        share = before / (before + 1.0)
        return mean + gap / (before + 1.0), squares + spread + gap * gap * (share * chunk)

    zero = jnp.zeros((1, width), f32)
    mean, squares = lax.fori_loop(0, rows // chunk, step, (zero, zero))
    send_rows(
        stats,
        [(h, mean[:, half(h)]) for h in range(width // LANES)]
        + [(2 + h, squares[:, half(h)]) for h in range(width // LANES)],
        extra[...],
    )
    finish()


def conv_stats(meta, extra, pieces, parts, cs, n_devices, weight_of):
    rows, width, channels = parts[0][0].shape[0], 2 * cs, pieces[0].shape[2]
    flat = [v for part in parts for v in part]
    return pl.pallas_call(
        functools.partial(conv_kernel, [len(p) for p in parts], len(parts), len(pieces)),
        in_specs=[SM, VM] + [HB] * len(pieces) + [VM] * len(flat),
        out_specs=(HB, VM),
        out_shape=(hbm_out((rows, width), f32), vmem_out((n_devices, ROWS, LANES), f32)),
        scratch_shapes=[
            pltpu.VMEM((rows + 2 * SIDE, channels), bf16),
            pltpu.VMEM((9, width, channels), bf16),
            pltpu.SemaphoreType.DMA((len(pieces),)),
            *stream_scratch(rows, width, CHUNK),
        ],
        compiler_params=params(20),
        cost_estimate=cost(weight_of * rows * width * channels, weight_of << 20),
        name="conv_stats",
    )(meta, extra, *[away(v) for v in pieces], *[held(v) for v in flat])


def act_kernel(n_parts, meta, source, got, weight, out, coefs, c, sems):
    rows, width = c.shape
    halves, cs = width // LANES, width // 2
    wait = stream_in(source, c, sems, BLOCK)
    mean, scale = norm_coefs(got, weight, loss_scale)
    coefs[...] = jnp.zeros(coefs.shape, f32)
    coefs[0:2, :] = mean
    coefs[2:4, :] = scale
    for v in range(4):
        for g in range(2):
            row = got[g * n_parts + meta[2], 4 + v : 5 + v, 0:cs]
            lo = g * cs
            coefs[4 + 2 * v + lo // LANES : 5 + 2 * v + lo // LANES, lo % LANES : lo % LANES + cs] = row

    def body(at, carry):
        wait(at.start // BLOCK)
        for h in range(halves):
            normed = (c[at, half(h)] - coefs[h : h + 1, :]) * coefs[2 + h : 3 + h, :]
            normed = normed * coefs[4 + h : 5 + h, :] + coefs[6 + h : 7 + h, :]
            out[at, half(h)] = (normed * sigmoid(normed)).astype(bf16)
        return carry

    row_blocks(rows, BLOCK, body, 0)


def activate(meta, c, got, weight, n_parts):
    rows, width = c.shape
    return pl.pallas_call(
        functools.partial(act_kernel, n_parts),
        in_specs=[SM, HB, VM, VM],
        out_specs=(VM, VM),
        out_shape=(vmem_out((rows, width), bf16), vmem_out((2 * ROWS, LANES), f32)),
        scratch_shapes=stream_scratch(rows, width, BLOCK),
        compiler_params=params(12),
        cost_estimate=cost(20 * rows * width, 6 * rows * width),
        name="activate",
    )(meta, away(c), held(got), weight)


def turn_kernel(meta, images, own, other, buffer, sems):
    g = meta[1]
    rows = own.shape[0]
    block = 1024
    n = rows // block

    def copy(i, s):
        cols = pl.ds(pl.multiple_of(i * block, block), block)
        which = (1 - g, g)[s]
        return pltpu.make_async_copy(images.at[which, :, cols], buffer.at[s, :, cols], sems.at[s, i])

    for s in range(2):
        for i in range(n):
            copy(i, s).start()
    for s, out in ((0, other), (1, own)):

        def step(i, carry, s=s, out=out):
            copy(i, s).wait()
            cols = pl.ds(pl.multiple_of(i * block, block), block)
            out[cols, :] = buffer[s, :, cols].T
            return carry

        lax.fori_loop(0, n, step, 0)


def turn(meta, images):
    slots, cs, rows = images.shape
    return pl.pallas_call(
        turn_kernel,
        in_specs=[SM, HB],
        out_specs=(VM, VM),
        out_shape=(vmem_out((rows, cs), bf16),) * 2,
        scratch_shapes=[pltpu.VMEM((slots, cs, rows), bf16), pltpu.SemaphoreType.DMA((slots, rows // 1024))],
        compiler_params=params(8),
        cost_estimate=cost(1 << 20, 8 * rows * cs),
        name="turn",
    )(meta, away(images))


def join_kernel(meta, got, half_done, out, buffer, sems):
    cs, rows = got.shape
    block = 1024
    n = rows // block
    del half_done

    def copy(i):
        cols = pl.ds(pl.multiple_of(i * block, block), block)
        return pltpu.make_async_copy(buffer.at[:, cols], out.at[1 - meta[1], :, cols], sems.at[i])

    for i in range(n):
        cols = slice(i * block, (i + 1) * block)
        buffer[:, cols] = got[:, cols].astype(f32)
        copy(i).start()
    for i in range(n):
        copy(i).wait()


def join(meta, got, half_done):
    cs, rows = got.shape
    return pl.pallas_call(
        join_kernel,
        in_specs=[SM, VM, HB],
        out_specs=HB,
        out_shape=hbm_out(half_done.shape, f32),
        scratch_shapes=[pltpu.VMEM((cs, rows), f32), pltpu.SemaphoreType.DMA((rows // 1024,))],
        input_output_aliases={2: 0},
        compiler_params=params(8),
        cost_estimate=cost(1 << 20, 8 * rows * cs),
        name="join",
    )(meta, held(got), away(half_done))


def pool_kernel(n_x, meta, source, *refs):
    x, (got, weight, coefs1, labels, out, coefs, c, sems) = refs[:n_x], refs[n_x:]
    rows, width = c.shape
    halves = width // LANES
    first = meta[1] == 0
    wait = stream_in(source, c, sems, BLOCK)
    mean, scale = norm_coefs(got, weight, loss_scale)
    coefs[...] = jnp.zeros(coefs.shape, f32)
    coefs[0:2, :] = mean
    coefs[2:4, :] = scale

    def body(at, carry):
        wait(at.start // BLOCK)
        sums = list(carry)
        for h in range(halves):
            hat = (c[at, half(h)] - coefs[h : h + 1, :]) * coefs[2 + h : 3 + h, :]
            v = hat * coefs1[8 + h : 9 + h, :] + coefs1[10 + h : 11 + h, :] + part_half(x, first, at, h)
            s = sigmoid(v)
            slope = s * (1.0 + v * (1.0 - s))
            sums[3 * h] += jnp.sum(v * s, axis=0, keepdims=True)
            sums[3 * h + 1] += jnp.sum(slope * hat, axis=0, keepdims=True)
            sums[3 * h + 2] += jnp.sum(slope, axis=0, keepdims=True)
        return tuple(sums)

    sums = row_blocks(rows, BLOCK, body, (jnp.zeros((1, LANES), f32),) * (3 * halves))
    valid = meta[3].astype(f32)
    lines = [(6, labels[0:1, :]), (7, labels[1:2, :])]
    for h in range(halves):
        lines.append((h, sums[3 * h] * (valid / loss_scale)))
        lines.append((2 + h, sums[3 * h + 1]))
        lines.append((4 + h, sums[3 * h + 2]))
    send_rows(out, lines)


def pool(meta, c, x, got, weight, coefs1, labels):
    rows, width = c.shape
    return pl.pallas_call(
        functools.partial(pool_kernel, len(x)),
        in_specs=[SM, HB] + [VM] * (4 + len(x)),
        out_specs=(VM, VM),
        out_shape=(vmem_out(got.shape, f32), vmem_out((ROWS, LANES), f32)),
        scratch_shapes=stream_scratch(rows, width, BLOCK),
        compiler_params=params(12),
        cost_estimate=cost(30 * rows * width, 6 * rows * width),
        name="pool",
    )(meta, away(c), *[held(v) for v in x], held(got), weight, held(coefs1), labels)


def head_kernel(n_parts, meta, got, ht, bias, valid, avg_row, avg_col, coefs, tw, an, hwg, hbg, pooled_own, pooled, slopes, shifts, labels, grads, mine_all, pooled_part):
    tasks, channels = ht.shape
    images = valid.shape[0]
    n_task = 2 * n_parts
    width = channels // n_parts
    halves = width // LANES
    r = meta[2]
    for n in range(images):
        base = (n // 2) * n_task + (n % 2) * n_parts
        for part in range(n_parts):
            for h in range(halves):
                lo = part * width + h * LANES
                pooled[n : n + 1, lo : lo + LANES] = got[base + part, h : h + 1, :]
        for h in range(halves):
            slopes[n : n + 1, half(h)] = got[base + r, 2 + h : 3 + h, :]
            shifts[n : n + 1, half(h)] = got[base + r, 4 + h : 5 + h, :]
        row = 6 + n % 2
        lab = got[(n // 2) * n_task, row : row + 1, :]
        for t in range(1, n_task):
            lab = lab + got[(n // 2) * n_task + t, row : row + 1, :]
        labels[n : n + 1, :] = lab
    pooled_all = pooled[...]
    table = ht[...]
    both_last = (((1,), (1,)), ((), ()))
    both_first = (((0,), (0,)), ((), ()))
    logits = lax.dot_general(pooled_all, table, both_last, precision=highest, preferred_element_type=f32) + bias[...]
    count = jnp.sum(valid[...], axis=0, keepdims=True)
    errors = valid[...] * (sigmoid(logits) - labels[:, 0:tasks]) / count
    gram = lax.dot_general(errors, errors, both_first, precision=highest, preferred_element_type=f32) * lax.dot_general(
        table, table, both_last, precision=highest, preferred_element_type=f32
    )
    row_id = lax.broadcasted_iota(jnp.int32, (tasks, tasks), 0)
    col_id = lax.broadcasted_iota(jnp.int32, (tasks, tasks), 1)
    trace = jnp.sum(jnp.sum(jnp.where(row_id == col_id, gram, 0.0), axis=1, keepdims=True), axis=0, keepdims=True)
    normalized = gram / (trace / tasks)
    start_row = avg_row[...] / jnp.sum(avg_row[...], axis=1, keepdims=True)
    start_col = avg_col[...] / jnp.sum(avg_col[...], axis=0, keepdims=True)
    w_row, w_col = start_row, start_col
    for j in range(FW_STEPS):
        rate = 1.0 / (j + 4.0)
        z_col = -tasks * jnp.sum(normalized * w_row, axis=1, keepdims=True)
        z_row = -tasks * jnp.sum(normalized * w_col, axis=0, keepdims=True)
        e_col = jnp.exp(z_col - jnp.max(z_col, axis=0, keepdims=True))
        e_row = jnp.exp(z_row - jnp.max(z_row, axis=1, keepdims=True))
        w_col = (1.0 - rate) * w_col + rate * (e_col / jnp.sum(e_col, axis=0, keepdims=True))
        w_row = (1.0 - rate) * w_row + rate * (e_row / jnp.sum(e_row, axis=1, keepdims=True))
    tw[...] = w_row
    an[...] = 0.9 * start_row + 0.1 * w_row
    logit_grads = errors * ((loss_scale * tasks) * w_row)
    hbg[...] = jnp.sum(logit_grads, axis=0, keepdims=True)
    hwg[...] = lax.dot_general(logit_grads, pooled_all, both_first, precision=highest, preferred_element_type=f32)
    grads[...] = jnp.dot(logit_grads, table, precision=highest, preferred_element_type=f32) / loss_scale
    own = pl.ds(pl.multiple_of(r * width, LANES), width)
    q = grads[:, own]
    mine_all[...] = q
    pooled_part[...] = pooled[:, own]
    gain = jnp.sum(q * slopes[...], axis=0, keepdims=True)
    shift = jnp.sum(q * shifts[...], axis=0, keepdims=True)
    mine = mine_all[pl.ds(2 * meta[0] + meta[1], 1), :]
    coefs[...] = jnp.zeros(coefs.shape, f32)
    for h in range(halves):
        coefs[h : h + 1, :] = gain[:, half(h)]
        coefs[2 + h : 3 + h, :] = shift[:, half(h)]
        coefs[4 + h : 5 + h, :] = mine[:, half(h)]
    for i in range(2):
        pooled_own[i : i + 1, :] = pooled_part[pl.ds(2 * meta[0] + i, 1), :]


def head(meta, got, ht, bias, valid, avg_row, avg_col, n_parts):
    tasks, channels = ht.shape
    images = valid.shape[0]
    width = channels // n_parts
    shapes = [(ROWS, LANES), (1, tasks), (1, tasks), (tasks, channels), (1, tasks), (2, width)]
    return pl.pallas_call(
        functools.partial(head_kernel, n_parts),
        in_specs=[SM] + [VM] * 6,
        out_specs=tuple(VM for _ in shapes),
        out_shape=tuple(jax.ShapeDtypeStruct(s, f32) for s in shapes),
        scratch_shapes=[
            pltpu.VMEM((images, channels), f32),
            pltpu.VMEM((images, width), f32),
            pltpu.VMEM((images, width), f32),
            pltpu.VMEM((images, LANES), f32),
            pltpu.VMEM((images, channels), f32),
            pltpu.VMEM((images, width), f32),
            pltpu.VMEM((images, width), f32),
        ],
        compiler_params=params(60),
        cost_estimate=cost(1 << 20, 1 << 20),
        name="head",
    )(meta, got, ht, bias, valid, avg_row, avg_col)


def grad_two_kernel(n_x, meta, source, *refs):
    x, (coefs, coefs1, heads, pixels, low, target, c, sems, summed, out_sems) = refs[:n_x], refs[n_x:]
    rows, width = c.shape
    valid = meta[3].astype(f32)
    first = meta[1] == 0
    wait = stream_in(source, c, sems, BLOCK)
    send, finish = stream_out(summed, target, out_sems, BLOCK)

    def body(at, carry):
        wait(at.start // BLOCK)
        for h in range(width // LANES):
            mean, scale = coefs[h : h + 1, :], coefs[2 + h : 3 + h, :]
            gain = coefs1[8 + h : 9 + h, :]
            hat = (c[at, half(h)] - mean) * scale
            v = hat * gain + coefs1[10 + h : 11 + h, :] + part_half(x, first, at, h)
            dn = (valid * heads[4 + h : 5 + h, :]) * silu_slope(v)
            summed[at, half(h)] = dn
            away = (heads[2 + h : 3 + h, :] + hat * heads[h : h + 1, :]) / pixels[0]
            low[at, half(h)] = ((valid * gain * scale) * (dn - away)).astype(bf16)
        send(at.start // BLOCK)
        return carry

    row_blocks(rows, BLOCK, body, 0)
    finish()


def grad_two(meta, c, x, coefs, coefs1, heads, pixels):
    rows, width = c.shape
    return pl.pallas_call(
        functools.partial(grad_two_kernel, len(x)),
        in_specs=[SM, HB] + [VM] * (3 + len(x)) + [SM],
        out_specs=(VM, HB),
        out_shape=(vmem_out((rows, width), bf16), hbm_out((rows, width), f32)),
        scratch_shapes=stream_scratch(rows, width, BLOCK) * 2,
        compiler_params=params(16),
        cost_estimate=cost(30 * rows * width, 12 * rows * width),
        name="grad_two",
    )(meta, away(c), *[held(v) for v in x], held(coefs), held(coefs1), held(heads), pixels)


def grad_one_kernel(meta, c_source, dn_source, got, weight, coefs, pixels, low, sums, c, c_sems, dn, dn_sems):
    rows, width = c.shape
    valid = meta[3].astype(f32)
    wait_c = stream_in(c_source, c, c_sems, BLOCK)
    wait_dn = stream_in(dn_source, dn, dn_sems, BLOCK)
    sums[...] = weighted(got, weight)

    def body(at, carry):
        wait_c(at.start // BLOCK)
        wait_dn(at.start // BLOCK)
        for h in range(width // LANES):
            mean, scale = coefs[h : h + 1, :], coefs[2 + h : 3 + h, :]
            hat = (c[at, half(h)] - mean) * scale
            away = (sums[2 + h : 3 + h, :] + hat * sums[h : h + 1, :]) / pixels[0]
            low[at, half(h)] = ((valid * coefs[4 + h : 5 + h, :] * scale) * (dn[at, half(h)] - away)).astype(bf16)
        return carry

    row_blocks(rows, BLOCK, body, 0)


def grad_one(meta, c, dn, got, weight, coefs, pixels):
    rows, width = c.shape
    return pl.pallas_call(
        grad_one_kernel,
        in_specs=[SM, HB, HB] + [VM] * 3 + [SM],
        out_specs=(VM, VM),
        out_shape=(vmem_out((rows, width), bf16), vmem_out((ROWS, LANES), f32)),
        scratch_shapes=stream_scratch(rows, width, BLOCK) * 2,
        compiler_params=params(16),
        cost_estimate=cost(10 * rows * width, 10 * rows * width),
        name="grad_one",
    )(meta, away(c), away(dn), held(got), weight, held(coefs), pixels)


def back_setup(gs, scratch, copies, rows, width):
    clear_ends(scratch, rows)
    place_columns(scratch, [(g, slice(0, width), i * width) for i, g in enumerate(gs)], SIDE)
    for c in copies:
        c.wait()


def back_products(scratch, w, at, chunk):
    total = None
    for dx in (0, 1, -1):
        acc = None
        for dy in (-1, 0, 1):
            lhs = scratch[pl.ds(pl.multiple_of(at + SIDE * (1 - dy), SIDE), chunk), :]
            term = jnp.dot(lhs, w[3 * (dy + 1) + dx + 1], preferred_element_type=f32)
            acc = term if acc is None else acc + term
        acc = moved(acc, -dx)
        total = acc if total is None else total + acc
    return total


def back_two_kernel(n_parts, n_pieces, meta, *refs):
    pieces, gs, refs = refs[:n_pieces], refs[n_pieces : n_pieces + n_parts], refs[n_pieces + n_parts :]
    source, coefs, target, stats, scratch, w, sems, c, c_sems, out, out_sems = refs
    rows, width = out.shape
    halves = width // LANES
    chunk = CHUNK
    push, finish = stream_out(out, target, out_sems, chunk)
    copies = backward_copies(meta, pieces, w, width // 2, n_parts, sems)
    for copy in copies:
        copy.start()
    wait = stream_in(source, c, c_sems, chunk)
    back_setup(gs, scratch, copies, rows, width)

    def step(j, carry):
        at = pl.multiple_of(j * chunk, chunk)
        acc = back_products(scratch, w, at, chunk)
        wait(j)
        sums = []
        for h in range(halves):
            hat = (c[pl.ds(at, chunk), half(h)] - coefs[h : h + 1, :]) * coefs[2 + h : 3 + h, :]
            dn = acc[:, half(h)] * silu_slope(hat * coefs[4 + h : 5 + h, :] + coefs[6 + h : 7 + h, :])
            out[pl.ds(at, chunk), half(h)] = dn
            sums.append(carry[2 * h] + jnp.sum(dn * hat, axis=0, keepdims=True))
            sums.append(carry[2 * h + 1] + jnp.sum(dn, axis=0, keepdims=True))
        push(j)
        return tuple(sums)

    zero = jnp.zeros((1, LANES), f32)
    sums = lax.fori_loop(0, rows // chunk, step, (zero,) * (2 * halves))
    send_rows(stats, [(2 * i + h, sums[2 * h + i]) for h in range(halves) for i in range(2)])
    finish()


def back_scratch(rows, width, n):
    return [
        pltpu.VMEM((rows + 2 * SIDE, n * width), bf16),
        pltpu.VMEM((9, n * width, width), bf16),
        pltpu.SemaphoreType.DMA((10 * n,)),
    ]


def back_two(meta, pieces, g_parts, c, coefs, n_devices):
    rows, width = c.shape
    n = len(g_parts)
    return pl.pallas_call(
        functools.partial(back_two_kernel, n, len(pieces)),
        in_specs=[SM] + [HB] * len(pieces) + [VM] * n + [HB, VM],
        out_specs=(HB, VM),
        out_shape=(hbm_out((rows, width), f32), vmem_out((n_devices, ROWS, LANES), f32)),
        scratch_shapes=back_scratch(rows, width, n) + stream_scratch(rows, width, CHUNK) * 2,
        compiler_params=params(28),
        cost_estimate=cost(2 * 9 * rows * width * width * n, 16 << 20),
        name="back_two",
    )(meta, *[away(v) for v in pieces], *[held(v) for v in g_parts], away(c), held(coefs))


def back_one_kernel(n_parts, n_pieces, meta, *refs):
    pieces, gs, refs = refs[:n_pieces], refs[n_pieces : n_pieces + n_parts], refs[n_pieces + n_parts :]
    source, out, send, scratch, w, sems, keep, keep_sems, summed, in_sems = refs
    rows, width = summed.shape
    cs = width // 2
    chunk = CHUNK
    g = meta[1]
    copies = backward_copies(meta, pieces, w, cs, n_parts, sems)
    for c in copies:
        c.start()
    wait = stream_in(source, summed, in_sems, chunk)
    first = g == 0
    back_setup(gs, scratch, copies, rows, width)

    def copy(j):
        cols = pl.ds(pl.multiple_of(j * chunk, chunk), chunk)
        return pltpu.make_async_copy(keep.at[:, cols], out.at[g, :, cols], keep_sems.at[j])

    def step(j, carry):
        at = pl.multiple_of(j * chunk, chunk)
        acc = back_products(scratch, w, at, chunk)
        wait(j)
        acc = acc + summed[pl.ds(at, chunk), :]
        a, b = acc[:, :cs], acc[:, cs:]
        keep[:, pl.ds(at, chunk)] = jnp.where(first, a, b).T
        copy(j).start()
        send[:, pl.ds(at, chunk)] = jnp.where(first, b, a).T.astype(bf16)
        return carry

    lax.fori_loop(0, rows // chunk, step, 0)
    for j in range(rows // chunk):
        copy(j).wait()


def back_one(meta, pieces, g_parts, summed):
    rows, width = summed.shape
    n = len(g_parts)
    cs = width // 2
    return pl.pallas_call(
        functools.partial(back_one_kernel, n, len(pieces)),
        in_specs=[SM] + [HB] * len(pieces) + [VM] * n + [HB],
        out_specs=(HB, VM),
        out_shape=(hbm_out((2, cs, rows), f32), vmem_out((cs, rows), bf16)),
        scratch_shapes=back_scratch(rows, width, n)
        + [pltpu.VMEM((cs, rows), f32), pltpu.SemaphoreType.DMA((rows // CHUNK,))]
        + stream_scratch(rows, width, CHUNK),
        compiler_params=params(28),
        cost_estimate=cost(2 * 9 * rows * width * width * n, 16 << 20),
        name="back_one",
    )(meta, *[away(v) for v in pieces], *[held(v) for v in g_parts], away(summed))


def weight_kernel(sizes, n_parts, taps, meta, g, *refs):
    n = sum(sizes)
    xs, (keep_out, send_out, shifted, x, keep, send, sems) = refs[:n], refs[n:]
    rows, width = g.shape
    cs = width // 2
    first = meta[1] == 0
    parts, at = [], 0
    for size in sizes:
        parts.append(xs[at : at + size])
        at += size
    place_columns(x, column_plan(meta, parts, n_parts, cs), 0)
    moves = sorted({1 - k % 3 for k in taps})
    for i in range(len(moves)):
        clear_ends(shifted.at[i], rows)

    def shift(at, carry):
        low = g[at, :]
        value = low.astype(f32)
        to = pl.ds(pl.multiple_of(at.start + SIDE, SIDE), at.size)
        for i, e in enumerate(moves):
            shifted[i, to, :] = moved(value, e).astype(bf16) if e else low
        return carry

    row_blocks(rows, BLOCK, shift, 0)

    def copies(j):
        pairs = ((send, send_out), (keep, keep_out))
        return [pltpu.make_async_copy(v.at[j], to.at[j], sems.at[i, j]) for i, (v, to) in enumerate(pairs)]

    for j, k in enumerate(taps):
        lo = SIDE * (2 - k // 3)
        lhs = shifted[moves.index(1 - k % 3), lo : lo + rows, :]
        term = lax.dot_general(lhs, x[...], (((0,), (0,)), ((), ())), preferred_element_type=f32)
        a, b = term[:cs], term[cs:]
        keep[j] = jnp.where(first, a, b)
        send[j] = jnp.where(first, b, a).astype(bf16)
        for c in copies(j):
            c.start()
    for j in range(len(taps)):
        for c in copies(j):
            c.wait()


def weight_grad(meta, g, parts, n_parts, taps):
    rows, width = g.shape
    flat = [v for p in parts for v in p]
    columns = n_parts * width
    shape = (len(taps), width // 2, columns)
    return pl.pallas_call(
        functools.partial(weight_kernel, [len(p) for p in parts], n_parts, taps),
        in_specs=[SM] + [VM] * (len(flat) + 1),
        out_specs=(HB, HB),
        out_shape=(hbm_out(shape, f32), hbm_out(shape, bf16)),
        scratch_shapes=[
            pltpu.VMEM((len({k % 3 for k in taps}), rows + 2 * SIDE, width), bf16),
            pltpu.VMEM((rows, columns), bf16),
            pltpu.VMEM(shape, f32),
            pltpu.VMEM(shape, bf16),
            pltpu.SemaphoreType.DMA((2, len(taps))),
        ],
        compiler_params=params(28),
        cost_estimate=cost(2 * len(taps) * rows * width * columns, 16 << 20),
        name="weight_grad",
    )(meta, held(g), *[held(v) for v in flat])


def swap(values, axis, by):
    n = lax.axis_size(axis)
    return lax.ppermute(values, axis, [(i, i ^ by) for i in range(n)])


def xor_order(values, r):
    bit = 1
    while bit < len(values):
        flip = (r & bit) != 0
        values = [jnp.where(flip, values[i ^ bit], v) for i, v in enumerate(values)]
        bit *= 2
    return values


def gate(values, *others):
    return lax.optimization_barrier((values, *others))[0]


def scatter_split(total, stage, kind):
    stride, size = stage
    k = (lax.axis_index("batch") // stride) % size
    split = total.reshape(size, -1, total.shape[1])
    mine = lax.dynamic_index_in_dim(split, k, keepdims=False)
    return mine, [lax.dynamic_index_in_dim(split, k ^ j, keepdims=False).astype(kind) for j in range(1, size)]


def scatter_move(sent, stage):
    return [swap(v, "batch", stage[0] * j) for j, v in enumerate(sent, 1)]


def scatter_add(mine, got, *after):
    for v in got:
        mine = mine + gate(v, *after).astype(f32)
    return mine


def gather_move(out, stage):
    return [swap(out, "batch", stage[0] * j) for j in range(1, stage[1])]


def gather_join(out, got, stage, *after):
    k = (lax.axis_index("batch") // stage[0]) % stage[1]
    return jnp.concatenate(xor_order([out] + [gate(v, *after) for v in got], k), axis=0)


def on_device(
    images,
    conv1_weight,
    norm1_gain,
    norm1_bias,
    conv2_weight,
    norm2_gain,
    norm2_bias,
    head_weight,
    head_bias,
    labels,
    image_counts,
    average_weights,
):
    n_task, n_batch = lax.axis_size("task"), lax.axis_size("batch")
    t, b = lax.axis_index("task"), lax.axis_index("batch")
    slots, cs, pixels = images.shape
    n_parts = n_task // slots
    g, r = t // n_parts, t % n_parts
    first = g == 0
    width = slots * cs
    channels = n_task * cs
    n_devices = n_task * n_batch
    tasks_here = head_weight.shape[1]
    tasks = tasks_here * n_task

    valid_images = (jnp.arange(slots)[None, :] < image_counts[:, None]).astype(f32)
    image_total = jnp.sum(image_counts).astype(f32)
    pixel_total = (image_total * pixels).reshape(1)
    own_valid = (g < lax.dynamic_index_in_dim(image_counts, b, keepdims=False)).astype(jnp.int32)
    place = jnp.stack([b, g, r, 0 * b, b % 4]).astype(jnp.int32)
    meta = jnp.stack([b, g, r, own_valid, b % 4]).astype(jnp.int32)
    same = (jnp.arange(n_parts) == r).astype(f32)
    weight = (valid_images[:, :, None] * same[None, None, :]).reshape(n_devices, 1)
    weight = jnp.broadcast_to(weight[:, :, None], (n_devices, ROWS, LANES))

    def relative(w):
        blocks = [w[..., i * cs : (i + 1) * cs] for i in range(n_task)]
        order = [xor_order(blocks[s * n_parts : (s + 1) * n_parts], r) for s in range(slots)]
        return [jnp.concatenate([order[s][i] for s in range(slots)], axis=-1) for i in range(n_parts)]

    def ordered(own, other, axis):
        return jnp.concatenate([jnp.where(first, own, other), jnp.where(first, other, own)], axis=axis)

    def joined(pieces):
        other = jnp.concatenate(xor_order(list(pieces[1:]), b % 4 if len(pieces) > 2 else 0), axis=1)
        return relative(ordered(pieces[0], other, 1))

    def forward_pieces(pieces):
        return pieces if aligned(cs) else [jnp.concatenate(joined(pieces), axis=2)]

    def backward_pieces(pieces):
        if aligned(cs):
            return [swap(v, "task", i) if i else v for i in range(n_parts) for v in pieces]
        return [swap(v, "task", i) if i else v for i, v in enumerate(joined(pieces))]

    def all_parts(v):
        return [v] + [swap(v, "task", i) for i in range(1, n_parts)]

    near_sent = lax.dynamic_index_in_dim(
        conv1_weight.reshape(9, 4, cs // 4, channels), b % 4, axis=1, keepdims=False
    )
    near = swap(near_sent, "task", n_parts)

    head_bias, head_weight = gate(head_bias, near_sent), gate(head_weight, near_sent)
    lines = jnp.pad(head_bias, (0, channels - tasks_here)).reshape(1, channels)
    mine = jnp.concatenate([head_weight.T.astype(f32), lines])
    mine = jnp.pad(mine, ((0, -mine.shape[0] % ROWS), (0, 0)))
    every = xor_order([mine] + [swap(mine, "task", i) for i in range(1, n_task)], t)
    table = jnp.concatenate([v[:tasks_here] for v in every])
    table = table.reshape(tasks, slots, n_parts, cs).swapaxes(1, 2).reshape(tasks, channels)
    bias_row = jnp.concatenate([v[tasks_here, :tasks_here] for v in every]).reshape(1, tasks)
    vecs = jnp.stack([norm1_gain, norm1_bias, norm2_gain, norm2_bias])
    vecs = jnp.pad(vecs, ((4, 0), (0, LANES - cs)))
    label_rows = lax.dynamic_update_slice(
        jnp.zeros((slots, LANES), f32), labels.astype(f32), (0, t * tasks_here)
    )
    columns = [label_rows, vecs, valid_images.reshape(-1, 1), average_weights.reshape(-1, 1)]

    x_own, x_send = turn(place, images)
    near = gate(near, x_send)
    x_other = swap(gate(x_send, near), "task", n_parts)
    side = swap(near, "batch", 1)
    w1 = [conv1_weight, near, side, swap(near, "batch", 2), swap(side, "batch", 2)]
    w2 = [conv2_weight, swap(gate(conv2_weight, near), "task", n_parts)]
    if aligned(cs):
        x_parts = list(zip(all_parts(x_own), all_parts(gate(x_other, *w1, table, bias_row, weight, *columns))))
    else:
        x_parts = [[v] for v in all_parts(ordered(x_own, x_other, 1))]

    def exchange(rows):
        flat_rows = rows.reshape(n_devices * ROWS, LANES)
        return lax.all_to_all(flat_rows, ("batch", "task"), 0, 0, tiled=True).reshape(rows.shape)

    c1, stats = conv_stats(meta, vecs, forward_pieces(w1), x_parts, cs, n_devices, 0)
    a_own, coefs1 = activate(meta, c1, exchange(gate(stats, w2[1])), weight, n_parts)
    a_parts = [[v] for v in all_parts(a_own)]
    c2, stats = conv_stats(meta, vecs, forward_pieces(w2), a_parts, cs, n_devices, 18)
    sums, coefs2 = pool(meta, c2, x_parts[0], exchange(stats), weight, coefs1, label_rows)
    heads, task_weights, average_next, head_grad, bias_grad, pooled_rows = head(
        meta,
        exchange(sums),
        table,
        bias_row,
        columns[2],
        average_weights.reshape(1, -1),
        columns[3],
        n_parts,
    )

    def both_groups(keep, got, *after):
        return (keep + gate(got, *after).astype(f32)).reshape(-1, channels)

    def assemble(done, taps):
        where = {k: (v, j) for v, ks in zip(done, taps) for j, k in enumerate(ks)}
        out = jnp.concatenate([where[k][0][where[k][1] * cs : (where[k][1] + 1) * cs] for k in range(9)])
        out = out.reshape(9, cs, channels)
        if not aligned(cs):
            parts = [out[:, :, i * width : (i + 1) * width] for i in range(n_parts)]
            order = [v for s in range(slots) for v in xor_order([p[:, :, s * cs : (s + 1) * cs] for p in parts], r)]
            out = jnp.concatenate(order, axis=2)
        return out.astype(f32)

    bits = n_batch.bit_length() - 1
    near = 1 << (bits // 2)
    one, two = (1, near), (near, n_batch // near)
    every_tap, taps_a, taps_b = tuple(range(9)), (0, 3, 6, 1), (4, 7, 2, 5, 8)
    low2, summed = grad_two(meta, c2, x_parts[0], coefs2, coefs1, heads, pixel_total)
    low2_parts = all_parts(low2)
    keep2, send2 = weight_grad(meta, low2, a_parts, n_parts, every_tap)
    got2 = swap(send2, "task", n_parts)
    low2_parts[0] = gate(low2_parts[0], keep2)
    dn1, stats = back_two(meta, backward_pieces(w2), low2_parts, c1, coefs1, n_devices)
    low1, sums1 = grad_one(meta, c1, dn1, exchange(stats), weight, coefs1, pixel_total)
    low1_parts = all_parts(low1)

    mine2, sent2 = scatter_split(both_groups(keep2, got2, low1), one, bf16)
    got2 = scatter_move(sent2, one)
    keep_a, send_a = weight_grad(meta, gate(low1, *sent2), x_parts, n_parts, taps_a)
    got_a = swap(send_a, "task", n_parts)
    keep_b, send_b = weight_grad(meta, gate(low1, keep_a), x_parts, n_parts, taps_b)
    got_b = swap(send_b, "task", n_parts)
    mine2, sent2 = scatter_split(scatter_add(mine2, got2, keep_b), two, f32)
    got2 = scatter_move(sent2, two)
    low1_parts[0] = gate(low1_parts[0], *sent2)
    half_done, send = back_one(meta, backward_pieces(w1), low1_parts, summed)
    got = swap(send, "task", n_parts)
    mine_a, sent_a = scatter_split(both_groups(keep_a, got_a, send), one, bf16)
    got_a = scatter_move(sent_a, one)
    mine_b, sent_b = scatter_split(both_groups(keep_b, got_b, *sent_a), one, bf16)
    got_b = scatter_move(sent_b, one)
    sum2 = scatter_add(mine2, got2, *sent_b).astype(bf16)
    got2 = gather_move(sum2, two)
    mine_a, sent_a = scatter_split(scatter_add(mine_a, got_a, sum2), two, bf16)
    got_a = scatter_move(sent_a, two)
    mine_b, sent_b = scatter_split(scatter_add(mine_b, got_b, *sent_a), two, bf16)
    got_b = scatter_move(sent_b, two)
    sum2 = gather_join(sum2, got2, two, *sent_b)
    got2 = gather_move(sum2, one)
    sum_a = scatter_add(mine_a, got_a, sum2).astype(bf16)
    got_a = gather_move(sum_a, two)
    sum_b = scatter_add(mine_b, got_b, sum_a).astype(bf16)
    got_b = gather_move(sum_b, two)
    sum_a = gather_join(sum_a, got_a, two, sum_b, got)
    got_a = gather_move(sum_a, one)
    sum_b = gather_join(sum_b, got_b, two, sum_a)
    got_b = gather_move(sum_b, one)
    input_grad = join(meta, gate(got, sum_b), half_done)
    conv2_grad = assemble([gather_join(sum2, got2, one, input_grad)], [every_tap])
    sum_a = gather_join(sum_a, got_a, one, conv2_grad)
    sum_b = gather_join(sum_b, got_b, one, sum_a)
    conv1_grad = assemble([sum_a, sum_b], [taps_a, taps_b])

    def own_slice(rows, at):
        line = rows[at : at + 2].reshape(-1)
        return lax.dynamic_slice_in_dim(line, g * cs, cs)

    head_weight_grad = lax.dynamic_slice_in_dim(head_grad, t * tasks_here, tasks_here, axis=0)
    head_weight_grad = head_weight_grad.reshape(tasks_here, n_parts, slots, cs).swapaxes(1, 2)
    head_weight_grad = head_weight_grad.reshape(tasks_here, channels).T
    head_bias_grad = lax.dynamic_slice_in_dim(bias_grad[0], t * tasks_here, tasks_here)
    pooled = lax.dynamic_slice_in_dim(pooled_rows, g * cs, cs, axis=1)
    return (
        pooled,
        input_grad,
        conv1_grad,
        own_slice(sums1, 0),
        own_slice(sums1, 2),
        conv2_grad,
        own_slice(heads, 0),
        own_slice(heads, 2),
        head_weight_grad,
        head_bias_grad,
        task_weights[0],
        average_next[0],
    )


def solution(mesh):
    in_specs = (
        P("batch", "task", None),
        P(None, "task", None),
        P("task"),
        P("task"),
        P(None, "task", None),
        P("task"),
        P("task"),
        P(None, "task"),
        P("task"),
        P("batch", "task"),
        P(),
        P(),
    )
    out_specs = (
        P("batch", "task"),
        P("batch", "task", None),
        P(None, "task", None),
        P("task"),
        P("task"),
        P(None, "task", None),
        P("task"),
        P("task"),
        P(None, "task"),
        P("task"),
        P(),
        P(),
    )
    return jax.shard_map(
        on_device, mesh=mesh, in_specs=in_specs, out_specs=out_specs, check_vma=False
    )
```

time: 551 us -> 310 us (0.56); the launches traced: 542 us -> 309 us
  waiting for transfers between devices: 208 us -> 74.7 us
  local copies, waits for them, and re-layouts: 89.6 us -> 17.4 us
  starting transfers between devices: 24.2 us -> 54.8 us
  other arithmetic: 36.8 us -> 8.94 us
  blocking collectives: 48.9 us -> 23 us
  between operations: 16.3 us -> 2.76 us
  Pallas kernels: 118 us -> 128 us
    psum x1 -> x0, waiting for transfers between devices: 123 us -> none  [settle(): total = lax.psum(keep + swap(send, 'task', n_parts).astype(f32), 'batch')]
    all_gather x1 -> x0, blocking collectives: 48.9 us -> none  [on_device(): gathered = lax.all_gather(mine, 'task', axis=0)]
    ppermute x12 -> x49, starting transfers between devices: 9.73 us -> 49 us  [swap(): return lax.ppermute(values, axis, [(i, i ^ by) for i in range(n)])]
    reshape x11 -> x3, local copies, waits for them, and re-layouts: 27.5 us -> 0.79 us  [on_device(): table.reshape(tasks, slots, n_parts, cs).swapaxes(1, 2)]
    all_to_all x0 -> x2, blocking collectives: none -> 23 us  [exchange(): lax.all_to_all(flat_rows, ('batch', 'task'), 0, 0, tiled=True)]
    unnamed x69 -> x61, local copies, waits for them, and re-layouts: 29 us -> 6.98 us
    another operation x4 -> x2, local copies, waits for them, and re-layouts: 20.8 us -> 0.17 us  [the longest x1 0.09 us: on_device(): meta = jnp.stack([b, g, r, own_valid, b % 4]).astype(jnp.int32)]
    select_n x5 -> x7, other arithmetic: 13.8 us -> 0.58 us  [xor_order(): values = [jnp.where(flip, values[i ^ bit], v) for i, v in enumerate(values)]]
  transfers between devices with their start and end apart: 17 -> 51, of which waited for: 9 -> 19; matrix products, arithmetic and copies ran while one was open for 14% -> 5% of each run, Pallas kernels for 9% -> 29%
where the time goes in v3:
time: 310 us; the launch traced here: 309 us
  Pallas kernels  128 us (41%)
  waiting for transfers between devices  74.7 us (24%)
  starting transfers between devices  54.8 us (18%)
  blocking collectives  23 us (7%)
  local copies, waits for them, and re-layouts  17.4 us (6%)
  other arithmetic  8.94 us (3%)
    ppermute x49, waiting for transfers between devices, swap(): return lax.ppermute(values, axis, [(i, i ^ by) for i in range(n)])  63.1 us
    ppermute x49, starting transfers between devices, swap(): return lax.ppermute(values, axis, [(i, i ^ by) for i in range(n)])  49 us
    pallas_call x3, Pallas kernels, weight_grad(): pl.pallas_call(functools.partial(weight_kernel, [len(p) for p in parts],...  31.5 us
    pallas_call x2, Pallas kernels, conv_stats(): pl.pallas_call(functools.partial(conv_kernel, [len(p) for p in parts], le...  30.2 us
    all_to_all x2, blocking collectives, exchange(): lax.all_to_all(flat_rows, ('batch', 'task'), 0, 0, tiled=True)  23 us
    pallas_call x1, Pallas kernels, back_two(): pl.pallas_call(functools.partial(back_two_kernel, n, len(pieces)), in_spe...  18.6 us
    pallas_call x1, Pallas kernels, back_one(): pl.pallas_call(functools.partial(back_one_kernel, n, len(pieces)), in_spe...  14.7 us
    all_to_all x2, waiting for transfers between devices, exchange(): lax.all_to_all(flat_rows, ('batch', 'task'), 0, 0, tiled=True)  11.6 us
  transfers between devices with their start and end apart: 51, of which 19 were waited for; matrix products, arithmetic and copies ran while one was open for 5% of the time, Pallas kernels for 29%

profile of v3, /device:TPU:0, one launch (start us, length us, event | category | flops | bytes accessed | tf_op | source)
XLA Modules:
  0.0 309.1 jit_solution(4906204491573165125)
XLA Ops:
  8.1 3.4 %turn.1 = (bf16[4096,128]{1,0:T(8,128)(2,1)S(1)}, bf16[4096,128]{1,0:T(8,128)(2,1)}) custom-call(s32[5]{0:T(128)S(1)} %stack.55.meta, bf16[2,128,4096]{2,1,0:T(8,128)(2,1)} %images.1), custom_call_target="tpu_custom_call" | custom-call | flops 1048576 | bytes 4194304 | tf_op jit(solution)/shard_map/turn/pallas_call | solution.py:360
  11.7 4.2 %collective-permute-done.refs_1_ = bf16[9,32,512]{2,1,0:T(8,128)(2,1)S(1)} collective-permute-done((bf16[9,32,512]{2,1,0:T(8,128)(2,1)S(1)}, bf16[9,32,512]{2,1,0:T(8,128)(2,1)S(1)}, u32[]{:S(2)}, u32[]{:S(2)}) %collective-permute-start) | collective-permute-done | bytes 294944 | tf_op jit(solution)/shard_map/ppermute | solution.py:816
  21.5 5.1 %collective-permute-done.2.refs_2_ = bf16[9,32,512]{2,1,0:T(8,128)(2,1)} collective-permute-done((bf16[9,32,512]{2,1,0:T(8,128)(2,1)}, bf16[9,32,512]{2,1,0:T(8,128)(2,1)}, u32[]{:S(2)}, u32[]{:S(2)}) %collective-permute-start.2) | collective-permute-done | bytes 294944 | tf_op jit(solution)/shard_map/ppermute | solution.py:816
  30.9 3.4 %collective-permute-done.4.refs_4_ = bf16[9,32,512]{2,1,0:T(8,128)(2,1)} collective-permute-done((bf16[9,32,512]{2,1,0:T(8,128)(2,1)}, bf16[9,32,512]{2,1,0:T(8,128)(2,1)}, u32[]{:S(2)}, u32[]{:S(2)}) %collective-permute-start.4) | collective-permute-done | bytes 294944 | tf_op jit(solution)/shard_map/ppermute | solution.py:816
  34.3 8.6 %collective-permute-done.5.refs_6_.refs_1_ = bf16[4096,128]{1,0:T(8,128)(2,1)S(1)} collective-permute-done((bf16[4096,128]{1,0:T(8,128)(2,1)}, bf16[4096,128]{1,0:T(8,128)(2,1)S(1)}, u32[]{:S(2)}, u32[]{:S(2)}) %collective-permute-start.5) | collective-permute-done | bytes 1048608 | tf_op jit(solution)/shard_map/ppermute | solution.py:816
  45.8 15.3 %conv_stats.2 = (f32[4096,256]{1,0:T(8,128)}, f32[32,8,128]{2,1,0:T(8,128)S(1)}) custom-call(s32[5]{0:T(128)S(1)} %stack.49.meta, f32[8,128]{1,0:T(8,128)S(1)} %select_maximum_fusion.1.extra, bf16[9,128,512]{2,1,0:T(8,128)(2,1)} %refs_0_.7, bf16[9,32,512]{2,1,0:T(8,128)(2,1)} %copy-done.13, bf16[9,32,512]{2,1,0:T(8,128)(2,1)} %collective-permute-done.2.refs_2_, ...), custom_call_target="tpu_custom_call" | custom-call | tf_op jit(solution)/shard_map/conv_stats/pallas_call | solution.py:277
  61.2 5.9 %collective-permute-done.1.refs_1_ = bf16[9,128,512]{2,1,0:T(8,128)(2,1)} collective-permute-done((bf16[9,128,512]{2,1,0:T(8,128)(2,1)}, bf16[9,128,512]{2,1,0:T(8,128)(2,1)}, u32[]{:S(2)}, u32[]{:S(2)}) %collective-permute-start.1) | collective-permute-done | bytes 1179680 | tf_op jit(solution)/shard_map/ppermute | solution.py:816
  67.1 13.0 %all_to_all.24.got = f32[32,8,128]{2,1,0:T(8,128)S(1)} all-to-all(f32[32,8,128]{2,1,0:T(8,128)S(1)} %get-tuple-element.90), channel_id=1, replica_groups=mesh['batch'=8,'task'=4] {'batch','task'}, dimensions={0} | all-to-all | bytes 262144 | tf_op jit(solution)/shard_map/all_to_all | solution.py:951
  80.1 3.3 %activate.1 = (bf16[4096,256]{1,0:T(8,128)(2,1)S(1)}, f32[16,128]{1,0:T(8,128)S(1)}) custom-call(s32[5]{0:T(128)S(1)} %stack.49.meta, f32[4096,256]{1,0:T(8,128)} %get-tuple-element.88.source.refs_6_.c_source, f32[32,8,128]{2,1,0:T(8,128)S(1)} %all_to_all.24.got, f32[32,8,128]{2,1,0:T(8,128)S(1)} %broadcast_in_dim.4.weight.refs_3_), custom_call_target="tpu_custom_call" | custom-call | flops 20971520 | bytes 6291456 | tf_op jit(solution)/shard_map/activate/pallas_call | solution.py:321
  83.7 3.9 %collective-permute-done.11.refs_3_.refs_1_ = bf16[4096,256]{1,0:T(8,128)(2,1)S(1)} collective-permute-done((bf16[4096,256]{1,0:T(8,128)(2,1)S(1)}, bf16[4096,256]{1,0:T(8,128)(2,1)S(1)}, u32[]{:S(2)}, u32[]{:S(2)}) %collective-permute-start.11) | collective-permute-done | bytes 2097184 | tf_op jit(solution)/shard_map/ppermute | solution.py:816
  87.6 14.9 %conv_stats.3 = (f32[4096,256]{1,0:T(8,128)}, f32[32,8,128]{2,1,0:T(8,128)S(1)}) custom-call(s32[5]{0:T(128)S(1)} %stack.49.meta, f32[8,128]{1,0:T(8,128)S(1)} %select_maximum_fusion.1.extra, bf16[9,128,512]{2,1,0:T(8,128)(2,1)} %refs_0_.6, bf16[9,128,512]{2,1,0:T(8,128)(2,1)} %collective-permute-done.1.refs_1_, ...), custom_call_target="tpu_custom_call" | custom-call | flops 9663676416 | bytes 18874368 | tf_op jit(solution)/shard_map/conv_stats/pallas_call | solution.py:277
  102.5 10.0 %all_to_all.25.refs_2_ = f32[32,8,128]{2,1,0:T(8,128)S(1)} all-to-all(f32[32,8,128]{2,1,0:T(8,128)S(1)} %get-tuple-element.93), channel_id=1, replica_groups=mesh['batch'=8,'task'=4] {'batch','task'}, dimensions={0} | all-to-all | bytes 262144 | tf_op jit(solution)/shard_map/all_to_all | solution.py:951
  112.5 6.1 %pool.1 = (f32[32,8,128]{2,1,0:T(8,128)}, f32[8,128]{1,0:T(8,128)S(1)}) custom-call(s32[5]{0:T(128)S(1)} %stack.49.meta, f32[4096,256]{1,0:T(8,128)} %get-tuple-element.92.source, bf16[4096,128]{1,0:T(8,128)(2,1)S(1)} %get-tuple-element.83.refs_5_.refs_0_, bf16[4096,128]{1,0:T(8,128)(2,1)S(1)} %collective-permute-done.5.refs_6_.refs_1_, ...), custom_call_target="tpu_custom_call" | custom-call | flops 31457280 | bytes 6291456 | tf_op jit(solution)/shard_map/pool/pallas_call | solution.py:441
  118.7 2.8 all-to-all-start.2
  124.1 5.4 %all-to-all-done.2.got = f32[32,8,128]{2,1,0:T(8,128)S(1)} async-done(((f32[32,8,128]{2,1,0:T(8,128)}), f32[32,8,128]{2,1,0:T(8,128)S(1)}, u32[]{:S(2)}, u32[]{:S(2)}) %all-to-all-start.2) | async-done | bytes 131104 | tf_op jit(solution)/shard_map/all_to_all | solution.py:951
  130.2 6.4 %head.1 = (f32[8,128]{1,0:T(8,128)}, f32[1,40]{1,0:T(1,128)}, f32[1,40]{1,0:T(1,128)}, f32[40,512]{1,0:T(8,128)}, f32[1,40]{1,0:T(1,128)}, /*index=5*/f32[2,256]{1,0:T(2,128)}) custom-call(s32[5]{0:T(128)} %copy-done, f32[32,8,128]{2,1,0:T(8,128)} %copy-done.12, f32[40,512]{1,0:T(8,128)} %reshape.187.ht, f32[1,40]{1,0:T(1,128)} %maximum_bitcast_fusion.bias, ...), custom_call_target="tpu_custom_call" | custom-call | flops 1048576 | bytes 1048576 | tf_op jit(solution)/shard_map/head/pallas_call | solution.py:526
  137.9 7.1 %grad_two.1 = (bf16[4096,256]{1,0:T(8,128)(2,1)}, f32[4096,256]{1,0:T(8,128)}) custom-call(s32[5]{0:T(128)S(1)} %copy-done.1, f32[4096,256]{1,0:T(8,128)} %get-tuple-element.92.source, bf16[4096,128]{1,0:T(8,128)(2,1)S(1)} %get-tuple-element.83.refs_5_.refs_0_, bf16[4096,128]{1,0:T(8,128)(2,1)S(1)} %collective-permute-done.5.refs_6_.refs_1_, ...), custom_call_target="tpu_custom_call" | custom-call | flops 31457280 | bytes 12582912 | tf_op jit(solution)/shard_map/grad_two/pallas_call | solution.py:574
  149.5 14.4 %weight_grad.3 = (f32[9,128,512]{2,1,0:T(8,128)}, bf16[9,128,512]{2,1,0:T(8,128)(2,1)}) custom-call(s32[5]{0:T(128)S(1)} %copy-done.1, bf16[4096,256]{1,0:T(8,128)(2,1)} %get-tuple-element.101.g.refs_4_, bf16[4096,256]{1,0:T(8,128)(2,1)S(1)} %copy-done.6, bf16[4096,256]{1,0:T(8,128)(2,1)S(1)} %copy-done.8), custom_call_target="tpu_custom_call" | custom-call | flops 9663676416 | bytes 16777216 | tf_op jit(solution)/shard_map/weight_grad/pallas_call | solution.py:796
  166.2 18.6 %back_two.1 = (f32[4096,256]{1,0:T(8,128)}, f32[32,8,128]{2,1,0:T(8,128)}) custom-call(s32[5]{0:T(128)S(1)} %copy-done.1, bf16[9,128,512]{2,1,0:T(8,128)(2,1)} %refs_0_.6, bf16[9,128,512]{2,1,0:T(8,128)(2,1)} %collective-permute-done.1.refs_1_, bf16[9,128,512]{2,1,0:T(8,128)(2,1)} %collective-permute-done.17.refs_2_, ...), custom_call_target="tpu_custom_call" | custom-call | flops 9663676416 | bytes 16777216 | tf_op jit(solution)/shard_map/back_two/pallas_call | solution.py:684
  184.8 3.0 all-to-all-start.3
  189.6 6.2 %all-to-all-done.3.got = f32[32,8,128]{2,1,0:T(8,128)S(1)} async-done(((f32[32,8,128]{2,1,0:T(8,128)}), f32[32,8,128]{2,1,0:T(8,128)S(1)}, u32[]{:S(2)}, u32[]{:S(2)}) %all-to-all-start.3) | async-done | bytes 131104 | tf_op jit(solution)/shard_map/all_to_all | solution.py:951
  195.8 4.4 %grad_one.1 = (bf16[4096,256]{1,0:T(8,128)(2,1)S(1)}, f32[8,128]{1,0:T(8,128)S(1)}) custom-call(s32[5]{0:T(128)S(1)} %copy-done.2, f32[4096,256]{1,0:T(8,128)} %get-tuple-element.88.source.refs_6_.c_source, f32[4096,256]{1,0:T(8,128)} %get-tuple-element.102.dn_source, f32[32,8,128]{2,1,0:T(8,128)S(1)} %all-to-all-done.3.got, ...), custom_call_target="tpu_custom_call" | custom-call | flops 10485760 | bytes 10485760 | tf_op jit(solution)/shard_map/grad_one/pallas_call | solution.py:608
  203.4 8.0 %weight_grad.4 = (f32[4,128,512]{2,1,0:T(8,128)}, bf16[4,128,512]{2,1,0:T(8,128)(2,1)}) custom-call(s32[5]{0:T(128)S(1)} %copy-done.2, bf16[4096,256]{1,0:T(8,128)(2,1)S(1)} %get-tuple-element.112.g.refs_10_, bf16[4096,128]{1,0:T(8,128)(2,1)S(1)} %get-tuple-element.83.refs_5_.refs_0_, bf16[4096,128]{1,0:T(8,128)(2,1)S(1)} %collective-permute-done.5.refs_6_.refs_1_, ...), custom_call_target="tpu_custom_call" | custom-call | flops 4294967296 | bytes 16777216 | tf_op jit(solution)/shard_map/weight_grad/pallas_call | solution.py:796
  212.6 9.1 %weight_grad.5 = (f32[5,128,512]{2,1,0:T(8,128)}, bf16[5,128,512]{2,1,0:T(8,128)(2,1)}) custom-call(s32[5]{0:T(128)S(1)} %copy-done.2, bf16[4096,256]{1,0:T(8,128)(2,1)S(1)} %get-tuple-element.112.g.refs_10_, bf16[4096,128]{1,0:T(8,128)(2,1)S(1)} %get-tuple-element.83.refs_5_.refs_0_, bf16[4096,128]{1,0:T(8,128)(2,1)S(1)} %collective-permute-done.5.refs_6_.refs_1_, ...), custom_call_target="tpu_custom_call" | custom-call | flops 5368709120 | bytes 16777216 | tf_op jit(solution)/shard_map/weight_grad/pallas_call | solution.py:796
  227.5 2.5 collective-permute-start.30
  230.0 14.7 %back_one.1 = (f32[2,128,4096]{2,1,0:T(8,128)}, bf16[128,4096]{1,0:T(8,128)(2,1)S(1)}) custom-call(s32[5]{0:T(128)S(1)} %copy-done.2, bf16[9,128,512]{2,1,0:T(8,128)(2,1)} %refs_0_.7, bf16[9,32,512]{2,1,0:T(8,128)(2,1)} %copy-done.13, bf16[9,32,512]{2,1,0:T(8,128)(2,1)} %collective-permute-done.2.refs_2_, ...), custom_call_target="tpu_custom_call" | custom-call | flops 9663676416 | bytes 16777216 | tf_op jit(solution)/shard_map/back_one/pallas_call | solution.py:734
  246.6 5.0 %collective-permute-done.24 = bf16[5,128,512]{2,1,0:T(8,128)(2,1)S(1)} collective-permute-done((bf16[5,128,512]{2,1,0:T(8,128)(2,1)S(1)}, bf16[5,128,512]{2,1,0:T(8,128)(2,1)S(1)}, u32[]{:S(2)}, u32[]{:S(2)}) %collective-permute-start.24) | collective-permute-done | bytes 655392 | tf_op jit(solution)/shard_map/ppermute | solution.py:816
  255.3 2.6 collective-permute-start.33
  263.0 6.7 %collective-permute-done.34 = bf16[144,512]{1,0:T(8,128)(2,1)S(1)} collective-permute-done((bf16[144,512]{1,0:T(8,128)(2,1)S(1)}, bf16[144,512]{1,0:T(8,128)(2,1)S(1)}, u32[]{:S(2)}, u32[]{:S(2)}) %collective-permute-start.34) | collective-permute-done | bytes 147488 | tf_op jit(solution)/shard_map/ppermute | solution.py:816
  279.4 4.3 %collective-permute-done.38 = bf16[80,512]{1,0:T(8,128)(2,1)S(1)} collective-permute-done((bf16[80,512]{1,0:T(8,128)(2,1)S(1)}, bf16[80,512]{1,0:T(8,128)(2,1)S(1)}, u32[]{:S(2)}, u32[]{:S(2)}) %collective-permute-start.38) | collective-permute-done | bytes 81952 | tf_op jit(solution)/shard_map/ppermute | solution.py:816
  292.9 3.1 %collective-permute-done.40 = bf16[80,512]{1,0:T(8,128)(2,1)S(1)} collective-permute-done((bf16[80,512]{1,0:T(8,128)(2,1)S(1)}, bf16[80,512]{1,0:T(8,128)(2,1)S(1)}, u32[]{:S(2)}, u32[]{:S(2)}) %collective-permute-start.40) | collective-permute-done | bytes 81952 | tf_op jit(solution)/shard_map/ppermute | solution.py:816
  303.8 3.4 %collective-permute-done.48 = bf16[320,512]{1,0:T(8,128)(2,1)S(1)} collective-permute-done((bf16[320,512]{1,0:T(8,128)(2,1)S(1)}, bf16[320,512]{1,0:T(8,128)(2,1)S(1)}, u32[]{:S(2)}, u32[]{:S(2)}) %collective-permute-start.48) | collective-permute-done | bytes 327712 | tf_op jit(solution)/shard_map/ppermute | solution.py:816
  (218 shorter events, 81.5 us)
Async XLA Ops:
  3.1 15.1 %collective-permute-start.6 = (f32[16,512]{1,0:T(8,128)S(1)}, f32[16,512]{1,0:T(8,128)S(1)}, u32[]{:S(2)}, u32[]{:S(2)}) collective-permute-start(f32[16,512]{1,0:T(8,128)S(1)} %select_maximum_fusion), channel_id=1, source_target_pairs={{0,3},{1,2},{2,1},{3,0},{4,7},{5,6},{6,5},{7,4},{8,11},{9,10},{10,... | collective-permute-start | bytes 98312 | tf_op jit(solution)/shard_map/ppermute | solution.py:816
  5.6 14.2 %collective-permute-start.7 = (f32[16,512]{1,0:T(8,128)S(1)}, f32[16,512]{1,0:T(8,128)S(1)}, u32[]{:S(2)}, u32[]{:S(2)}) collective-permute-start(f32[16,512]{1,0:T(8,128)S(1)} %select_maximum_fusion), channel_id=1, source_target_pairs={{0,2},{1,3},{2,0},{3,1},{4,6},{5,7},{6,4},{7,5},{8,10},{9,11},{10,... | collective-permute-start | bytes 98312 | tf_op jit(solution)/shard_map/ppermute | solution.py:816
  6.3 13.6 %collective-permute-start.8 = (f32[16,512]{1,0:T(8,128)S(1)}, f32[16,512]{1,0:T(8,128)S(1)}, u32[]{:S(2)}, u32[]{:S(2)}) collective-permute-start(f32[16,512]{1,0:T(8,128)S(1)} %select_maximum_fusion), channel_id=1, source_target_pairs={{0,1},{1,0},{2,3},{3,2},{4,5},{5,4},{6,7},{7,6},{8,9},{9,8},{10,11... | collective-permute-start | bytes 98312 | tf_op jit(solution)/shard_map/ppermute | solution.py:816
  11.6 32.8 %collective-permute-start.9 = (bf16[4096,128]{1,0:T(8,128)(2,1)S(1)}, bf16[4096,128]{1,0:T(8,128)(2,1)S(1)}, u32[]{:S(2)}, u32[]{:S(2)}) collective-permute-start(bf16[4096,128]{1,0:T(8,128)(2,1)S(1)} %get-tuple-element.83.refs_5_.refs_0_), channel_id=1, source_target_pairs={{0,1},{1,0},{2,3},{3,2},{4,5},{5,4},{6,7},{7,6},{8,9},{9,8},{10,11... | collective-permute-start | bytes 3145736 | tf_op jit(solution)/shard_map/ppermute | solution.py:816
  16.6 26.3 %collective-permute-start.5 = (bf16[4096,128]{1,0:T(8,128)(2,1)}, bf16[4096,128]{1,0:T(8,128)(2,1)S(1)}, u32[]{:S(2)}, u32[]{:S(2)}) collective-permute-start(bf16[4096,128]{1,0:T(8,128)(2,1)} %get-tuple-element.84), channel_id=1, source_target_pairs={{0,2},{1,3},{2,0},{3,1},{4,6},{5,7},{6,4},{7,5},{8,10},{9,11},{10,... | collective-permute-start | bytes 3145736 | tf_op jit(solution)/shard_map/ppermute | solution.py:816
  19.9 11.0 %collective-permute-start.3 = (bf16[9,32,512]{2,1,0:T(8,128)(2,1)}, bf16[9,32,512]{2,1,0:T(8,128)(2,1)}, u32[]{:S(2)}, u32[]{:S(2)}) collective-permute-start(bf16[9,32,512]{2,1,0:T(8,128)(2,1)} %copy-done.13), channel_id=1, source_target_pairs={{0,8},{4,12},{8,0},{12,4},{16,24},{20,28},{24,16},{28,20},{1,9},{5... | collective-permute-start | bytes 884744 | tf_op jit(solution)/shard_map/ppermute | solution.py:816
  28.3 38.9 %collective-permute-start.1 = (bf16[9,128,512]{2,1,0:T(8,128)(2,1)}, bf16[9,128,512]{2,1,0:T(8,128)(2,1)}, u32[]{:S(2)}, u32[]{:S(2)}) collective-permute-start(bf16[9,128,512]{2,1,0:T(8,128)(2,1)} %refs_0_.6), channel_id=1, source_target_pairs={{0,2},{1,3},{2,0},{3,1},{4,6},{5,7},{6,4},{7,5},{8,10},{9,11},{10,... | collective-permute-start | bytes 3538952 | tf_op jit(solution)/shard_map/ppermute | solution.py:816
  145.0 21.2 %collective-permute-start.19 = (bf16[4096,256]{1,0:T(8,128)(2,1)}, bf16[4096,256]{1,0:T(8,128)(2,1)}, u32[]{:S(2)}, u32[]{:S(2)}) collective-permute-start(bf16[4096,256]{1,0:T(8,128)(2,1)} %get-tuple-element.101.g.refs_4_), channel_id=1, source_target_pairs={{0,1},{1,0},{2,3},{3,2},{4,5},{5,4},{6,7},{7,6},{8,9},{9,8},{10,11... | collective-permute-start | bytes 6291464 | tf_op jit(solution)/shard_map/ppermute | solution.py:816
  145.3 20.1 %collective-permute-start.17 = (bf16[9,128,512]{2,1,0:T(8,128)(2,1)}, bf16[9,128,512]{2,1,0:T(8,128)(2,1)}, u32[]{:S(2)}, u32[]{:S(2)}) collective-permute-start(bf16[9,128,512]{2,1,0:T(8,128)(2,1)} %refs_0_.6), channel_id=1, source_target_pairs={{0,1},{1,0},{2,3},{3,2},{4,5},{5,4},{6,7},{7,6},{8,9},{9,8},{10,11... | collective-permute-start | bytes 3538952 | tf_op jit(solution)/shard_map/ppermute | solution.py:816
  145.6 20.1 %collective-permute-start.18 = (bf16[9,128,512]{2,1,0:T(8,128)(2,1)}, bf16[9,128,512]{2,1,0:T(8,128)(2,1)}, u32[]{:S(2)}, u32[]{:S(2)}) collective-permute-start(bf16[9,128,512]{2,1,0:T(8,128)(2,1)} %collective-permute-done.1.refs_1_), channel_id=1, source_target_pairs={{0,1},{1,0},{2,3},{3,2},{4,5},{5,4},{6,7},{7,6},{8,9},{9,8},{10,11... | collective-permute-start | bytes 3538952 | tf_op jit(solution)/shard_map/ppermute | solution.py:816
  145.8 80.4 %collective-permute-start.12 = (bf16[9,128,512]{2,1,0:T(8,128)(2,1)}, bf16[9,128,512]{2,1,0:T(8,128)(2,1)}, u32[]{:S(2)}, u32[]{:S(2)}) collective-permute-start(bf16[9,128,512]{2,1,0:T(8,128)(2,1)} %refs_0_.7), channel_id=1, source_target_pairs={{0,1},{1,0},{2,3},{3,2},{4,5},{5,4},{6,7},{7,6},{8,9},{9,8},{10,11... | collective-permute-start | bytes 3538952 | tf_op jit(solution)/shard_map/ppermute | solution.py:816
  146.1 75.8 %collective-permute-start.13 = (bf16[9,32,512]{2,1,0:T(8,128)(2,1)}, bf16[9,32,512]{2,1,0:T(8,128)(2,1)}, u32[]{:S(2)}, u32[]{:S(2)}) collective-permute-start(bf16[9,32,512]{2,1,0:T(8,128)(2,1)} %copy-done.13), channel_id=1, source_target_pairs={{0,1},{1,0},{2,3},{3,2},{4,5},{5,4},{6,7},{7,6},{8,9},{9,8},{10,11... | collective-permute-start | bytes 884744 | tf_op jit(solution)/shard_map/ppermute | solution.py:816
  165.4 57.1 %collective-permute-start.14 = (bf16[9,32,512]{2,1,0:T(8,128)(2,1)}, bf16[9,32,512]{2,1,0:T(8,128)(2,1)}, u32[]{:S(2)}, u32[]{:S(2)}) collective-permute-start(bf16[9,32,512]{2,1,0:T(8,128)(2,1)} %collective-permute-done.2.refs_2_), channel_id=1, source_target_pairs={{0,1},{1,0},{2,3},{3,2},{4,5},{5,4},{6,7},{7,6},{8,9},{9,8},{10,11... | collective-permute-start | bytes 884744 | tf_op jit(solution)/shard_map/ppermute | solution.py:816
  165.7 35.4 %collective-permute-start.20 = (bf16[9,128,512]{2,1,0:T(8,128)(2,1)}, bf16[9,128,512]{2,1,0:T(8,128)(2,1)}, u32[]{:S(2)}, u32[]{:S(2)}) collective-permute-start(bf16[9,128,512]{2,1,0:T(8,128)(2,1)} %get-tuple-element.105), channel_id=1, source_target_pairs={{0,2},{1,3},{2,0},{3,1},{4,6},{5,7},{6,4},{7,5},{8,10},{9,11},{10,... | collective-permute-start | bytes 3538952 | tf_op jit(solution)/shard_map/ppermute | solution.py:816
  184.8 11.0 %all-to-all-start.3 = ((f32[32,8,128]{2,1,0:T(8,128)}), f32[32,8,128]{2,1,0:T(8,128)S(1)}, u32[]{:S(2)}, u32[]{:S(2)}) async-start(f32[32,8,128]{2,1,0:T(8,128)} %get-tuple-element.103), calls=%async_computation.3 | async-start | bytes 262144 | tf_op jit(solution)/shard_map/all_to_all | solution.py:951
  200.2 27.2 %collective-permute-start.22 = (bf16[4096,256]{1,0:T(8,128)(2,1)S(1)}, bf16[4096,256]{1,0:T(8,128)(2,1)S(1)}, u32[]{:S(2)}, u32[]{:S(2)}) collective-permute-start(bf16[4096,256]{1,0:T(8,128)(2,1)S(1)} %get-tuple-element.112.g.refs_10_), channel_id=1, source_target_pairs={{0,1},{1,0},{2,3},{3,2},{4,5},{5,4},{6,7},{7,6},{8,9},{9,8},{10,11... | collective-permute-start | bytes 6291464 | tf_op jit(solution)/shard_map/ppermute | solution.py:816
  202.8 18.8 %collective-permute-start.21 = (bf16[576,512]{1,0:T(8,128)(2,1)S(1)}, bf16[576,512]{1,0:T(8,128)(2,1)S(1)}, u32[]{:S(2)}, u32[]{:S(2)}) collective-permute-start(bf16[576,512]{1,0:T(8,128)(2,1)S(1)} %fusion.6), channel_id=1, source_target_pairs={{0,4},{4,0},{8,12},{12,8},{16,20},{20,16},{24,28},{28,24},{1,5},{5... | collective-permute-start | bytes 1769480 | tf_op jit(solution)/shard_map/ppermute | solution.py:816
  223.5 21.2 %collective-permute-start.25 = (bf16[4,128,512]{2,1,0:T(8,128)(2,1)S(1)}, bf16[4,128,512]{2,1,0:T(8,128)(2,1)S(1)}, u32[]{:S(2)}, u32[]{:S(2)}) collective-permute-start(bf16[4,128,512]{2,1,0:T(8,128)(2,1)S(1)} %copy-done.23), channel_id=1, source_target_pairs={{0,2},{1,3},{2,0},{3,1},{4,6},{5,7},{6,4},{7,5},{8,10},{9,11},{10,... | collective-permute-start | bytes 1572872 | tf_op jit(solution)/shard_map/ppermute | solution.py:816
  224.2 27.3 %collective-permute-start.24 = (bf16[5,128,512]{2,1,0:T(8,128)(2,1)S(1)}, bf16[5,128,512]{2,1,0:T(8,128)(2,1)S(1)}, u32[]{:S(2)}, u32[]{:S(2)}) collective-permute-start(bf16[5,128,512]{2,1,0:T(8,128)(2,1)S(1)} %copy-done.22), channel_id=1, source_target_pairs={{0,2},{1,3},{2,0},{3,1},{4,6},{5,7},{6,4},{7,5},{8,10},{9,11},{10,... | collective-permute-start | bytes 1966088 | tf_op jit(solution)/shard_map/ppermute | solution.py:816
  225.6 27.8 %collective-permute-start.28 = (f32[144,512]{1,0:T(8,128)S(1)}, f32[144,512]{1,0:T(8,128)S(1)}, u32[]{:S(2)}, u32[]{:S(2)}) collective-permute-start(f32[144,512]{1,0:T(8,128)S(1)} %get-tuple-element.152), channel_id=1, source_target_pairs={{0,8},{4,12},{8,0},{12,4},{16,24},{20,28},{24,16},{28,20},{1,9},{5... | collective-permute-start | bytes 884744 | tf_op jit(solution)/shard_map/ppermute | solution.py:816
  226.2 27.1 %collective-permute-start.29 = (f32[144,512]{1,0:T(8,128)S(1)}, f32[144,512]{1,0:T(8,128)S(1)}, u32[]{:S(2)}, u32[]{:S(2)}) collective-permute-start(f32[144,512]{1,0:T(8,128)S(1)} %get-tuple-element.151), channel_id=1, source_target_pairs={{0,16},{4,20},{8,24},{12,28},{16,0},{20,4},{24,8},{28,12},{1,17},{... | collective-permute-start | bytes 884744 | tf_op jit(solution)/shard_map/ppermute | solution.py:816
  227.5 25.9 %collective-permute-start.30 = (f32[144,512]{1,0:T(8,128)S(1)}, f32[144,512]{1,0:T(8,128)S(1)}, u32[]{:S(2)}, u32[]{:S(2)}) collective-permute-start(f32[144,512]{1,0:T(8,128)S(1)} %get-tuple-element.150), channel_id=1, source_target_pairs={{0,24},{4,28},{8,16},{12,20},{16,8},{20,12},{24,0},{28,4},{1,25},{... | collective-permute-start | bytes 884744 | tf_op jit(solution)/shard_map/ppermute | solution.py:816
  244.9 13.0 %collective-permute-start.27 = (bf16[256,512]{1,0:T(8,128)(2,1)S(1)}, bf16[256,512]{1,0:T(8,128)(2,1)S(1)}, u32[]{:S(2)}, u32[]{:S(2)}) collective-permute-start(bf16[256,512]{1,0:T(8,128)(2,1)S(1)} %fusion.11), channel_id=1, source_target_pairs={{0,4},{4,0},{8,12},{12,8},{16,20},{20,16},{24,28},{28,24},{1,5},{5... | collective-permute-start | bytes 786440 | tf_op jit(solution)/shard_map/ppermute | solution.py:816
  255.1 14.5 %collective-permute-start.34 = (bf16[144,512]{1,0:T(8,128)(2,1)S(1)}, bf16[144,512]{1,0:T(8,128)(2,1)S(1)}, u32[]{:S(2)}, u32[]{:S(2)}) collective-permute-start(bf16[144,512]{1,0:T(8,128)(2,1)S(1)} %fusion.10), channel_id=1, source_target_pairs={{0,16},{4,20},{8,24},{12,28},{16,0},{20,4},{24,8},{28,12},{1,17},{... | collective-permute-start | bytes 442376 | tf_op jit(solution)/shard_map/ppermute | solution.py:816
  255.3 16.2 %collective-permute-start.33 = (bf16[144,512]{1,0:T(8,128)(2,1)S(1)}, bf16[144,512]{1,0:T(8,128)(2,1)S(1)}, u32[]{:S(2)}, u32[]{:S(2)}) collective-permute-start(bf16[144,512]{1,0:T(8,128)(2,1)S(1)} %fusion.10), channel_id=1, source_target_pairs={{0,24},{4,28},{8,16},{12,20},{16,8},{20,12},{24,0},{28,4},{1,25},{... | collective-permute-start | bytes 442376 | tf_op jit(solution)/shard_map/ppermute | solution.py:816
  257.9 29.6 %collective-permute-start.23 = (bf16[128,4096]{1,0:T(8,128)(2,1)S(1)}, bf16[128,4096]{1,0:T(8,128)(2,1)S(1)}, u32[]{:S(2)}, u32[]{:S(2)}) collective-permute-start(bf16[128,4096]{1,0:T(8,128)(2,1)S(1)} %get-tuple-element.114), channel_id=1, source_target_pairs={{0,2},{1,3},{2,0},{3,1},{4,6},{5,7},{6,4},{7,5},{8,10},{9,11},{10,... | collective-permute-start | bytes 3145736 | tf_op jit(solution)/shard_map/ppermute | solution.py:816
  260.9 12.6 %collective-permute-start.32 = (bf16[64,512]{1,0:T(8,128)(2,1)S(1)}, bf16[64,512]{1,0:T(8,128)(2,1)S(1)}, u32[]{:S(2)}, u32[]{:S(2)}) collective-permute-start(bf16[64,512]{1,0:T(8,128)(2,1)S(1)} %get-tuple-element.166), channel_id=1, source_target_pairs={{0,8},{4,12},{8,0},{12,4},{16,24},{20,28},{24,16},{28,20},{1,9},{5... | collective-permute-start | bytes 196616 | tf_op jit(solution)/shard_map/ppermute | solution.py:816
  261.7 12.5 %collective-permute-start.36 = (bf16[64,512]{1,0:T(8,128)(2,1)S(1)}, bf16[64,512]{1,0:T(8,128)(2,1)S(1)}, u32[]{:S(2)}, u32[]{:S(2)}) collective-permute-start(bf16[64,512]{1,0:T(8,128)(2,1)S(1)} %get-tuple-element.165), channel_id=1, source_target_pairs={{0,16},{4,20},{8,24},{12,28},{16,0},{20,4},{24,8},{28,12},{1,17},{... | collective-permute-start | bytes 196616 | tf_op jit(solution)/shard_map/ppermute | solution.py:816
  274.2 11.2 %collective-permute-start.39 = (bf16[80,512]{1,0:T(8,128)(2,1)S(1)}, bf16[80,512]{1,0:T(8,128)(2,1)S(1)}, u32[]{:S(2)}, u32[]{:S(2)}) collective-permute-start(bf16[80,512]{1,0:T(8,128)(2,1)S(1)} %get-tuple-element.156), channel_id=1, source_target_pairs={{0,24},{4,28},{8,16},{12,20},{16,8},{20,12},{24,0},{28,4},{1,25},{... | collective-permute-start | bytes 245768 | tf_op jit(solution)/shard_map/ppermute | solution.py:816
  285.5 15.3 %collective-permute-start.47 = (bf16[576,512]{1,0:T(8,128)(2,1)S(1)}, bf16[576,512]{1,0:T(8,128)(2,1)S(1)}, u32[]{:S(2)}, u32[]{:S(2)}) collective-permute-start(bf16[576,512]{1,0:T(8,128)(2,1)S(1)} %pad_maximum_fusion), channel_id=1, source_target_pairs={{0,4},{4,0},{8,12},{12,8},{16,20},{20,16},{24,28},{28,24},{1,5},{5... | collective-permute-start | bytes 1769480 | tf_op jit(solution)/shard_map/ppermute | solution.py:816
  291.6 12.1 %collective-permute-start.46 = (bf16[256,512]{1,0:T(8,128)(2,1)S(1)}, bf16[256,512]{1,0:T(8,128)(2,1)S(1)}, u32[]{:S(2)}, u32[]{:S(2)}) collective-permute-start(bf16[256,512]{1,0:T(8,128)(2,1)S(1)} %pad_maximum_fusion.2), channel_id=1, source_target_pairs={{0,4},{4,0},{8,12},{12,8},{16,20},{20,16},{24,28},{28,24},{1,5},{5... | collective-permute-start | bytes 786440 | tf_op jit(solution)/shard_map/ppermute | solution.py:816
  296.0 11.1 %collective-permute-start.48 = (bf16[320,512]{1,0:T(8,128)(2,1)S(1)}, bf16[320,512]{1,0:T(8,128)(2,1)S(1)}, u32[]{:S(2)}, u32[]{:S(2)}) collective-permute-start(bf16[320,512]{1,0:T(8,128)(2,1)S(1)} %pad_maximum_fusion.1), channel_id=1, source_target_pairs={{0,4},{4,0},{8,12},{12,8},{16,20},{20,16},{24,28},{28,24},{1,5},{5... | collective-permute-start | bytes 983048 | tf_op jit(solution)/shard_map/ppermute | solution.py:816
  (46 other events, 466.0 us)
